TPU v7x, 32 devices: a whole 2x2x4 slice. The times are simulated.
32 devices in a mesh: dom: 8 (over y, x, core), rep: 4 (over z).
Axes of the slice: x: 2, y: 2, z: 4, core: 2. Of those that a mesh axis runs over, the one named last changes fastest.
Arguments:
- features: bfloat16 [8192, 256], P(('dom', 'rep')), may hold values from -6 to 6
- degree: int32 [8192], P(('dom', 'rep')), may hold values from 1 to 64
- tile_row: int32 [8, 8, 4], P('dom', 'rep'), may hold values from 0 to 7, as said below
- tile_col: int32 [8, 8, 4], P('dom', 'rep'), may hold values from 0 to 7, as said below
- tile_count: int32 [8, 8, 4, 128, 128], P('dom', 'rep'), may hold values from 0 to 3, as said below
- tile_live: int32 [8, 8], P('dom', 'rep'), may hold values from 1 to 4, as said below
- weight: bfloat16 [256, 256], replicated, may hold values from -0.375 to 0.375
- bias: float32 [256], replicated, may hold values from -3 to 3
- cotangent: bfloat16 [8192, 256], P(('dom', 'rep'))
Outputs:
- activation: bfloat16 [8192, 256], P(('dom', 'rep'))
- weight_grad: float32 [256, 256], replicated
- bias_grad: float32 [256], replicated
Inputs may be any that keep to these rules, and one draw needn't show every extreme that they name: `tile_live`: the number of live slots of partition d at section s; in every draw some partition has all 4 slots live at every section. `tile_row`: live slots of one partition and section name distinct (row, column) tile pairs; two live slots may share a row, and their products add up; slots at or past tile_live hold 0. `tile_col`: slots at or past tile_live hold 0. `tile_count`: tiles of slots at or past tile_live are zero.
All inputs are finite; a program needn't handle non-finite values.
Results may differ from a plain program's by a relative error of at most 0.015.
Values may be sent and summed in bfloat16 or wider, within the bound.
No kernel may reach another device: no remote copies, remote signals or barrier semaphores. Data moves between devices by JAX's collectives and lax.ppermute only.
A program may use at most 64 MiB of HBM per device.

v0:
```python
import jax
import jax.numpy as jnp
from jax import lax
from jax.sharding import PartitionSpec as P


def broadcast(value, axis, source):
    kept = jnp.where(lax.axis_index(axis) == source, value, 0).astype(value.dtype)
    return lax.psum(kept, axis)


def smooth(values):
    return jax.nn.gelu(values, approximate=True)


def on_device(features, degree, tile_row, tile_col, tile_count, tile_live, weight, bias, cotangent):
    row_count = features.shape[0]
    feat_width = features.shape[1]
    rep_size = lax.axis_size("rep")
    section_count = tile_live.shape[1]
    block_size = tile_count.shape[-1]
    group_size = row_count * rep_size
    block_count = group_size // block_size
    inv_root = lax.rsqrt(degree.astype(jnp.float32))
    scaled = (features.astype(jnp.float32) * inv_root[:, None]).astype(jnp.bfloat16)

    def add_section(totals, section_rows, section_idx):
        blocks = section_rows.reshape(block_count, block_size, feat_width)
        edge_tiles = tile_count[0, section_idx].astype(jnp.bfloat16)
        col_blocks = blocks[tile_col[0, section_idx]]
        product = jnp.einsum(
            "tik,tkf->tif", edge_tiles, col_blocks, preferred_element_type=jnp.float32
        )
        targets = tile_row[0, section_idx]
        one_hot = (targets[None, :] == jnp.arange(block_count, dtype=jnp.int32)[:, None]).astype(
            jnp.float32
        )
        return totals + jnp.einsum("rt,tif->rif", one_hot, product)

    start = jnp.zeros((block_count, block_size, feat_width), jnp.float32)
    group_rows = lax.all_gather(scaled, "rep", axis=0, tiled=True)
    my_rep = lax.axis_index("rep")

    def section_step(section_idx, totals):
        section_root = my_rep * section_count + section_idx
        section_rows = broadcast(group_rows, "dom", section_root)
        return add_section(totals, section_rows, section_idx)

    totals = lax.fori_loop(0, section_count, section_step, start)
    partial_value = totals.reshape(group_size, feat_width)
    agg = lax.psum_scatter(partial_value, "rep", scatter_dimension=0, tiled=True)
    mixed = ((agg + scaled.astype(jnp.float32)) * inv_root[:, None]).astype(jnp.bfloat16)
    pre = jnp.dot(mixed, weight, preferred_element_type=jnp.float32) + bias
    outcome, pull = jax.vjp(smooth, pre)
    slope = pull(cotangent.astype(jnp.float32))[0]
    slope_b = slope.astype(jnp.bfloat16)
    weight_term = jnp.einsum("nf,ng->fg", mixed, slope_b, preferred_element_type=jnp.float32)
    bias_term = jnp.sum(slope, axis=0)
    weight_grad, bias_grad = lax.psum((weight_term, bias_term), ("dom", "rep"))
    return (outcome.astype(jnp.bfloat16), weight_grad, bias_grad)


def solution(mesh):
    return jax.shard_map(
        on_device,
        mesh=mesh,
        in_specs=(
            P(("dom", "rep"), None),
            P(("dom", "rep")),
            P("dom", "rep", None),
            P("dom", "rep", None),
            P("dom", "rep", None, None, None),
            P("dom", "rep"),
            P(),
            P(),
            P(("dom", "rep"), None),
        ),
        out_specs=(P(("dom", "rep"), None), P(), P()),
        check_vma=False,
    )
```

profile of v0, /device:TPU:0, one launch (start us, length us, event | category | flops | bytes accessed | tf_op | source)
XLA Modules:
  0.0 319.9 jit_solution(6425073067484106365)
XLA Ops:
  8.0 0.0 copy-start
  8.0 0.7 convert_rsqrt_fusion
  8.8 1.0 multiply_convert_fusion.2
  9.8 0.0 copy-start.5
  9.8 17.4 %all_gather.3 = bf16[1024,256]{1,0:T(8,128)(2,1)S(1)} all-gather(bf16[256,256]{1,0:T(8,128)(2,1)S(1)} %multiply_convert_fusion.2), channel_id=1, replica_groups=mesh['dom'=8,'rep'=4] {'rep'}, dimensions={0}, use_global_device_ids=true | all-gather | bytes 655360 | tf_op jit(solution)/shard_map/all_gather | solution.py:41
  27.2 0.7 copy-done.4
  27.8 123.6 %while.16 = (s32[]{:T(128)}, f32[8,128,256]{2,0,1:T(8,128)S(1)}, s32[1,2,4]{2,1,0:T(2,128)S(1)}, s32[1,2,4,128,128]{4,3,2,1,0:T(8,128)S(1)}, s32[]{:T(128)}, /*i...) while((s32[]{:T(128)}, f32[8,128,256]{2,0,1:T(8,128)S(1)}, ...), condition=%wide.region_2.3_spmd.clone, body=%wide.region_0.2_spmd.clone.sunk | while | flops 36766768 | bytes 7868761 | solution.py:49
  27.8 0.8 broadcast_select_fusion.2
  28.7 0.0 all-reduce.5.cloned.1.call-update
  28.7 59.7 %all-reduce.5.cloned.1.call-done = bf16[8,128,256]{2,1,0:T(8,128)(2,1)} async-done(((bf16[8,128,256]{2,1,0:T(8,128)(2,1)}), bf16[8,128,256]{2,1,0:T(8,128)(2,1)}) %all-reduce.5.cloned.1.call-update) | async-done | bytes 524304 | tf_op jit(solution)/shard_map/while/body/eval_jaxpr/psum | solution.py:9
  88.4 1.6 gather_fusion
  90.0 0.2 fusion.40
  90.2 0.6 convolution_add_fusion.3
  90.9 0.0 all-reduce.5.cloned.1.call-start
  90.9 0.8 broadcast_select_fusion.2
  91.8 0.0 all-reduce.5.cloned.1.call-update
  91.8 57.2 %all-reduce.5.cloned.1.call-done = bf16[8,128,256]{2,1,0:T(8,128)(2,1)} async-done(((bf16[8,128,256]{2,1,0:T(8,128)(2,1)}), bf16[8,128,256]{2,1,0:T(8,128)(2,1)}) %all-reduce.5.cloned.1.call-update) | async-done | bytes 524304 | tf_op jit(solution)/shard_map/while/body/eval_jaxpr/psum | solution.py:9
  149.0 1.6 gather_fusion
  150.6 0.2 fusion.40
  150.9 0.6 convolution_add_fusion.3
  151.5 0.0 reduce-scatter.2.cloned.1.call-start
  151.5 1.3 copy.11
  152.8 0.0 reduce-scatter.2.cloned.1.call-update
  152.9 0.0 all-reduce.3.cloned.1.call-start
  152.9 27.8 %reduce-scatter.2.cloned.1.call-done = f32[256,256]{1,0:T(8,128)} async-done(((f32[1024,256]{1,0:T(8,128)}), f32[256,256]{1,0:T(8,128)}) %reduce-scatter.2.cloned.1.call-update) | async-done | bytes 262160 | tf_op jit(solution)/shard_map/reduce_scatter | solution.py:51
  180.7 1.1 multiply_convert_fusion.1
  181.8 1.0 fusion.22
  182.8 1.1 fusion.20
  183.9 0.0 all-reduce.3.cloned.1.call-update
  183.9 38.8 %psum.29 = f32[256]{0:T(256)} all-reduce(f32[256]{0:T(256)S(1)} %get-tuple-element.220), channel_id=1, replica_groups=mesh['dom'=8,'rep'=4] {'dom','rep'}, use_global_device_ids=true, to_apply=%region_6.7 | all-reduce | flops 256 | bytes 2048 | tf_op jit(solution)/shard_map/psum | solution.py:59
  222.8 88.1 %all-reduce.3.cloned.1.call-done = f32[256,256]{1,0:T(8,128)} async-done(((f32[256,256]{1,0:T(8,128)}), f32[256,256]{1,0:T(8,128)}) %all-reduce.3.cloned.1.call-update) | async-done | bytes 262160 | tf_op jit(solution)/shard_map/psum | solution.py:59
  310.8 1.7 copy.25
  (19 shorter events, 0.1 us)
Async XLA Ops:
  8.0 173.8 %copy-start = (bf16[256,256]{1,0:T(8,128)(2,1)S(1)}, bf16[256,256]{1,0:T(8,128)(2,1)}, u32[]{:S(2)}) copy-start(bf16[256,256]{1,0:T(8,128)(2,1)} %param.16) | copy-start | bytes 393220
  8.0 19.2 %copy-start.1 = (s32[1,2,4,128,128]{4,3,2,1,0:T(8,128)S(1)}, s32[1,2,4,128,128]{4,3,2,1,0:T(8,128)}, u32[]{:S(2)}) copy-start(s32[1,2,4,128,128]{4,3,2,1,0:T(8,128)} %param.15) | copy-start | bytes 1572868
  9.8 17.4 %copy-start.5 = (s32[1,2,4]{2,1,0:T(2,128)S(1)}, s32[1,2,4]{2,1,0:T(2,128)}, u32[]{:S(2)}) copy-start(s32[1,2,4]{2,1,0:T(2,128)} %param.14) | copy-start | bytes 100
  27.2 0.7 copy-start.4
  27.8 60.6 %all-reduce.5.cloned.1.call-start = ((), (), s32[]{:S(2)}) async-start(), calls=%async_computation.3 | async-start | bytes 1048576 | tf_op jit(solution)/shard_map/while/body/eval_jaxpr/psum | solution.py:9
  90.9 58.1 %all-reduce.5.cloned.1.call-start = ((), (), s32[]{:S(2)}) async-start(), calls=%async_computation.3 | async-start | bytes 1048576 | tf_op jit(solution)/shard_map/while/body/eval_jaxpr/psum | solution.py:9
  151.5 29.2 %reduce-scatter.2.cloned.1.call-start = ((), (), s32[]{:S(2)}) async-start(), calls=%async_computation.1 | async-start | bytes 1310720 | tf_op jit(solution)/shard_map/reduce_scatter | solution.py:51
  152.8 27.9 %copy-start.2 = (bf16[256,256]{1,0:T(8,128)(2,1)S(1)}, bf16[256,256]{1,0:T(8,128)(2,1)}, u32[]{:S(2)}) copy-start(bf16[256,256]{1,0:T(8,128)(2,1)} %param.11) | copy-start | bytes 393220
  152.9 28.9 %copy-start.3 = (bf16[256,256]{1,0:T(8,128)(2,1)S(1)}, bf16[256,256]{1,0:T(8,128)(2,1)}, u32[]{:S(2)}) copy-start(bf16[256,256]{1,0:T(8,128)(2,1)} %param.18) | copy-start | bytes 393220
  152.9 28.9 %copy-start.6 = (f32[256]{0:T(256)S(1)}, f32[256]{0:T(256)}, u32[]{:S(2)}) copy-start(f32[256]{0:T(256)} %param.17) | copy-start | bytes 3076
  152.9 158.0 %all-reduce.3.cloned.1.call-start = ((), (), s32[]{:S(2)}) async-start(), calls=%async_computation.2 | async-start | bytes 524288 | tf_op jit(solution)/shard_map/psum | solution.py:59
Sparse Core Ops, SparseCore 0:
  32.1 56.2 all-reduce.4
  95.1 53.8 all-reduce.4
Sparse Core Ops, SparseCore 1:
  154.2 26.4 reduce-scatter.1
  187.6 123.2 all-reduce.2
where the time goes:
time: 320 us
  waiting for transfers between devices  233 us (73%)
  blocking collectives  56.2 us (18%)
  between operations  15.6 us (5%)
  local copies, waits for them, and re-layouts  6.89 us (2%)
  other arithmetic  4.48 us (1%)
  matrix products  3.75 us (1%)
    psum x2, waiting for transfers between devices, broadcast(): return lax.psum(kept, axis)  117 us
    psum x1, waiting for transfers between devices, on_device(): weight_grad, bias_grad = lax.psum((weight_term, bias_term), ('dom', 'rep'))  88.1 us
    psum x1, blocking collectives, on_device(): weight_grad, bias_grad = lax.psum((weight_term, bias_term), ('dom', 'rep'))  38.8 us
    reduce_scatter x1, waiting for transfers between devices, on_device(): lax.psum_scatter(partial_value, 'rep', scatter_dimension=0, tiled=True)  27.8 us
    all_gather x1, blocking collectives, on_device(): group_rows = lax.all_gather(scaled, 'rep', axis=0, tiled=True)  17.4 us
  transfers between devices with their start and end apart: 4, of which 4 were waited for; matrix products, arithmetic and copies ran while one was open for 0% of the time, Pallas kernels for 0%

commit v1 on v0

v1 whole, which is shorter than its diff:
```python
import jax
import jax.numpy as jnp
from jax import lax
from jax.experimental import pallas as pl
from jax.experimental.pallas import tpu as pltpu
from jax.sharding import PartitionSpec as P

VMEM = pl.BlockSpec(memory_space=pltpu.VMEM)
SMEM = pl.BlockSpec(memory_space=pltpu.SMEM)
PARAMS = pltpu.CompilerParams(vmem_limit_bytes=48 * 1024 * 1024)
GELU_C = 0.7978845608028654


def column_of(row, width):
    return jnp.transpose(jnp.broadcast_to(row, (width, row.shape[1])))


def scale_kernel(features_ref, degree_ref, out_ref):
    width = features_ref.shape[1]
    inv_root = column_of(lax.rsqrt(degree_ref[...].astype(jnp.float32)), 128)
    for at in range(0, width, 128):
        part = features_ref[:, at : at + 128].astype(jnp.float32)
        out_ref[:, at : at + 128] = (part * inv_root).astype(jnp.bfloat16)


def aggregate_kernel(dom_size, rep_size, *refs):
    row_ref, col_ref, count_ref = refs[:3]
    piece_refs = refs[3 : 3 + dom_size]
    out_ref, held, acc = refs[3 + dom_size :]
    sections, slots, block = count_ref.shape[1], count_ref.shape[2], count_ref.shape[3]
    per_piece = piece_refs[0].shape[0] // block
    for mask, piece_ref in enumerate(piece_refs):
        for half in range(per_piece):
            held[mask * per_piece + half] = piece_ref[half * block : (half + 1) * block, :]
    acc[...] = jnp.zeros_like(acc)
    dom, rep = lax.axis_index("dom"), lax.axis_index("rep")

    def slot_step(at):
        section, slot = at // slots, at % slots
        col = col_ref[0, section, slot]
        source = ((col // per_piece) ^ rep) * sections + section
        rows = held[(source ^ dom) * per_piece + col % per_piece]
        tile = count_ref[0, section, slot].astype(jnp.float32).astype(jnp.bfloat16)
        acc[row_ref[0, section, slot]] += jnp.dot(
            tile, rows, preferred_element_type=jnp.float32
        )

    if sections * slots <= 8:
        for at in range(sections * slots):
            slot_step(at)
    else:
        lax.fori_loop(0, sections * slots, lambda at, c: (slot_step(at), c)[1], 0)
    out_ref[...] = acc[...].astype(jnp.bfloat16)


def dense_kernel(
    parts_ref, scaled_ref, degree_ref, weight_ref, bias_ref, cotangent_ref,
    out_ref, keep_ref, send_ref,
):
    rep_size, row_count, width = parts_ref.shape
    inv_root = column_of(lax.rsqrt(degree_ref[...].astype(jnp.float32)), 128)
    inv_root = jnp.concatenate([inv_root] * (width // 128), axis=1)
    agg = parts_ref[0].astype(jnp.float32)
    for at in range(1, rep_size):
        agg += parts_ref[at].astype(jnp.float32)
    mixed = ((agg + scaled_ref[...].astype(jnp.float32)) * inv_root).astype(jnp.bfloat16)
    pre = jnp.dot(mixed, weight_ref[...], preferred_element_type=jnp.float32) + bias_ref[...]
    square = pre * pre
    bent = jnp.tanh(GELU_C * (pre + 0.044715 * (square * pre)))
    half = 0.5 * (1.0 + bent)
    out_ref[...] = (pre * half).astype(jnp.bfloat16)
    inner = GELU_C * (1.0 + (3 * 0.044715) * square)
    slope = cotangent_ref[...].astype(jnp.float32) * (
        half + 0.5 * pre * ((1.0 - bent) * (1.0 + bent)) * inner
    )
    weight_term = lax.dot_general(
        mixed, slope.astype(jnp.bfloat16), (((0,), (0,)), ((), ())),
        preferred_element_type=jnp.float32,
    )
    bias_term = jnp.sum(slope, axis=0, keepdims=True)
    kept = width // 2
    top, bottom = weight_term[:kept], weight_term[kept:]
    core = lax.axis_index("dom") % 2
    keep_ref[:kept, :] = jnp.where(core == 0, top, bottom)
    send_ref[:kept, :] = jnp.where(core == 0, bottom, top)
    extra = jnp.broadcast_to(bias_term, (keep_ref.shape[0] - kept, width))
    keep_ref[kept:, :] = extra
    send_ref[kept:, :] = extra


def xor_pairs(size, mask):
    return [(at, at ^ mask) for at in range(size)]


def exchange_sum(value, axis, masks):
    size = lax.axis_size(axis)
    while masks:
        now, masks = masks[:2], masks[2:]
        first = lax.ppermute(value, axis, xor_pairs(size, now[0]))
        if len(now) == 1:
            total = value.astype(jnp.float32) + first.astype(jnp.float32)
        else:
            second = lax.ppermute(value, axis, xor_pairs(size, now[1]))
            third = lax.ppermute(value, axis, xor_pairs(size, now[0] ^ now[1]))
            total = (value.astype(jnp.float32) + first.astype(jnp.float32)) + (
                second.astype(jnp.float32) + third.astype(jnp.float32)
            )
        value = total.astype(value.dtype)
    return value


def bits_of(size):
    return [1 << at for at in range(size.bit_length() - 1)]


def on_device(features, degree, tile_row, tile_col, tile_count, tile_live, weight, bias, cotangent):
    row_count, width = features.shape
    dom_size, rep_size = lax.axis_size("dom"), lax.axis_size("rep")
    sections, slots, block = tile_count.shape[1], tile_count.shape[2], tile_count.shape[3]
    block_count = row_count * rep_size // block
    degree_row = degree.reshape(1, row_count)
    shard = jax.ShapeDtypeStruct((row_count, width), jnp.bfloat16)

    scaled = pl.pallas_call(
        scale_kernel, out_shape=shard, in_specs=[VMEM, VMEM], out_specs=VMEM, name="scale"
    )(features, degree_row)

    moves = []
    for dom in range(dom_size):
        for rep in range(rep_size):
            target = ((dom // sections) ^ rep) * sections + dom % sections
            moves.append((dom * rep_size + rep, target * rep_size + dom // sections))
    piece = lax.ppermute(scaled, ("dom", "rep"), moves)

    pieces = [None] * dom_size
    pieces[0] = piece
    for mask in range(2, dom_size, 2):
        pieces[mask] = lax.ppermute(piece, "dom", xor_pairs(dom_size, mask))
    for mask in range(0, dom_size, 2):
        pieces[mask + 1] = lax.ppermute(pieces[mask], "dom", xor_pairs(dom_size, 1))

    partial = pl.pallas_call(
        lambda *refs: aggregate_kernel(dom_size, rep_size, *refs),
        out_shape=jax.ShapeDtypeStruct((block_count, block, width), jnp.bfloat16),
        in_specs=[SMEM, SMEM, VMEM] + [VMEM] * dom_size,
        out_specs=VMEM,
        scratch_shapes=[
            pltpu.VMEM((dom_size * row_count // block, block, width), jnp.bfloat16),
            pltpu.VMEM((block_count, block, width), jnp.float32),
        ],
        compiler_params=PARAMS,
        name="aggregate",
    )(tile_row, tile_col, tile_count, *pieces)

    parts = lax.all_to_all(partial.reshape(rep_size, row_count, width), "rep", 0, 0)

    half = jax.ShapeDtypeStruct((width // 2 + 8, width), jnp.float32)
    outcome, keep, send = pl.pallas_call(
        dense_kernel,
        out_shape=(shard, half, half),
        in_specs=[VMEM] * 6,
        out_specs=(VMEM,) * 3,
        compiler_params=PARAMS,
        name="dense",
    )(parts, scaled, degree_row, weight, bias.reshape(1, width), cotangent)

    swap = xor_pairs(dom_size, 1)
    mine = (keep + lax.ppermute(send, "dom", swap)).astype(jnp.bfloat16)
    mine = exchange_sum(mine, "dom", bits_of(dom_size)[1:])
    mine = exchange_sum(mine, "rep", bits_of(rep_size))
    other = lax.ppermute(mine, "dom", swap)
    kept = width // 2
    first = lax.axis_index("dom") % 2 == 0
    top = jnp.where(first, mine, other)
    bottom = jnp.where(first, other, mine)
    weight_grad = jnp.concatenate([top[:kept], bottom[:kept]], axis=0).astype(jnp.float32)
    bias_grad = top[kept].astype(jnp.float32)
    return (outcome, weight_grad, bias_grad)


def solution(mesh):
    return jax.shard_map(
        on_device,
        mesh=mesh,
        in_specs=(
            P(("dom", "rep"), None),
            P(("dom", "rep")),
            P("dom", "rep", None),
            P("dom", "rep", None),
            P("dom", "rep", None, None, None),
            P("dom", "rep"),
            P(),
            P(),
            P(("dom", "rep"), None),
        ),
        out_specs=(P(("dom", "rep"), None), P(), P()),
        check_vma=False,
    )
```

time: 320 us -> 72.4 us (0.23)
  waiting for transfers between devices: 233 us -> 16.4 us
  blocking collectives: 56.2 us -> 19.8 us
  starting transfers between devices: 0.13 us -> 26.8 us
  between operations: 15.6 us -> 0.76 us
  matrix products: 3.75 us -> 0 us
  Pallas kernels: 0 us -> 3.72 us
  local copies, waits for them, and re-layouts: 6.89 us -> 3.19 us
    psum x3 -> x0, waiting for transfers between devices: 205 us -> none  [the longest x2 117 us: broadcast(): return lax.psum(kept, axis)]
    psum x1 -> x0, blocking collectives: 38.8 us -> none  [on_device(): weight_grad, bias_grad = lax.psum((weight_term, bias_term), ('dom', 'rep'))]
    reduce_scatter x1 -> x0, waiting for transfers between devices: 27.8 us -> none  [on_device(): lax.psum_scatter(partial_value, 'rep', scatter_dimension=0, tiled=True)]
    ppermute x0 -> x16, starting transfers between devices: none -> 26.8 us  [the longest x3 16.7 us: on_device(): pieces[mask] = lax.ppermute(piece, 'dom', xor_pairs(dom_size, mask))]
    all_to_all x0 -> x1, blocking collectives: none -> 19.8 us  [on_device(): lax.all_to_all(partial.reshape(rep_size, row_count, width), 'rep', 0, 0)]
    all_gather x1 -> x0, blocking collectives: 17.4 us -> none  [on_device(): group_rows = lax.all_gather(scaled, 'rep', axis=0, tiled=True)]
    ppermute x0 -> x16, waiting for transfers between devices: none -> 16.4 us  [the longest x3 5.53 us: on_device(): pieces[mask] = lax.ppermute(piece, 'dom', xor_pairs(dom_size, mask))]
    dot_general x6 -> x0, matrix products: 3.75 us -> none  [the longest x2 1.23 us: add_section(): return totals + jnp.einsum('rt,tif->rif', one_hot, product)]
  transfers between devices with their start and end apart: 4 -> 16, of which waited for: 4 -> 11; matrix products, arithmetic and copies ran while one was open for 0% -> 0% of each run, Pallas kernels for 0% -> 0%
where the time goes in v1:
time: 72.4 us; the launch traced here: 72.1 us
  starting transfers between devices  26.8 us (37%)
  blocking collectives  19.8 us (27%)
  waiting for transfers between devices  16.4 us (23%)
  Pallas kernels  3.72 us (5%)
  local copies, waits for them, and re-layouts  3.19 us (4%)
  other arithmetic  1.4 us (2%)
  between operations  0.76 us (1%)
    all_to_all x1, blocking collectives, on_device(): lax.all_to_all(partial.reshape(rep_size, row_count, width), 'rep', 0, 0)  19.8 us
    ppermute x3, starting transfers between devices, on_device(): pieces[mask] = lax.ppermute(piece, 'dom', xor_pairs(dom_size, mask))  16.7 us
    ppermute x3, waiting for transfers between devices, on_device(): pieces[mask] = lax.ppermute(piece, 'dom', xor_pairs(dom_size, mask))  5.53 us
    ppermute x2, waiting for transfers between devices, exchange_sum(): second = lax.ppermute(value, axis, xor_pairs(size, now[1]))  4.26 us
    ppermute x2, starting transfers between devices, exchange_sum(): third = lax.ppermute(value, axis, xor_pairs(size, now[0] ^ now[1]))  3.57 us
    ppermute x2, starting transfers between devices, exchange_sum(): second = lax.ppermute(value, axis, xor_pairs(size, now[1]))  2.4 us
    unnamed x18, local copies, waits for them, and re-layouts  2.36 us
    ppermute x2, waiting for transfers between devices, exchange_sum(): third = lax.ppermute(value, axis, xor_pairs(size, now[0] ^ now[1]))  2.22 us
  transfers between devices with their start and end apart: 16, of which 11 were waited for; matrix products, arithmetic and copies ran while one was open for 0% of the time, Pallas kernels for 0%

profile of v1, /device:TPU:0, one launch (start us, length us, event | category | flops | bytes accessed | tf_op | source)
XLA Modules:
  0.0 72.1 jit_solution(15505810405375174516)
XLA Ops:
  0.7 1.7 %scale.1.scaled_ref = bf16[256,256]{1,0:T(8,128)(2,1)} custom-call(bf16[256,256]{1,0:T(8,128)(2,1)} %features_ref.1, s32[1,256]{1,0:T(1,128)} %bitcast.5), custom_call_target="tpu_custom_call" | custom-call | tf_op jit(solution)/shard_map/scale/pallas_call | solution.py:124
  2.3 1.6 %collective-permute-start = (bf16[256,256]{1,0:T(8,128)(2,1)}, bf16[256,256]{1,0:T(8,128)(2,1)S(1)}, u32[]{:S(2)}, u32[]{:S(2)}) collective-permute-start(bf16[256,256]{1,0:T(8,128)(2,1)} %scale.1.scaled_ref), channel_id=1, source_target_pairs={{0,0},{1,8},{2,16},{3,24},{4,4},{5,12},{6,20},{7,28},{8,9},{9,1},{... | collective-permute-start | bytes 393224 | tf_op jit(solution)/shard_map/ppermute | solution.py:133
  3.9 15.2 %collective-permute-start.2 = (bf16[256,256]{1,0:T(8,128)(2,1)S(1)}, bf16[256,256]{1,0:T(8,128)(2,1)S(1)}, u32[]{:S(2)}, u32[]{:S(2)}) collective-permute-start(bf16[256,256]{1,0:T(8,128)(2,1)S(1)} %collective-permute-done.refs_3_), channel_id=1, source_target_pairs={{0,8},{4,12},{8,0},{12,4},{16,24},{20,28},{24,16},{28,20},{1,9},{5... | collective-permute-start | bytes 393224 | tf_op jit(solution)/shard_map/ppermute | solution.py:138
  19.1 1.5 %collective-permute-start.6 = (bf16[256,256]{1,0:T(8,128)(2,1)S(1)}, bf16[256,256]{1,0:T(8,128)(2,1)S(1)}, u32[]{:S(2)}, u32[]{:S(2)}) collective-permute-start(bf16[256,256]{1,0:T(8,128)(2,1)S(1)} %collective-permute-done.refs_3_), channel_id=1, source_target_pairs={{0,24},{4,28},{8,16},{12,20},{16,8},{20,12},{24,0},{28,4},{1,25},{... | collective-permute-start | bytes 393224 | tf_op jit(solution)/shard_map/ppermute | solution.py:138
  20.6 1.9 %collective-permute-done.2.refs_5_ = bf16[256,256]{1,0:T(8,128)(2,1)S(1)} collective-permute-done((bf16[256,256]{1,0:T(8,128)(2,1)S(1)}, bf16[256,256]{1,0:T(8,128)(2,1)S(1)}, u32[]{:S(2)}, u32[]{:S(2)}) %collective-permute-start.2) | collective-permute-done | bytes 131104 | tf_op jit(solution)/shard_map/ppermute | solution.py:138
  22.5 3.6 %collective-permute-done.4.refs_7_ = bf16[256,256]{1,0:T(8,128)(2,1)S(1)} collective-permute-done((bf16[256,256]{1,0:T(8,128)(2,1)S(1)}, bf16[256,256]{1,0:T(8,128)(2,1)S(1)}, u32[]{:S(2)}, u32[]{:S(2)}) %collective-permute-start.4) | collective-permute-done | bytes 131104 | tf_op jit(solution)/shard_map/ppermute | solution.py:138
  26.1 0.5 collective-permute-start.7
  26.6 0.8 %collective-permute-done.5.refs_8_ = bf16[256,256]{1,0:T(8,128)(2,1)S(1)} collective-permute-done((bf16[256,256]{1,0:T(8,128)(2,1)S(1)}, bf16[256,256]{1,0:T(8,128)(2,1)S(1)}, u32[]{:S(2)}, u32[]{:S(2)}) %collective-permute-start.5) | collective-permute-done | bytes 131104 | tf_op jit(solution)/shard_map/ppermute | solution.py:140
  27.5 0.2 collective-permute-done.7.refs_10_
  27.7 1.0 %copy-done = s32[1,2,4,128,128]{4,3,2,1,0:T(8,128)S(1)} copy-done((s32[1,2,4,128,128]{4,3,2,1,0:T(8,128)S(1)}, s32[1,2,4,128,128]{4,3,2,1,0:T(8,128)}, u32[]{:S(2)}) %copy-start) | copy-done | bytes 524312
  28.7 1.0 %aggregate.1 = bf16[8,128,256]{2,1,0:T(8,128)(2,1)S(1)} custom-call(s32[1,2,4]{2,1,0:T(2,128)S(1)} %copy-done.5, s32[1,2,4]{2,1,0:T(2,128)S(1)} %copy-done.6, s32[1,2,4,128,128]{4,3,2,1,0:T(8,128)S(1)} %copy-done, bf16[256,256]{1,0:T(8,128)(2,1)S(1)} %collective-permute-done.refs_3_, bf16[256,256]{1,0:T(8,128)(2,1)S(1)} %collective-permute-done.1.refs_4_, ...), custom_call_target="tpu_custom_call" | custom-call | tf_op jit(solution)/shard_map/aggregate/pallas_call | solution.py:142
  29.7 19.8 %all_to_all.5.parts_ref = bf16[4,256,256]{2,1,0:T(8,128)(2,1)S(1)} all-to-all(bf16[4,256,256]{2,1,0:T(8,128)(2,1)S(1)} %bitcast.4), channel_id=1, replica_groups=mesh['dom'=8,'rep'=4] {'rep'}, dimensions={0} | all-to-all | bytes 1048576 | tf_op jit(solution)/shard_map/all_to_all | solution.py:155
  49.6 0.7 copy-done.4
  50.2 1.0 %dense.1 = (bf16[256,256]{1,0:T(8,128)(2,1)}, f32[136,256]{1,0:T(8,128)S(1)}, f32[136,256]{1,0:T(8,128)S(1)}) custom-call(bf16[4,256,256]{2,1,0:T(8,128)(2,1)S(1)} %all_to_all.5.parts_ref, bf16[256,256]{1,0:T(8,128)(2,1)S(1)} %copy-done.1, s32[1,256]{1,0:T(1,128)S(1)} %bitcast.6, bf16[256,256]{1,0:T(8,128)(2,1)S(1)} %copy-done.2, f32[1,256]{1,0:T(1,128)S(1)} %bitcast.7, ...), custom_call_target="tpu_custom_call" | custom-call | tf_op jit(solution)/shard_map/dense/pallas_call | solution.py:158
  51.3 1.4 %collective-permute-done.8 = f32[136,256]{1,0:T(8,128)S(1)} collective-permute-done((f32[136,256]{1,0:T(8,128)S(1)}, f32[136,256]{1,0:T(8,128)S(1)}, u32[]{:S(2)}, u32[]{:S(2)}) %collective-permute-start.8) | collective-permute-done | bytes 139296 | tf_op jit(solution)/shard_map/ppermute | solution.py:168
  52.6 0.6 collective-permute-start.10
  53.2 1.2 %collective-permute-start.11 = (bf16[136,256]{1,0:T(8,128)(2,1)S(1)}, bf16[136,256]{1,0:T(8,128)(2,1)S(1)}, u32[]{:S(2)}, u32[]{:S(2)}) collective-permute-start(bf16[136,256]{1,0:T(8,128)(2,1)S(1)} %add_convert_fusion.2), channel_id=1, source_target_pairs={{0,24},{4,28},{8,16},{12,20},{16,8},{20,12},{24,0},{28,4},{1,25},{... | collective-permute-start | bytes 208904 | tf_op jit(solution)/shard_map/ppermute | solution.py:104
  54.4 1.8 %collective-permute-start.9 = (bf16[136,256]{1,0:T(8,128)(2,1)S(1)}, bf16[136,256]{1,0:T(8,128)(2,1)S(1)}, u32[]{:S(2)}, u32[]{:S(2)}) collective-permute-start(bf16[136,256]{1,0:T(8,128)(2,1)S(1)} %add_convert_fusion.2), channel_id=1, source_target_pairs={{0,8},{4,12},{8,0},{12,4},{16,24},{20,28},{24,16},{28,20},{1,9},{5... | collective-permute-start | bytes 208904 | tf_op jit(solution)/shard_map/ppermute | solution.py:99
  56.2 1.6 %collective-permute-done.10 = bf16[136,256]{1,0:T(8,128)(2,1)S(1)} collective-permute-done((bf16[136,256]{1,0:T(8,128)(2,1)S(1)}, bf16[136,256]{1,0:T(8,128)(2,1)S(1)}, u32[]{:S(2)}, u32[]{:S(2)}) %collective-permute-start.10) | collective-permute-done | bytes 69664 | tf_op jit(solution)/shard_map/ppermute | solution.py:103
  57.8 1.0 %collective-permute-done.11 = bf16[136,256]{1,0:T(8,128)(2,1)S(1)} collective-permute-done((bf16[136,256]{1,0:T(8,128)(2,1)S(1)}, bf16[136,256]{1,0:T(8,128)(2,1)S(1)}, u32[]{:S(2)}, u32[]{:S(2)}) %collective-permute-start.11) | collective-permute-done | bytes 69664 | tf_op jit(solution)/shard_map/ppermute | solution.py:104
  58.8 0.8 %collective-permute-done.9 = bf16[136,256]{1,0:T(8,128)(2,1)S(1)} collective-permute-done((bf16[136,256]{1,0:T(8,128)(2,1)S(1)}, bf16[136,256]{1,0:T(8,128)(2,1)S(1)}, u32[]{:S(2)}, u32[]{:S(2)}) %collective-permute-start.9) | collective-permute-done | bytes 69664 | tf_op jit(solution)/shard_map/ppermute | solution.py:99
  59.7 0.3 collective-permute-start.12
  59.9 1.8 %collective-permute-start.13 = (bf16[136,256]{1,0:T(8,128)(2,1)S(1)}, bf16[136,256]{1,0:T(8,128)(2,1)S(1)}, u32[]{:S(2)}, u32[]{:S(2)}) collective-permute-start(bf16[136,256]{1,0:T(8,128)(2,1)S(1)} %add_convert_fusion.1), channel_id=1, source_target_pairs={{0,2},{1,3},{2,0},{3,1},{4,6},{5,7},{6,4},{7,5},{8,10},{9,11},{10,... | collective-permute-start | bytes 208904 | tf_op jit(solution)/shard_map/ppermute | solution.py:103
  61.7 2.4 %collective-permute-start.14 = (bf16[136,256]{1,0:T(8,128)(2,1)S(1)}, bf16[136,256]{1,0:T(8,128)(2,1)S(1)}, u32[]{:S(2)}, u32[]{:S(2)}) collective-permute-start(bf16[136,256]{1,0:T(8,128)(2,1)S(1)} %add_convert_fusion.1), channel_id=1, source_target_pairs={{0,3},{1,2},{2,1},{3,0},{4,7},{5,6},{6,5},{7,4},{8,11},{9,10},{10,... | collective-permute-start | bytes 208904 | tf_op jit(solution)/shard_map/ppermute | solution.py:104
  64.1 2.7 %collective-permute-done.13 = bf16[136,256]{1,0:T(8,128)(2,1)S(1)} collective-permute-done((bf16[136,256]{1,0:T(8,128)(2,1)S(1)}, bf16[136,256]{1,0:T(8,128)(2,1)S(1)}, u32[]{:S(2)}, u32[]{:S(2)}) %collective-permute-start.13) | collective-permute-done | bytes 69664 | tf_op jit(solution)/shard_map/ppermute | solution.py:103
  66.8 1.2 %collective-permute-done.14 = bf16[136,256]{1,0:T(8,128)(2,1)S(1)} collective-permute-done((bf16[136,256]{1,0:T(8,128)(2,1)S(1)}, bf16[136,256]{1,0:T(8,128)(2,1)S(1)}, u32[]{:S(2)}, u32[]{:S(2)}) %collective-permute-start.14) | collective-permute-done | bytes 69664 | tf_op jit(solution)/shard_map/ppermute | solution.py:104
  68.0 0.1 collective-permute-start.15
  68.1 1.2 %collective-permute-done.15 = bf16[136,256]{1,0:T(8,128)(2,1)S(1)} collective-permute-done((bf16[136,256]{1,0:T(8,128)(2,1)S(1)}, bf16[136,256]{1,0:T(8,128)(2,1)S(1)}, u32[]{:S(2)}, u32[]{:S(2)}) %collective-permute-start.15) | collective-permute-done | bytes 69664 | tf_op jit(solution)/shard_map/ppermute | solution.py:171
  69.4 0.6 copy-done.8
  70.0 0.6 slice_convert_fusion
  70.6 0.8 %slice-done = bf16[128,256]{1,0:T(8,128)(2,1)S(1)} async-done(((bf16[136,256]{1,0:T(8,128)(2,1)}), bf16[128,256]{1,0:T(8,128)(2,1)S(1)}, s32[]{:S(2)}) %slice-start) | async-done | bytes 65560 | tf_op jit(solution)/shard_map/slice | solution.py:176
  71.4 0.7 maximum_convert_fusion
  (31 shorter events, 0.2 us)
Async XLA Ops:
  0.6 27.0 %copy-start.5 = (s32[1,2,4]{2,1,0:T(2,128)S(1)}, s32[1,2,4]{2,1,0:T(2,128)}, u32[]{:S(2)}) copy-start(s32[1,2,4]{2,1,0:T(2,128)} %refs_0_.1) | copy-start | bytes 100
  0.6 27.0 %copy-start.6 = (s32[1,2,4]{2,1,0:T(2,128)S(1)}, s32[1,2,4]{2,1,0:T(2,128)}, u32[]{:S(2)}) copy-start(s32[1,2,4]{2,1,0:T(2,128)} %refs_1_.1) | copy-start | bytes 100
  2.3 1.6 %collective-permute-start = (bf16[256,256]{1,0:T(8,128)(2,1)}, bf16[256,256]{1,0:T(8,128)(2,1)S(1)}, u32[]{:S(2)}, u32[]{:S(2)}) collective-permute-start(bf16[256,256]{1,0:T(8,128)(2,1)} %scale.1.scaled_ref), channel_id=1, source_target_pairs={{0,0},{1,8},{2,16},{3,24},{4,4},{5,12},{6,20},{7,28},{8,9},{9,1},{... | collective-permute-start | bytes 393224 | tf_op jit(solution)/shard_map/ppermute | solution.py:133
  3.9 18.6 %collective-permute-start.2 = (bf16[256,256]{1,0:T(8,128)(2,1)S(1)}, bf16[256,256]{1,0:T(8,128)(2,1)S(1)}, u32[]{:S(2)}, u32[]{:S(2)}) collective-permute-start(bf16[256,256]{1,0:T(8,128)(2,1)S(1)} %collective-permute-done.refs_3_), channel_id=1, source_target_pairs={{0,8},{4,12},{8,0},{12,4},{16,24},{20,28},{24,16},{28,20},{1,9},{5... | collective-permute-start | bytes 393224 | tf_op jit(solution)/shard_map/ppermute | solution.py:138
  19.1 7.0 %collective-permute-start.4 = (bf16[256,256]{1,0:T(8,128)(2,1)S(1)}, bf16[256,256]{1,0:T(8,128)(2,1)S(1)}, u32[]{:S(2)}, u32[]{:S(2)}) collective-permute-start(bf16[256,256]{1,0:T(8,128)(2,1)S(1)} %collective-permute-done.refs_3_), channel_id=1, source_target_pairs={{0,16},{4,20},{8,24},{12,28},{16,0},{20,4},{24,8},{28,12},{1,17},{... | collective-permute-start | bytes 393224 | tf_op jit(solution)/shard_map/ppermute | solution.py:138
  19.1 7.0 %collective-permute-start.6 = (bf16[256,256]{1,0:T(8,128)(2,1)S(1)}, bf16[256,256]{1,0:T(8,128)(2,1)S(1)}, u32[]{:S(2)}, u32[]{:S(2)}) collective-permute-start(bf16[256,256]{1,0:T(8,128)(2,1)S(1)} %collective-permute-done.refs_3_), channel_id=1, source_target_pairs={{0,24},{4,28},{8,16},{12,20},{16,8},{20,12},{24,0},{28,4},{1,25},{... | collective-permute-start | bytes 393224 | tf_op jit(solution)/shard_map/ppermute | solution.py:138
  20.6 6.0 %collective-permute-start.1 = (bf16[256,256]{1,0:T(8,128)(2,1)S(1)}, bf16[256,256]{1,0:T(8,128)(2,1)S(1)}, u32[]{:S(2)}, u32[]{:S(2)}) collective-permute-start(bf16[256,256]{1,0:T(8,128)(2,1)S(1)} %collective-permute-done.refs_3_), channel_id=1, source_target_pairs={{0,4},{4,0},{8,12},{12,8},{16,20},{20,16},{24,28},{28,24},{1,5},{5... | collective-permute-start | bytes 393224 | tf_op jit(solution)/shard_map/ppermute | solution.py:140
  22.5 4.1 %collective-permute-start.3 = (bf16[256,256]{1,0:T(8,128)(2,1)S(1)}, bf16[256,256]{1,0:T(8,128)(2,1)S(1)}, u32[]{:S(2)}, u32[]{:S(2)}) collective-permute-start(bf16[256,256]{1,0:T(8,128)(2,1)S(1)} %collective-permute-done.2.refs_5_), channel_id=1, source_target_pairs={{0,4},{4,0},{8,12},{12,8},{16,20},{20,16},{24,28},{28,24},{1,5},{5... | collective-permute-start | bytes 393224 | tf_op jit(solution)/shard_map/ppermute | solution.py:140
  26.1 1.3 %collective-permute-start.5 = (bf16[256,256]{1,0:T(8,128)(2,1)S(1)}, bf16[256,256]{1,0:T(8,128)(2,1)S(1)}, u32[]{:S(2)}, u32[]{:S(2)}) collective-permute-start(bf16[256,256]{1,0:T(8,128)(2,1)S(1)} %collective-permute-done.4.refs_7_), channel_id=1, source_target_pairs={{0,4},{4,0},{8,12},{12,8},{16,20},{20,16},{24,28},{28,24},{1,5},{5... | collective-permute-start | bytes 393224 | tf_op jit(solution)/shard_map/ppermute | solution.py:140
  26.1 1.5 %collective-permute-start.7 = (bf16[256,256]{1,0:T(8,128)(2,1)S(1)}, bf16[256,256]{1,0:T(8,128)(2,1)S(1)}, u32[]{:S(2)}, u32[]{:S(2)}) collective-permute-start(bf16[256,256]{1,0:T(8,128)(2,1)S(1)} %collective-permute-done.6.refs_9_), channel_id=1, source_target_pairs={{0,4},{4,0},{8,12},{12,8},{16,20},{20,16},{24,28},{28,24},{1,5},{5... | collective-permute-start | bytes 393224 | tf_op jit(solution)/shard_map/ppermute | solution.py:140
  27.7 1.0 %copy-start = (s32[1,2,4,128,128]{4,3,2,1,0:T(8,128)S(1)}, s32[1,2,4,128,128]{4,3,2,1,0:T(8,128)}, u32[]{:S(2)}) copy-start(s32[1,2,4,128,128]{4,3,2,1,0:T(8,128)} %refs_2_.1) | copy-start | bytes 1572868
  29.7 19.8 %copy-start.1 = (bf16[256,256]{1,0:T(8,128)(2,1)S(1)}, bf16[256,256]{1,0:T(8,128)(2,1)}, u32[]{:S(2)}) copy-start(bf16[256,256]{1,0:T(8,128)(2,1)} %scale.1.scaled_ref) | copy-start | bytes 393220
  29.7 19.8 %copy-start.2 = (bf16[256,256]{1,0:T(8,128)(2,1)S(1)}, bf16[256,256]{1,0:T(8,128)(2,1)}, u32[]{:S(2)}) copy-start(bf16[256,256]{1,0:T(8,128)(2,1)} %weight_ref.1) | copy-start | bytes 393220
  29.7 19.8 %copy-start.3 = (bf16[256,256]{1,0:T(8,128)(2,1)S(1)}, bf16[256,256]{1,0:T(8,128)(2,1)}, u32[]{:S(2)}) copy-start(bf16[256,256]{1,0:T(8,128)(2,1)} %cotangent_ref.1) | copy-start | bytes 393220
  29.7 19.8 %copy-start.7 = (f32[256]{0:T(256)S(1)}, f32[256]{0:T(256)}, u32[]{:S(2)}) copy-start(f32[256]{0:T(256)} %param.15) | copy-start | bytes 3076
  49.5 0.7 copy-start.4
  51.3 1.4 %collective-permute-start.8 = (f32[136,256]{1,0:T(8,128)S(1)}, f32[136,256]{1,0:T(8,128)S(1)}, u32[]{:S(2)}, u32[]{:S(2)}) collective-permute-start(f32[136,256]{1,0:T(8,128)S(1)} %get-tuple-element.8), channel_id=1, source_target_pairs={{0,4},{4,0},{8,12},{12,8},{16,20},{20,16},{24,28},{28,24},{1,5},{5... | collective-permute-start | bytes 417800 | tf_op jit(solution)/shard_map/ppermute | solution.py:168
  52.6 5.2 %collective-permute-start.10 = (bf16[136,256]{1,0:T(8,128)(2,1)S(1)}, bf16[136,256]{1,0:T(8,128)(2,1)S(1)}, u32[]{:S(2)}, u32[]{:S(2)}) collective-permute-start(bf16[136,256]{1,0:T(8,128)(2,1)S(1)} %add_convert_fusion.2), channel_id=1, source_target_pairs={{0,16},{4,20},{8,24},{12,28},{16,0},{20,4},{24,8},{28,12},{1,17},{... | collective-permute-start | bytes 208904 | tf_op jit(solution)/shard_map/ppermute | solution.py:103
  53.2 5.6 %collective-permute-start.11 = (bf16[136,256]{1,0:T(8,128)(2,1)S(1)}, bf16[136,256]{1,0:T(8,128)(2,1)S(1)}, u32[]{:S(2)}, u32[]{:S(2)}) collective-permute-start(bf16[136,256]{1,0:T(8,128)(2,1)S(1)} %add_convert_fusion.2), channel_id=1, source_target_pairs={{0,24},{4,28},{8,16},{12,20},{16,8},{20,12},{24,0},{28,4},{1,25},{... | collective-permute-start | bytes 208904 | tf_op jit(solution)/shard_map/ppermute | solution.py:104
  54.4 5.2 %collective-permute-start.9 = (bf16[136,256]{1,0:T(8,128)(2,1)S(1)}, bf16[136,256]{1,0:T(8,128)(2,1)S(1)}, u32[]{:S(2)}, u32[]{:S(2)}) collective-permute-start(bf16[136,256]{1,0:T(8,128)(2,1)S(1)} %add_convert_fusion.2), channel_id=1, source_target_pairs={{0,8},{4,12},{8,0},{12,4},{16,24},{20,28},{24,16},{28,20},{1,9},{5... | collective-permute-start | bytes 208904 | tf_op jit(solution)/shard_map/ppermute | solution.py:99
  59.7 4.5 %collective-permute-start.12 = (bf16[136,256]{1,0:T(8,128)(2,1)S(1)}, bf16[136,256]{1,0:T(8,128)(2,1)S(1)}, u32[]{:S(2)}, u32[]{:S(2)}) collective-permute-start(bf16[136,256]{1,0:T(8,128)(2,1)S(1)} %add_convert_fusion.1), channel_id=1, source_target_pairs={{0,1},{1,0},{2,3},{3,2},{4,5},{5,4},{6,7},{7,6},{8,9},{9,8},{10,11... | collective-permute-start | bytes 208904 | tf_op jit(solution)/shard_map/ppermute | solution.py:99
  59.9 6.8 %collective-permute-start.13 = (bf16[136,256]{1,0:T(8,128)(2,1)S(1)}, bf16[136,256]{1,0:T(8,128)(2,1)S(1)}, u32[]{:S(2)}, u32[]{:S(2)}) collective-permute-start(bf16[136,256]{1,0:T(8,128)(2,1)S(1)} %add_convert_fusion.1), channel_id=1, source_target_pairs={{0,2},{1,3},{2,0},{3,1},{4,6},{5,7},{6,4},{7,5},{8,10},{9,11},{10,... | collective-permute-start | bytes 208904 | tf_op jit(solution)/shard_map/ppermute | solution.py:103
  61.7 6.2 %collective-permute-start.14 = (bf16[136,256]{1,0:T(8,128)(2,1)S(1)}, bf16[136,256]{1,0:T(8,128)(2,1)S(1)}, u32[]{:S(2)}, u32[]{:S(2)}) collective-permute-start(bf16[136,256]{1,0:T(8,128)(2,1)S(1)} %add_convert_fusion.1), channel_id=1, source_target_pairs={{0,3},{1,2},{2,1},{3,0},{4,7},{5,6},{6,5},{7,4},{8,11},{9,10},{10,... | collective-permute-start | bytes 208904 | tf_op jit(solution)/shard_map/ppermute | solution.py:104
  68.0 1.3 %collective-permute-start.15 = (bf16[136,256]{1,0:T(8,128)(2,1)S(1)}, bf16[136,256]{1,0:T(8,128)(2,1)S(1)}, u32[]{:S(2)}, u32[]{:S(2)}) collective-permute-start(bf16[136,256]{1,0:T(8,128)(2,1)S(1)} %add_convert_fusion), channel_id=1, source_target_pairs={{0,4},{4,0},{8,12},{12,8},{16,20},{20,16},{24,28},{28,24},{1,5},{5... | collective-permute-start | bytes 208904 | tf_op jit(solution)/shard_map/ppermute | solution.py:171
  69.3 0.6 copy-start.8
  70.5 0.8 %slice-start = ((bf16[136,256]{1,0:T(8,128)(2,1)}), bf16[128,256]{1,0:T(8,128)(2,1)S(1)}, s32[]{:S(2)}) async-start(bf16[136,256]{1,0:T(8,128)(2,1)} %copy-done.8), calls=%async_computation.1 | async-start | bytes 131072 | tf_op jit(solution)/shard_map/slice | solution.py:176

commit v2 on v1

v2 whole, which is shorter than its diff:
```python
import jax
import jax.numpy as jnp
from jax import lax
from jax.experimental import pallas as pl
from jax.experimental.pallas import tpu as pltpu
from jax.sharding import PartitionSpec as P

VMEM = pl.BlockSpec(memory_space=pltpu.VMEM)
SMEM = pl.BlockSpec(memory_space=pltpu.SMEM)
PARAMS = pltpu.CompilerParams(vmem_limit_bytes=32 * 1024 * 1024)
GELU_C = 0.7978845608028654


LATIN = ((1, 0, 2, 3), (3, 2, 0, 1), (0, 1, 3, 2), (2, 3, 1, 0))
LATIN_BITS = sum(
    to << (2 * (4 * plane + rep)) for plane, row in enumerate(LATIN) for rep, to in enumerate(row)
)


def chip_of(plane, rep, rep_size):
    if rep_size != 4:
        return plane ^ rep
    if isinstance(plane, int):
        return LATIN[plane][rep]
    bits = jnp.int32(LATIN_BITS - (1 << 32) if LATIN_BITS >> 31 else LATIN_BITS)
    return lax.shift_right_logical(bits, 2 * (4 * plane + rep)) & 3


def column_of(row, width):
    return jnp.transpose(jnp.broadcast_to(row, (width, row.shape[1])))


def scale_kernel(sections, features_ref, degree_ref, *out_refs):
    width = features_ref.shape[1] // 2
    inv_root = column_of(lax.rsqrt(degree_ref[...].astype(jnp.float32)), width)
    halves = []
    for half in range(2):
        part = features_ref[:, half * width : (half + 1) * width].astype(jnp.float32)
        halves.append((part * inv_root).astype(jnp.bfloat16))
    odd = (lax.axis_index("dom") // sections) % 2
    for out_ref, first, second in zip(out_refs, halves, halves[::-1]):
        out_ref[...] = jnp.where(odd == 0, first, second)


def cast_kernel(count_ref, out_ref):
    out_ref[...] = count_ref[0].reshape(out_ref.shape).astype(jnp.float32).astype(jnp.bfloat16)


def join_kernel(first_ref, second_ref, out_ref):
    rows = first_ref.shape[0]
    out_ref[:rows, :] = first_ref[...]
    out_ref[rows:, :] = second_ref[...]


def aggregate_kernel(dom_size, rep_size, sections, *refs):
    code_refs, tile_refs, refs = refs[:2], refs[2:4], refs[4:]
    piece_refs, refs = refs[:dom_size], refs[dom_size:]
    out_refs, (held, acc) = refs[:rep_size], refs[rep_size:]
    slots, block = tile_refs[0].shape[0] // sections, tile_refs[0].shape[1]
    block_count = acc.shape[0]
    per_piece = piece_refs[0].shape[0] // block
    per_slice = per_piece // 2
    for mask, piece_ref in enumerate(piece_refs):
        for at in range(per_piece):
            held[mask * per_piece + at] = piece_ref[at * block : (at + 1) * block, :]
    acc[...] = jnp.zeros_like(acc)
    dom, rep = lax.axis_index("dom"), lax.axis_index("rep")

    for which in range(2):
        code_ref, tile_ref = code_refs[which], tile_refs[which]

        def slot_step(at):
            section, slot = at // slots, at % slots
            code = code_ref[0, section, slot]
            row, col = code // block_count, code % block_count
            chip = chip_of(rep ^ which, col // per_slice, rep_size)
            mask = (chip * sections + section) ^ dom
            rows = held[mask * per_piece + which * per_slice + col % per_slice]
            acc[row] += jnp.dot(tile_ref[at], rows, preferred_element_type=jnp.float32)

        if sections * slots <= 8:
            for at in range(sections * slots):
                slot_step(at)
        else:
            lax.fori_loop(0, sections * slots, lambda at, c: (slot_step(at), c)[1], 0)

    for mask, out_ref in enumerate(out_refs):
        for at in range(per_slice):
            part = acc[(rep ^ mask) * per_slice + at]
            out_ref[at * block : (at + 1) * block, :] = part.astype(jnp.bfloat16)


def dense_kernel(rep_size, *refs):
    part_refs, refs = refs[:rep_size], refs[rep_size:]
    features_ref, degree_ref, weight_ref, bias_ref, cotangent_ref, out_ref, keep_ref, send_ref = refs
    width = features_ref.shape[1]
    inv_root = column_of(lax.rsqrt(degree_ref[...].astype(jnp.float32)), width // 2)
    inv_root = jnp.concatenate([inv_root, inv_root], axis=1)
    sums = [0.0, 0.0]
    for mask, part_ref in enumerate(part_refs):
        sums[mask % 2] += part_ref[...].astype(jnp.float32)
    odd = lax.axis_index("rep") % 2
    agg = jnp.concatenate(
        [jnp.where(odd == 0, sums[0], sums[1]), jnp.where(odd == 0, sums[1], sums[0])], axis=1
    )
    scaled = (features_ref[...].astype(jnp.float32) * inv_root).astype(jnp.bfloat16)
    mixed = ((agg + scaled.astype(jnp.float32)) * inv_root).astype(jnp.bfloat16)
    pre = jnp.dot(mixed, weight_ref[...], preferred_element_type=jnp.float32) + bias_ref[...]
    square = pre * pre
    bent = jnp.tanh(GELU_C * (pre + 0.044715 * (square * pre)))
    half = 0.5 * (1.0 + bent)
    out_ref[...] = (pre * half).astype(jnp.bfloat16)
    inner = GELU_C * (1.0 + (3 * 0.044715) * square)
    slope = cotangent_ref[...].astype(jnp.float32) * (
        half + 0.5 * pre * ((1.0 - bent) * (1.0 + bent)) * inner
    )
    weight_term = lax.dot_general(
        mixed, slope.astype(jnp.bfloat16), (((0,), (0,)), ((), ())),
        preferred_element_type=jnp.float32,
    )
    bias_term = jnp.sum(slope, axis=0, keepdims=True)
    kept = width // 2
    top, bottom = weight_term[:kept], weight_term[kept:]
    core = lax.axis_index("dom") % 2
    keep_ref[:kept, :] = jnp.where(core == 0, top, bottom)
    send_ref[:kept, :] = jnp.where(core == 0, bottom, top)
    extra = jnp.broadcast_to(bias_term, (keep_ref.shape[0] - kept, width))
    keep_ref[kept:, :] = extra
    send_ref[kept:, :] = extra


def finish_kernel(mine_ref, other_ref, weight_ref, bias_ref):
    kept = weight_ref.shape[0] // 2
    first = lax.axis_index("dom") % 2 == 0
    mine = mine_ref[...].astype(jnp.float32)
    other = other_ref[...].astype(jnp.float32)
    weight_ref[:kept, :] = jnp.where(first, mine[:kept], other[:kept])
    weight_ref[kept:, :] = jnp.where(first, other[:kept], mine[:kept])
    bias_ref[...] = mine[kept : kept + 1]


def xor_pairs(size, mask):
    return [(at, at ^ mask) for at in range(size)]


def exchange_sum(value, axis, masks):
    size = lax.axis_size(axis)
    while masks:
        now, masks = masks[:2], masks[2:]
        first = lax.ppermute(value, axis, xor_pairs(size, now[0]))
        if len(now) == 1:
            total = value.astype(jnp.float32) + first.astype(jnp.float32)
        else:
            second = lax.ppermute(value, axis, xor_pairs(size, now[1]))
            third = lax.ppermute(value, axis, xor_pairs(size, now[0] ^ now[1]))
            total = (value.astype(jnp.float32) + first.astype(jnp.float32)) + (
                second.astype(jnp.float32) + third.astype(jnp.float32)
            )
        value = total.astype(value.dtype)
    return value


def bits_of(size):
    return [1 << at for at in range(size.bit_length() - 1)]


def on_device(features, degree, tile_row, tile_col, tile_count, tile_live, weight, bias, cotangent):
    row_count, width = features.shape
    dom_size, rep_size = lax.axis_size("dom"), lax.axis_size("rep")
    sections, slots, block = tile_count.shape[1], tile_count.shape[2], tile_count.shape[3]
    block_count = row_count * rep_size // block
    degree_row = degree.reshape(1, row_count)
    bf16, f32 = jnp.bfloat16, jnp.float32
    half = jax.ShapeDtypeStruct((row_count, width // 2), bf16)

    outgoing = pl.pallas_call(
        lambda *refs: scale_kernel(sections, *refs),
        out_shape=(half, half), in_specs=[VMEM, VMEM], out_specs=(VMEM, VMEM), name="scale",
    )(features, degree_row)
    arrived = []
    for flip, part in enumerate(outgoing):
        moves = []
        for dom in range(dom_size):
            plane = dom // sections
            for rep in range(rep_size):
                target = chip_of(plane, rep, rep_size) * sections + dom % sections
                moves.append((dom * rep_size + rep, target * rep_size + (plane ^ flip)))
        arrived.append(lax.ppermute(part, ("dom", "rep"), moves))

    tiles = pl.pallas_call(
        cast_kernel,
        out_shape=jax.ShapeDtypeStruct((sections * slots, block, block), bf16),
        in_specs=[VMEM], out_specs=VMEM, compiler_params=PARAMS, name="cast",
    )(tile_count)
    codes = tile_row * block_count + tile_col
    pair = xor_pairs(rep_size, 1)
    their_codes = lax.ppermute(codes, "rep", pair)
    their_tiles = lax.ppermute(tiles, "rep", pair)

    pieces = [None] * dom_size
    pieces[0] = pl.pallas_call(
        join_kernel,
        out_shape=jax.ShapeDtypeStruct((2 * row_count, width // 2), bf16),
        in_specs=[VMEM, VMEM], out_specs=VMEM, name="join",
    )(*arrived)
    for mask in range(2, dom_size, 2):
        pieces[mask] = lax.ppermute(pieces[0], "dom", xor_pairs(dom_size, mask))
    for mask in range(0, dom_size, 2):
        pieces[mask + 1] = lax.ppermute(pieces[mask], "dom", xor_pairs(dom_size, 1))

    held_shape = (dom_size * 2 * row_count // block, block, width // 2)
    partials = pl.pallas_call(
        lambda *refs: aggregate_kernel(dom_size, rep_size, sections, *refs),
        out_shape=(half,) * rep_size,
        in_specs=[SMEM, SMEM] + [VMEM] * (2 + dom_size),
        out_specs=(VMEM,) * rep_size,
        scratch_shapes=[
            pltpu.VMEM(held_shape, bf16),
            pltpu.VMEM((block_count, block, width // 2), f32),
        ],
        compiler_params=PARAMS,
        name="aggregate",
    )(codes, their_codes, tiles, their_tiles, *pieces)

    parts = [partials[0]]
    for mask in range(1, rep_size):
        parts.append(lax.ppermute(partials[mask], "rep", xor_pairs(rep_size, mask)))

    share = jax.ShapeDtypeStruct((width // 2 + 16, width), f32)
    outcome, keep, send = pl.pallas_call(
        lambda *refs: dense_kernel(rep_size, *refs),
        out_shape=(jax.ShapeDtypeStruct((row_count, width), bf16), share, share),
        in_specs=[VMEM] * (rep_size + 5),
        out_specs=(VMEM,) * 3,
        compiler_params=PARAMS,
        name="dense",
    )(*parts, features, degree_row, weight, bias.reshape(1, width), cotangent)

    swap = xor_pairs(dom_size, 1)
    mine = (keep + lax.ppermute(send, "dom", swap)).astype(bf16)
    mine = exchange_sum(mine, "dom", bits_of(dom_size)[1:])
    mine = exchange_sum(mine, "rep", bits_of(rep_size))
    other = lax.ppermute(mine, "dom", swap)
    weight_grad, bias_grad = pl.pallas_call(
        finish_kernel,
        out_shape=(
            jax.ShapeDtypeStruct((width, width), f32), jax.ShapeDtypeStruct((1, width), f32),
        ),
        in_specs=[VMEM, VMEM], out_specs=(VMEM, VMEM), name="finish",
    )(mine, other)
    return (outcome, weight_grad, bias_grad.reshape(width))


def solution(mesh):
    return jax.shard_map(
        on_device,
        mesh=mesh,
        in_specs=(
            P(("dom", "rep"), None),
            P(("dom", "rep")),
            P("dom", "rep", None),
            P("dom", "rep", None),
            P("dom", "rep", None, None, None),
            P("dom", "rep"),
            P(),
            P(),
            P(("dom", "rep"), None),
        ),
        out_specs=(P(("dom", "rep"), None), P(), P()),
        check_vma=False,
    )
```

time: 72.4 us -> 63.5 us (0.88)
  blocking collectives: 19.8 us -> 0 us
  waiting for transfers between devices: 16.4 us -> 24.4 us
  Pallas kernels: 3.72 us -> 7.01 us
  other arithmetic: 1.4 us -> 0.1 us
    all_to_all x1 -> x0, blocking collectives: 19.8 us -> none  [on_device(): lax.all_to_all(partial.reshape(rep_size, row_count, width), 'rep', 0, 0)]
    ppermute x5 -> x11, waiting for transfers between devices: 6.89 us -> 12.9 us  [the longest x3 5.23 us: on_device(): parts.append(lax.ppermute(partials[mask], 'rep', xor_pairs(rep_size, mask)))]
    pallas_call x3 -> x6, Pallas kernels: 3.72 us -> 7.01 us  [the longest x1 1.67 us: on_device(): pl.pallas_call(lambda *refs: scale_kernel(sections, *refs), out_shape=(ha...]
    ppermute x2, waiting for transfers between devices: 2.22 us -> 4.41 us  [exchange_sum(): third = lax.ppermute(value, axis, xor_pairs(size, now[0] ^ now[1]))]
    unnamed x18 -> x26, local copies, waits for them, and re-layouts: 2.36 us -> 3.88 us
    convert_element_type x3 -> x1, other arithmetic: 1.3 us -> 0.02 us  [on_device(): mine = (keep + lax.ppermute(send, 'dom', swap)).astype(bf16)]
    slice x2 -> x0, local copies, waits for them, and re-layouts: 0.83 us -> none  [on_device(): top[:kept]]
    ppermute x2, waiting for transfers between devices: 0.78 us -> 0.01 us  [exchange_sum(): first = lax.ppermute(value, axis, xor_pairs(size, now[0]))]
  transfers between devices with their start and end apart: 16 -> 22, of which waited for: 11 -> 13; matrix products, arithmetic and copies ran while one was open for 0% -> 0% of each run, Pallas kernels for 0% -> 3%
where the time goes in v2:
time: 63.5 us; the launch traced here: 63.2 us
  starting transfers between devices  27 us (43%)
  waiting for transfers between devices  24.4 us (38%)
  Pallas kernels  7.01 us (11%)
  local copies, waits for them, and re-layouts  3.88 us (6%)
  between operations  0.79 us (1%)
    ppermute x2, starting transfers between devices, on_device(): arrived.append(lax.ppermute(part, ('dom', 'rep'), moves))  7.34 us
    ppermute x3, waiting for transfers between devices, on_device(): parts.append(lax.ppermute(partials[mask], 'rep', xor_pairs(rep_size, mask)))  5.23 us
    ppermute x3, starting transfers between devices, on_device(): pieces[mask] = lax.ppermute(pieces[0], 'dom', xor_pairs(dom_size, mask))  5.08 us
    ppermute x3, starting transfers between devices, on_device(): parts.append(lax.ppermute(partials[mask], 'rep', xor_pairs(rep_size, mask)))  4.45 us
    ppermute x2, waiting for transfers between devices, exchange_sum(): second = lax.ppermute(value, axis, xor_pairs(size, now[1]))  4.44 us
    ppermute x2, waiting for transfers between devices, exchange_sum(): third = lax.ppermute(value, axis, xor_pairs(size, now[0] ^ now[1]))  4.41 us
    unnamed x26, local copies, waits for them, and re-layouts  3.88 us
    ppermute x2, starting transfers between devices, exchange_sum(): third = lax.ppermute(value, axis, xor_pairs(size, now[0] ^ now[1]))  3.41 us
  transfers between devices with their start and end apart: 22, of which 13 were waited for; matrix products, arithmetic and copies ran while one was open for 0% of the time, Pallas kernels for 3%

profile of v2, /device:TPU:0, one launch (start us, length us, event | category | flops | bytes accessed | tf_op | source)
XLA Modules:
  0.0 63.2 jit_solution(9834937831062162009)
XLA Ops:
  0.6 1.7 %scale.1 = (bf16[256,128]{1,0:T(8,128)(2,1)}, bf16[256,128]{1,0:T(8,128)(2,1)}) custom-call(bf16[256,256]{1,0:T(8,128)(2,1)} %refs_4_.1, s32[1,256]{1,0:T(1,128)} %bitcast.3), custom_call_target="tpu_custom_call" | custom-call | tf_op jit(solution)/shard_map/scale/pallas_call | solution.py:176
  2.3 2.9 %collective-permute-start.2 = (bf16[256,128]{1,0:T(8,128)(2,1)}, bf16[256,128]{1,0:T(8,128)(2,1)S(1)}, u32[]{:S(2)}, u32[]{:S(2)}) collective-permute-start(bf16[256,128]{1,0:T(8,128)(2,1)} %get-tuple-element.14), channel_id=1, source_target_pairs={{0,8},{1,0},{2,16},{3,24},{4,12},{5,4},{6,20},{7,28},{8,25},{9,17}... | collective-permute-start | bytes 196616 | tf_op jit(solution)/shard_map/ppermute | solution.py:188
  5.2 4.4 %collective-permute-start.3 = (bf16[256,128]{1,0:T(8,128)(2,1)}, bf16[256,128]{1,0:T(8,128)(2,1)S(1)}, u32[]{:S(2)}, u32[]{:S(2)}) collective-permute-start(bf16[256,128]{1,0:T(8,128)(2,1)} %get-tuple-element.15), channel_id=1, source_target_pairs={{0,9},{1,1},{2,17},{3,25},{4,13},{5,5},{6,21},{7,29},{8,24},{9,16}... | collective-permute-start | bytes 196616 | tf_op jit(solution)/shard_map/ppermute | solution.py:188
  9.7 1.0 %copy-done.2 = s32[1,2,4,128,128]{4,3,2,1,0:T(8,128)S(1)} copy-done((s32[1,2,4,128,128]{4,3,2,1,0:T(8,128)S(1)}, s32[1,2,4,128,128]{4,3,2,1,0:T(8,128)}, u32[]{:S(2)}) %copy-start.2) | copy-done | bytes 524312
  10.8 3.3 %collective-permute-done.3.second_ref = bf16[256,128]{1,0:T(8,128)(2,1)S(1)} collective-permute-done((bf16[256,128]{1,0:T(8,128)(2,1)}, bf16[256,128]{1,0:T(8,128)(2,1)S(1)}, u32[]{:S(2)}, u32[]{:S(2)}) %collective-permute-start.3) | collective-permute-done | bytes 65568 | tf_op jit(solution)/shard_map/ppermute | solution.py:188
  14.8 1.6 %join.1.refs_4_ = bf16[512,128]{1,0:T(8,128)(2,1)} custom-call(bf16[256,128]{1,0:T(8,128)(2,1)} %copy-done.9, bf16[256,128]{1,0:T(8,128)(2,1)} %copy-done.10), custom_call_target="tpu_custom_call" | custom-call | tf_op jit(solution)/shard_map/join/pallas_call | solution.py:201
  16.4 1.9 %collective-permute-start.9 = (bf16[512,128]{1,0:T(8,128)(2,1)}, bf16[512,128]{1,0:T(8,128)(2,1)S(1)}, u32[]{:S(2)}, u32[]{:S(2)}) collective-permute-start(bf16[512,128]{1,0:T(8,128)(2,1)} %join.1.refs_4_), channel_id=1, source_target_pairs={{0,24},{4,28},{8,16},{12,20},{16,8},{20,12},{24,0},{28,4},{1,25},{... | collective-permute-start | bytes 393224 | tf_op jit(solution)/shard_map/ppermute | solution.py:207
  18.3 1.9 %collective-permute-start.7 = (bf16[512,128]{1,0:T(8,128)(2,1)}, bf16[512,128]{1,0:T(8,128)(2,1)S(1)}, u32[]{:S(2)}, u32[]{:S(2)}) collective-permute-start(bf16[512,128]{1,0:T(8,128)(2,1)} %join.1.refs_4_), channel_id=1, source_target_pairs={{0,16},{4,20},{8,24},{12,28},{16,0},{20,4},{24,8},{28,12},{1,17},{... | collective-permute-start | bytes 393224 | tf_op jit(solution)/shard_map/ppermute | solution.py:207
  20.2 1.3 %collective-permute-start.5 = (bf16[512,128]{1,0:T(8,128)(2,1)}, bf16[512,128]{1,0:T(8,128)(2,1)S(1)}, u32[]{:S(2)}, u32[]{:S(2)}) collective-permute-start(bf16[512,128]{1,0:T(8,128)(2,1)} %join.1.refs_4_), channel_id=1, source_target_pairs={{0,8},{4,12},{8,0},{12,4},{16,24},{20,28},{24,16},{28,20},{1,9},{5... | collective-permute-start | bytes 393224 | tf_op jit(solution)/shard_map/ppermute | solution.py:207
  21.5 1.4 %collective-permute-start = (s32[1,2,4]{2,1,0:T(2,128)S(1)}, s32[1,2,4]{2,1,0:T(2,128)S(1)}, u32[]{:S(2)}, u32[]{:S(2)}) collective-permute-start(s32[1,2,4]{2,1,0:T(2,128)S(1)} %multiply_add_fusion.refs_0_), channel_id=1, source_target_pairs={{0,1},{1,0},{2,3},{3,2},{4,5},{5,4},{6,7},{7,6},{8,9},{9,8},{10,11... | collective-permute-start | bytes 104 | tf_op jit(solution)/shard_map/ppermute | solution.py:197
  22.9 2.3 %collective-permute-done.refs_1_ = s32[1,2,4]{2,1,0:T(2,128)S(1)} collective-permute-done((s32[1,2,4]{2,1,0:T(2,128)S(1)}, s32[1,2,4]{2,1,0:T(2,128)S(1)}, u32[]{:S(2)}, u32[]{:S(2)}) %collective-permute-start) | collective-permute-done | bytes 64 | tf_op jit(solution)/shard_map/ppermute | solution.py:197
  25.7 0.7 %collective-permute-done.5.refs_6_ = bf16[512,128]{1,0:T(8,128)(2,1)S(1)} collective-permute-done((bf16[512,128]{1,0:T(8,128)(2,1)}, bf16[512,128]{1,0:T(8,128)(2,1)S(1)}, u32[]{:S(2)}, u32[]{:S(2)}) %collective-permute-start.5) | collective-permute-done | bytes 131104 | tf_op jit(solution)/shard_map/ppermute | solution.py:207
  27.0 0.8 %collective-permute-done.6.refs_7_ = bf16[512,128]{1,0:T(8,128)(2,1)S(1)} collective-permute-done((bf16[512,128]{1,0:T(8,128)(2,1)S(1)}, bf16[512,128]{1,0:T(8,128)(2,1)S(1)}, u32[]{:S(2)}, u32[]{:S(2)}) %collective-permute-start.6) | collective-permute-done | bytes 131104 | tf_op jit(solution)/shard_map/ppermute | solution.py:209
  27.8 0.9 %copy-done.1 = bf16[512,128]{1,0:T(8,128)(2,1)S(1)} copy-done((bf16[512,128]{1,0:T(8,128)(2,1)S(1)}, bf16[512,128]{1,0:T(8,128)(2,1)}, u32[]{:S(2)}) %copy-start.1) | copy-done | bytes 131096
  28.7 1.0 %aggregate.1 = (bf16[256,128]{1,0:T(8,128)(2,1)S(1)}, bf16[256,128]{1,0:T(8,128)(2,1)S(1)}, bf16[256,128]{1,0:T(8,128)(2,1)S(1)}, bf16[256,128]{1,0:T(8,128)(2,1)S(1)}) custom-call(s32[1,2,4]{2,1,0:T(2,128)S(1)} %multiply_add_fusion.refs_0_, s32[1,2,4]{2,1,0:T(2,128)S(1)} %collective-permute-done.refs_1_, bf16[8,128,128]{2,1,0:T(8,128)(2,1)S(1)} %cast.1.refs_2_, ...), custom_call_target="tpu_custom_call" | custom-call | tf_op jit(solution)/shard_map/aggregate/pallas_call | solution.py:212
  29.8 1.6 %collective-permute-start.11 = (bf16[256,128]{1,0:T(8,128)(2,1)S(1)}, bf16[256,128]{1,0:T(8,128)(2,1)S(1)}, u32[]{:S(2)}, u32[]{:S(2)}) collective-permute-start(bf16[256,128]{1,0:T(8,128)(2,1)S(1)} %get-tuple-element.17), channel_id=1, source_target_pairs={{0,1},{1,0},{2,3},{3,2},{4,5},{5,4},{6,7},{7,6},{8,9},{9,8},{10,11... | collective-permute-start | bytes 196616 | tf_op jit(solution)/shard_map/ppermute | solution.py:227
  31.4 1.8 %collective-permute-start.12 = (bf16[256,128]{1,0:T(8,128)(2,1)S(1)}, bf16[256,128]{1,0:T(8,128)(2,1)S(1)}, u32[]{:S(2)}, u32[]{:S(2)}) collective-permute-start(bf16[256,128]{1,0:T(8,128)(2,1)S(1)} %get-tuple-element.18), channel_id=1, source_target_pairs={{0,2},{1,3},{2,0},{3,1},{4,6},{5,7},{6,4},{7,5},{8,10},{9,11},{10,... | collective-permute-start | bytes 196616 | tf_op jit(solution)/shard_map/ppermute | solution.py:227
  33.1 1.1 %collective-permute-start.13 = (bf16[256,128]{1,0:T(8,128)(2,1)S(1)}, bf16[256,128]{1,0:T(8,128)(2,1)S(1)}, u32[]{:S(2)}, u32[]{:S(2)}) collective-permute-start(bf16[256,128]{1,0:T(8,128)(2,1)S(1)} %get-tuple-element.19), channel_id=1, source_target_pairs={{0,3},{1,2},{2,1},{3,0},{4,7},{5,6},{6,5},{7,4},{8,11},{9,10},{10,... | collective-permute-start | bytes 196616 | tf_op jit(solution)/shard_map/ppermute | solution.py:227
  34.2 5.2 %collective-permute-done.12.refs_2_ = bf16[256,128]{1,0:T(8,128)(2,1)S(1)} collective-permute-done((bf16[256,128]{1,0:T(8,128)(2,1)S(1)}, bf16[256,128]{1,0:T(8,128)(2,1)S(1)}, u32[]{:S(2)}, u32[]{:S(2)}) %collective-permute-start.12) | collective-permute-done | bytes 65568 | tf_op jit(solution)/shard_map/ppermute | solution.py:227
  40.1 1.1 %dense.1 = (bf16[256,256]{1,0:T(8,128)(2,1)}, f32[144,256]{1,0:T(8,128)S(1)}, f32[144,256]{1,0:T(8,128)S(1)}) custom-call(bf16[256,128]{1,0:T(8,128)(2,1)S(1)} %get-tuple-element.16.refs_0_, bf16[256,128]{1,0:T(8,128)(2,1)S(1)} %collective-permute-done.11.refs_1_, bf16[256,128]{1,0:T(8,128)(2,1)S(1)} %collective-permute-done.12.refs_2_, ...), custom_call_target="tpu_custom_call" | custom-call | tf_op jit(solution)/shard_map/dense/pallas_call | solution.py:230
  41.2 1.4 %collective-permute-done.14 = f32[144,256]{1,0:T(8,128)S(1)} collective-permute-done((f32[144,256]{1,0:T(8,128)S(1)}, f32[144,256]{1,0:T(8,128)S(1)}, u32[]{:S(2)}, u32[]{:S(2)}) %collective-permute-start.14) | collective-permute-done | bytes 147488 | tf_op jit(solution)/shard_map/ppermute | solution.py:240
  42.6 1.7 %collective-permute-start.17 = (bf16[144,256]{1,0:T(8,128)(2,1)S(1)}, bf16[144,256]{1,0:T(8,128)(2,1)S(1)}, u32[]{:S(2)}, u32[]{:S(2)}) collective-permute-start(bf16[144,256]{1,0:T(8,128)(2,1)S(1)} %add_convert_fusion.2), channel_id=1, source_target_pairs={{0,24},{4,28},{8,16},{12,20},{16,8},{20,12},{24,0},{28,4},{1,25},{... | collective-permute-start | bytes 221192 | tf_op jit(solution)/shard_map/ppermute | solution.py:155
  44.8 1.4 %collective-permute-start.15 = (bf16[144,256]{1,0:T(8,128)(2,1)S(1)}, bf16[144,256]{1,0:T(8,128)(2,1)S(1)}, u32[]{:S(2)}, u32[]{:S(2)}) collective-permute-start(bf16[144,256]{1,0:T(8,128)(2,1)S(1)} %add_convert_fusion.2), channel_id=1, source_target_pairs={{0,8},{4,12},{8,0},{12,4},{16,24},{20,28},{24,16},{28,20},{1,9},{5... | collective-permute-start | bytes 221192 | tf_op jit(solution)/shard_map/ppermute | solution.py:150
  46.1 1.8 %collective-permute-done.17 = bf16[144,256]{1,0:T(8,128)(2,1)S(1)} collective-permute-done((bf16[144,256]{1,0:T(8,128)(2,1)S(1)}, bf16[144,256]{1,0:T(8,128)(2,1)S(1)}, u32[]{:S(2)}, u32[]{:S(2)}) %collective-permute-start.17) | collective-permute-done | bytes 73760 | tf_op jit(solution)/shard_map/ppermute | solution.py:155
  48.0 1.5 %collective-permute-done.16 = bf16[144,256]{1,0:T(8,128)(2,1)S(1)} collective-permute-done((bf16[144,256]{1,0:T(8,128)(2,1)S(1)}, bf16[144,256]{1,0:T(8,128)(2,1)S(1)}, u32[]{:S(2)}, u32[]{:S(2)}) %collective-permute-start.16) | collective-permute-done | bytes 73760 | tf_op jit(solution)/shard_map/ppermute | solution.py:154
  49.5 1.7 %collective-permute-start.20 = (bf16[144,256]{1,0:T(8,128)(2,1)S(1)}, bf16[144,256]{1,0:T(8,128)(2,1)S(1)}, u32[]{:S(2)}, u32[]{:S(2)}) collective-permute-start(bf16[144,256]{1,0:T(8,128)(2,1)S(1)} %add_convert_fusion.1), channel_id=1, source_target_pairs={{0,3},{1,2},{2,1},{3,0},{4,7},{5,6},{6,5},{7,4},{8,11},{9,10},{10,... | collective-permute-start | bytes 221192 | tf_op jit(solution)/shard_map/ppermute | solution.py:155
  51.2 1.5 %collective-permute-start.19 = (bf16[144,256]{1,0:T(8,128)(2,1)S(1)}, bf16[144,256]{1,0:T(8,128)(2,1)S(1)}, u32[]{:S(2)}, u32[]{:S(2)}) collective-permute-start(bf16[144,256]{1,0:T(8,128)(2,1)S(1)} %add_convert_fusion.1), channel_id=1, source_target_pairs={{0,2},{1,3},{2,0},{3,1},{4,6},{5,7},{6,4},{7,5},{8,10},{9,11},{10,... | collective-permute-start | bytes 221192 | tf_op jit(solution)/shard_map/ppermute | solution.py:154
  52.6 1.3 %collective-permute-start.18 = (bf16[144,256]{1,0:T(8,128)(2,1)S(1)}, bf16[144,256]{1,0:T(8,128)(2,1)S(1)}, u32[]{:S(2)}, u32[]{:S(2)}) collective-permute-start(bf16[144,256]{1,0:T(8,128)(2,1)S(1)} %add_convert_fusion.1), channel_id=1, source_target_pairs={{0,1},{1,0},{2,3},{3,2},{4,5},{5,4},{6,7},{7,6},{8,9},{9,8},{10,11... | collective-permute-start | bytes 221192 | tf_op jit(solution)/shard_map/ppermute | solution.py:150
  53.9 2.6 %collective-permute-done.20 = bf16[144,256]{1,0:T(8,128)(2,1)S(1)} collective-permute-done((bf16[144,256]{1,0:T(8,128)(2,1)S(1)}, bf16[144,256]{1,0:T(8,128)(2,1)S(1)}, u32[]{:S(2)}, u32[]{:S(2)}) %collective-permute-start.20) | collective-permute-done | bytes 73760 | tf_op jit(solution)/shard_map/ppermute | solution.py:155
  56.5 3.0 %collective-permute-done.19 = bf16[144,256]{1,0:T(8,128)(2,1)S(1)} collective-permute-done((bf16[144,256]{1,0:T(8,128)(2,1)S(1)}, bf16[144,256]{1,0:T(8,128)(2,1)S(1)}, u32[]{:S(2)}, u32[]{:S(2)}) %collective-permute-start.19) | collective-permute-done | bytes 73760 | tf_op jit(solution)/shard_map/ppermute | solution.py:154
  59.6 1.3 %collective-permute-done.21.other_ref = bf16[144,256]{1,0:T(8,128)(2,1)S(1)} collective-permute-done((bf16[144,256]{1,0:T(8,128)(2,1)S(1)}, bf16[144,256]{1,0:T(8,128)(2,1)S(1)}, u32[]{:S(2)}, u32[]{:S(2)}) %collective-permute-start.21) | collective-permute-done | bytes 73760 | tf_op jit(solution)/shard_map/ppermute | solution.py:243
  61.5 1.7 %finish.1 = (f32[256,256]{1,0:T(8,128)}, f32[1,256]{1,0:T(1,128)}) custom-call(bf16[144,256]{1,0:T(8,128)(2,1)} %copy-done.7, bf16[144,256]{1,0:T(8,128)(2,1)} %copy-done.8), custom_call_target="tpu_custom_call" | custom-call | tf_op jit(solution)/shard_map/finish/pallas_call | solution.py:244
  (48 shorter events, 3.8 us)
Async XLA Ops:
  2.3 8.5 %collective-permute-start.2 = (bf16[256,128]{1,0:T(8,128)(2,1)}, bf16[256,128]{1,0:T(8,128)(2,1)S(1)}, u32[]{:S(2)}, u32[]{:S(2)}) collective-permute-start(bf16[256,128]{1,0:T(8,128)(2,1)} %get-tuple-element.14), channel_id=1, source_target_pairs={{0,8},{1,0},{2,16},{3,24},{4,12},{5,4},{6,20},{7,28},{8,25},{9,17}... | collective-permute-start | bytes 196616 | tf_op jit(solution)/shard_map/ppermute | solution.py:188
  5.2 9.0 %collective-permute-start.3 = (bf16[256,128]{1,0:T(8,128)(2,1)}, bf16[256,128]{1,0:T(8,128)(2,1)S(1)}, u32[]{:S(2)}, u32[]{:S(2)}) collective-permute-start(bf16[256,128]{1,0:T(8,128)(2,1)} %get-tuple-element.15), channel_id=1, source_target_pairs={{0,9},{1,1},{2,17},{3,25},{4,13},{5,5},{6,21},{7,29},{8,24},{9,16}... | collective-permute-start | bytes 196616 | tf_op jit(solution)/shard_map/ppermute | solution.py:188
  9.6 1.0 %copy-start.2 = (s32[1,2,4,128,128]{4,3,2,1,0:T(8,128)S(1)}, s32[1,2,4,128,128]{4,3,2,1,0:T(8,128)}, u32[]{:S(2)}) copy-start(s32[1,2,4,128,128]{4,3,2,1,0:T(8,128)} %count_ref.1) | copy-start | bytes 1572868
  10.7 10.8 %copy-start.11 = (s32[1,2,4]{2,1,0:T(2,128)S(1)}, s32[1,2,4]{2,1,0:T(2,128)}, u32[]{:S(2)}) copy-start(s32[1,2,4]{2,1,0:T(2,128)} %param.12) | copy-start | bytes 100
  10.7 10.8 %copy-start.12 = (s32[1,2,4]{2,1,0:T(2,128)S(1)}, s32[1,2,4]{2,1,0:T(2,128)}, u32[]{:S(2)}) copy-start(s32[1,2,4]{2,1,0:T(2,128)} %param.11) | copy-start | bytes 100
  10.7 16.1 %collective-permute-start.1 = (bf16[8,128,128]{2,1,0:T(8,128)(2,1)S(1)}, bf16[8,128,128]{2,1,0:T(8,128)(2,1)S(1)}, u32[]{:S(2)}, u32[]{:S(2)}) collective-permute-start(bf16[8,128,128]{2,1,0:T(8,128)(2,1)S(1)} %cast.1.refs_2_), channel_id=1, source_target_pairs={{0,1},{1,0},{2,3},{3,2},{4,5},{5,4},{6,7},{7,6},{8,9},{9,8},{10,11... | collective-permute-start | bytes 786440 | tf_op jit(solution)/shard_map/ppermute | solution.py:198
  10.8 3.4 %copy-start.9 = (bf16[256,128]{1,0:T(8,128)(2,1)}, bf16[256,128]{1,0:T(8,128)(2,1)S(1)}, u32[]{:S(2)}) copy-start(bf16[256,128]{1,0:T(8,128)(2,1)S(1)} %collective-permute-done.2.first_ref) | copy-start | bytes 196612
  14.8 24.6 %copy-start.3 = (bf16[256,256]{1,0:T(8,128)(2,1)S(1)}, bf16[256,256]{1,0:T(8,128)(2,1)}, u32[]{:S(2)}) copy-start(bf16[256,256]{1,0:T(8,128)(2,1)} %refs_6_.1) | copy-start | bytes 393220
  14.8 24.6 %copy-start.4 = (bf16[256,256]{1,0:T(8,128)(2,1)S(1)}, bf16[256,256]{1,0:T(8,128)(2,1)}, u32[]{:S(2)}) copy-start(bf16[256,256]{1,0:T(8,128)(2,1)} %refs_8_.1) | copy-start | bytes 393220
  16.4 8.7 %collective-permute-start.9 = (bf16[512,128]{1,0:T(8,128)(2,1)}, bf16[512,128]{1,0:T(8,128)(2,1)S(1)}, u32[]{:S(2)}, u32[]{:S(2)}) collective-permute-start(bf16[512,128]{1,0:T(8,128)(2,1)} %join.1.refs_4_), channel_id=1, source_target_pairs={{0,24},{4,28},{8,16},{12,20},{16,8},{20,12},{24,0},{28,4},{1,25},{... | collective-permute-start | bytes 393224 | tf_op jit(solution)/shard_map/ppermute | solution.py:207
  18.3 7.3 %collective-permute-start.7 = (bf16[512,128]{1,0:T(8,128)(2,1)}, bf16[512,128]{1,0:T(8,128)(2,1)S(1)}, u32[]{:S(2)}, u32[]{:S(2)}) collective-permute-start(bf16[512,128]{1,0:T(8,128)(2,1)} %join.1.refs_4_), channel_id=1, source_target_pairs={{0,16},{4,20},{8,24},{12,28},{16,0},{20,4},{24,8},{28,12},{1,17},{... | collective-permute-start | bytes 393224 | tf_op jit(solution)/shard_map/ppermute | solution.py:207
  20.2 6.2 %collective-permute-start.5 = (bf16[512,128]{1,0:T(8,128)(2,1)}, bf16[512,128]{1,0:T(8,128)(2,1)S(1)}, u32[]{:S(2)}, u32[]{:S(2)}) collective-permute-start(bf16[512,128]{1,0:T(8,128)(2,1)} %join.1.refs_4_), channel_id=1, source_target_pairs={{0,8},{4,12},{8,0},{12,4},{16,24},{20,28},{24,16},{28,20},{1,9},{5... | collective-permute-start | bytes 393224 | tf_op jit(solution)/shard_map/ppermute | solution.py:207
  21.5 18.0 %copy-start = (bf16[256,256]{1,0:T(8,128)(2,1)S(1)}, bf16[256,256]{1,0:T(8,128)(2,1)}, u32[]{:S(2)}) copy-start(bf16[256,256]{1,0:T(8,128)(2,1)} %refs_4_.1) | copy-start | bytes 393220
  21.5 3.6 %collective-permute-start = (s32[1,2,4]{2,1,0:T(2,128)S(1)}, s32[1,2,4]{2,1,0:T(2,128)S(1)}, u32[]{:S(2)}, u32[]{:S(2)}) collective-permute-start(s32[1,2,4]{2,1,0:T(2,128)S(1)} %multiply_add_fusion.refs_0_), channel_id=1, source_target_pairs={{0,1},{1,0},{2,3},{3,2},{4,5},{5,4},{6,7},{7,6},{8,9},{9,8},{10,11... | collective-permute-start | bytes 104 | tf_op jit(solution)/shard_map/ppermute | solution.py:197
  25.2 1.7 %collective-permute-start.4 = (bf16[512,128]{1,0:T(8,128)(2,1)}, bf16[512,128]{1,0:T(8,128)(2,1)S(1)}, u32[]{:S(2)}, u32[]{:S(2)}) collective-permute-start(bf16[512,128]{1,0:T(8,128)(2,1)} %join.1.refs_4_), channel_id=1, source_target_pairs={{0,4},{4,0},{8,12},{12,8},{16,20},{20,16},{24,28},{28,24},{1,5},{5... | collective-permute-start | bytes 393224 | tf_op jit(solution)/shard_map/ppermute | solution.py:209
  25.2 1.7 %collective-permute-start.10 = (bf16[512,128]{1,0:T(8,128)(2,1)S(1)}, bf16[512,128]{1,0:T(8,128)(2,1)S(1)}, u32[]{:S(2)}, u32[]{:S(2)}) collective-permute-start(bf16[512,128]{1,0:T(8,128)(2,1)S(1)} %collective-permute-done.9.refs_10_), channel_id=1, source_target_pairs={{0,4},{4,0},{8,12},{12,8},{16,20},{20,16},{24,28},{28,24},{1,5},{5... | collective-permute-start | bytes 393224 | tf_op jit(solution)/shard_map/ppermute | solution.py:209
  25.7 1.3 %collective-permute-start.8 = (bf16[512,128]{1,0:T(8,128)(2,1)S(1)}, bf16[512,128]{1,0:T(8,128)(2,1)S(1)}, u32[]{:S(2)}, u32[]{:S(2)}) collective-permute-start(bf16[512,128]{1,0:T(8,128)(2,1)S(1)} %collective-permute-done.7.refs_8_), channel_id=1, source_target_pairs={{0,4},{4,0},{8,12},{12,8},{16,20},{20,16},{24,28},{28,24},{1,5},{5... | collective-permute-start | bytes 393224 | tf_op jit(solution)/shard_map/ppermute | solution.py:209
  26.5 1.3 %collective-permute-start.6 = (bf16[512,128]{1,0:T(8,128)(2,1)S(1)}, bf16[512,128]{1,0:T(8,128)(2,1)S(1)}, u32[]{:S(2)}, u32[]{:S(2)}) collective-permute-start(bf16[512,128]{1,0:T(8,128)(2,1)S(1)} %collective-permute-done.5.refs_6_), channel_id=1, source_target_pairs={{0,4},{4,0},{8,12},{12,8},{16,20},{20,16},{24,28},{28,24},{1,5},{5... | collective-permute-start | bytes 393224 | tf_op jit(solution)/shard_map/ppermute | solution.py:209
  27.8 0.9 %copy-start.1 = (bf16[512,128]{1,0:T(8,128)(2,1)S(1)}, bf16[512,128]{1,0:T(8,128)(2,1)}, u32[]{:S(2)}) copy-start(bf16[512,128]{1,0:T(8,128)(2,1)} %join.1.refs_4_) | copy-start | bytes 393220
  28.7 10.8 %copy-start.6 = (f32[256]{0:T(256)S(1)}, f32[256]{0:T(256)}, u32[]{:S(2)}) copy-start(f32[256]{0:T(256)} %param.15) | copy-start | bytes 3076
  29.8 4.5 %collective-permute-start.11 = (bf16[256,128]{1,0:T(8,128)(2,1)S(1)}, bf16[256,128]{1,0:T(8,128)(2,1)S(1)}, u32[]{:S(2)}, u32[]{:S(2)}) collective-permute-start(bf16[256,128]{1,0:T(8,128)(2,1)S(1)} %get-tuple-element.17), channel_id=1, source_target_pairs={{0,1},{1,0},{2,3},{3,2},{4,5},{5,4},{6,7},{7,6},{8,9},{9,8},{10,11... | collective-permute-start | bytes 196616 | tf_op jit(solution)/shard_map/ppermute | solution.py:227
  31.4 8.1 %collective-permute-start.12 = (bf16[256,128]{1,0:T(8,128)(2,1)S(1)}, bf16[256,128]{1,0:T(8,128)(2,1)S(1)}, u32[]{:S(2)}, u32[]{:S(2)}) collective-permute-start(bf16[256,128]{1,0:T(8,128)(2,1)S(1)} %get-tuple-element.18), channel_id=1, source_target_pairs={{0,2},{1,3},{2,0},{3,1},{4,6},{5,7},{6,4},{7,5},{8,10},{9,11},{10,... | collective-permute-start | bytes 196616 | tf_op jit(solution)/shard_map/ppermute | solution.py:227
  33.1 6.3 %collective-permute-start.13 = (bf16[256,128]{1,0:T(8,128)(2,1)S(1)}, bf16[256,128]{1,0:T(8,128)(2,1)S(1)}, u32[]{:S(2)}, u32[]{:S(2)}) collective-permute-start(bf16[256,128]{1,0:T(8,128)(2,1)S(1)} %get-tuple-element.19), channel_id=1, source_target_pairs={{0,3},{1,2},{2,1},{3,0},{4,7},{5,6},{6,5},{7,4},{8,11},{9,10},{10,... | collective-permute-start | bytes 196616 | tf_op jit(solution)/shard_map/ppermute | solution.py:227
  41.2 1.4 %collective-permute-start.14 = (f32[144,256]{1,0:T(8,128)S(1)}, f32[144,256]{1,0:T(8,128)S(1)}, u32[]{:S(2)}, u32[]{:S(2)}) collective-permute-start(f32[144,256]{1,0:T(8,128)S(1)} %get-tuple-element.22), channel_id=1, source_target_pairs={{0,4},{4,0},{8,12},{12,8},{16,20},{20,16},{24,28},{28,24},{1,5},{5... | collective-permute-start | bytes 442376 | tf_op jit(solution)/shard_map/ppermute | solution.py:240
  42.6 5.4 %collective-permute-start.17 = (bf16[144,256]{1,0:T(8,128)(2,1)S(1)}, bf16[144,256]{1,0:T(8,128)(2,1)S(1)}, u32[]{:S(2)}, u32[]{:S(2)}) collective-permute-start(bf16[144,256]{1,0:T(8,128)(2,1)S(1)} %add_convert_fusion.2), channel_id=1, source_target_pairs={{0,24},{4,28},{8,16},{12,20},{16,8},{20,12},{24,0},{28,4},{1,25},{... | collective-permute-start | bytes 221192 | tf_op jit(solution)/shard_map/ppermute | solution.py:155
  44.3 5.1 %collective-permute-start.16 = (bf16[144,256]{1,0:T(8,128)(2,1)S(1)}, bf16[144,256]{1,0:T(8,128)(2,1)S(1)}, u32[]{:S(2)}, u32[]{:S(2)}) collective-permute-start(bf16[144,256]{1,0:T(8,128)(2,1)S(1)} %add_convert_fusion.2), channel_id=1, source_target_pairs={{0,16},{4,20},{8,24},{12,28},{16,0},{20,4},{24,8},{28,12},{1,17},{... | collective-permute-start | bytes 221192 | tf_op jit(solution)/shard_map/ppermute | solution.py:154
  44.8 4.7 %collective-permute-start.15 = (bf16[144,256]{1,0:T(8,128)(2,1)S(1)}, bf16[144,256]{1,0:T(8,128)(2,1)S(1)}, u32[]{:S(2)}, u32[]{:S(2)}) collective-permute-start(bf16[144,256]{1,0:T(8,128)(2,1)S(1)} %add_convert_fusion.2), channel_id=1, source_target_pairs={{0,8},{4,12},{8,0},{12,4},{16,24},{20,28},{24,16},{28,20},{1,9},{5... | collective-permute-start | bytes 221192 | tf_op jit(solution)/shard_map/ppermute | solution.py:150
  49.5 7.0 %collective-permute-start.20 = (bf16[144,256]{1,0:T(8,128)(2,1)S(1)}, bf16[144,256]{1,0:T(8,128)(2,1)S(1)}, u32[]{:S(2)}, u32[]{:S(2)}) collective-permute-start(bf16[144,256]{1,0:T(8,128)(2,1)S(1)} %add_convert_fusion.1), channel_id=1, source_target_pairs={{0,3},{1,2},{2,1},{3,0},{4,7},{5,6},{6,5},{7,4},{8,11},{9,10},{10,... | collective-permute-start | bytes 221192 | tf_op jit(solution)/shard_map/ppermute | solution.py:155
  51.2 8.3 %collective-permute-start.19 = (bf16[144,256]{1,0:T(8,128)(2,1)S(1)}, bf16[144,256]{1,0:T(8,128)(2,1)S(1)}, u32[]{:S(2)}, u32[]{:S(2)}) collective-permute-start(bf16[144,256]{1,0:T(8,128)(2,1)S(1)} %add_convert_fusion.1), channel_id=1, source_target_pairs={{0,2},{1,3},{2,0},{3,1},{4,6},{5,7},{6,4},{7,5},{8,10},{9,11},{10,... | collective-permute-start | bytes 221192 | tf_op jit(solution)/shard_map/ppermute | solution.py:154
  52.6 6.9 %collective-permute-start.18 = (bf16[144,256]{1,0:T(8,128)(2,1)S(1)}, bf16[144,256]{1,0:T(8,128)(2,1)S(1)}, u32[]{:S(2)}, u32[]{:S(2)}) collective-permute-start(bf16[144,256]{1,0:T(8,128)(2,1)S(1)} %add_convert_fusion.1), channel_id=1, source_target_pairs={{0,1},{1,0},{2,3},{3,2},{4,5},{5,4},{6,7},{7,6},{8,9},{9,8},{10,11... | collective-permute-start | bytes 221192 | tf_op jit(solution)/shard_map/ppermute | solution.py:150
  59.5 1.3 %copy-start.7 = (bf16[144,256]{1,0:T(8,128)(2,1)}, bf16[144,256]{1,0:T(8,128)(2,1)S(1)}, u32[]{:S(2)}) copy-start(bf16[144,256]{1,0:T(8,128)(2,1)S(1)} %add_convert_fusion.mine_ref) | copy-start | bytes 221188
  59.5 1.3 %collective-permute-start.21 = (bf16[144,256]{1,0:T(8,128)(2,1)S(1)}, bf16[144,256]{1,0:T(8,128)(2,1)S(1)}, u32[]{:S(2)}, u32[]{:S(2)}) collective-permute-start(bf16[144,256]{1,0:T(8,128)(2,1)S(1)} %add_convert_fusion.mine_ref), channel_id=1, source_target_pairs={{0,4},{4,0},{8,12},{12,8},{16,20},{20,16},{24,28},{28,24},{1,5},{5... | collective-permute-start | bytes 221192 | tf_op jit(solution)/shard_map/ppermute | solution.py:243
  (3 other events, 1.9 us)

commit v3 on v2

--- a/solution.py
+++ b/solution.py
@@ -1,3 +1,5 @@
+import math
+
 import jax
 import jax.numpy as jnp
 from jax import lax
@@ -7,7 +9,6 @@
 
 VMEM = pl.BlockSpec(memory_space=pltpu.VMEM)
 SMEM = pl.BlockSpec(memory_space=pltpu.SMEM)
-PARAMS = pltpu.CompilerParams(vmem_limit_bytes=32 * 1024 * 1024)
 GELU_C = 0.7978845608028654
 
 
@@ -24,6 +25,22 @@
         return LATIN[plane][rep]
     bits = jnp.int32(LATIN_BITS - (1 << 32) if LATIN_BITS >> 31 else LATIN_BITS)
     return lax.shift_right_logical(bits, 2 * (4 * plane + rep)) & 3
+
+
+def local_call(kernel, name, inputs, in_specs, out_shape, scratch=()):
+    size = sum(
+        math.prod(each.shape) * each.dtype.itemsize
+        for each in (*inputs, *jax.tree.leaves(out_shape), *scratch)
+    )
+    return pl.pallas_call(
+        kernel,
+        out_shape=out_shape,
+        in_specs=in_specs,
+        out_specs=jax.tree.map(lambda each: SMEM if each.dtype == jnp.int32 else VMEM, out_shape),
+        scratch_shapes=[pltpu.VMEM(each.shape, each.dtype) for each in scratch],
+        compiler_params=pltpu.CompilerParams(vmem_limit_bytes=size + 4 * 1024 * 1024),
+        name=name,
+    )(*inputs)
 
 
 def column_of(row, width):
@@ -42,8 +59,26 @@
         out_ref[...] = jnp.where(odd == 0, first, second)
 
 
-def cast_kernel(count_ref, out_ref):
-    out_ref[...] = count_ref[0].reshape(out_ref.shape).astype(jnp.float32).astype(jnp.bfloat16)
+def prepare_kernel(
+    block_count, count_ref, row_ref, col_ref, features_ref, degree_ref,
+    tiles_ref, codes_ref, scaled_ref, inv_ref,
+):
+    tiles_ref[...] = count_ref[0].reshape(tiles_ref.shape).astype(jnp.float32).astype(jnp.bfloat16)
+    sections, slots = codes_ref.shape[1:]
+
+    def code_step(at, carry):
+        section, slot = at // slots, at % slots
+        code = row_ref[0, section, slot] * block_count + col_ref[0, section, slot]
+        codes_ref[0, section, slot] = code
+        return carry
+
+    lax.fori_loop(0, sections * slots, code_step, 0)
+    width = inv_ref.shape[1]
+    inv_root = column_of(lax.rsqrt(degree_ref[...].astype(jnp.float32)), width)
+    inv_ref[...] = inv_root
+    for at in range(0, features_ref.shape[1], width):
+        part = features_ref[:, at : at + width].astype(jnp.float32)
+        scaled_ref[:, at : at + width] = (part * inv_root).astype(jnp.bfloat16)
 
 
 def join_kernel(first_ref, second_ref, out_ref):
@@ -92,10 +127,9 @@
 
 def dense_kernel(rep_size, *refs):
     part_refs, refs = refs[:rep_size], refs[rep_size:]
-    features_ref, degree_ref, weight_ref, bias_ref, cotangent_ref, out_ref, keep_ref, send_ref = refs
-    width = features_ref.shape[1]
-    inv_root = column_of(lax.rsqrt(degree_ref[...].astype(jnp.float32)), width // 2)
-    inv_root = jnp.concatenate([inv_root, inv_root], axis=1)
+    scaled_ref, inv_ref, weight_ref, bias_ref, cotangent_ref, out_ref, keep_ref, send_ref = refs
+    width = scaled_ref.shape[1]
+    inv_root = jnp.concatenate([inv_ref[...]] * 2, axis=1)
     sums = [0.0, 0.0]
     for mask, part_ref in enumerate(part_refs):
         sums[mask % 2] += part_ref[...].astype(jnp.float32)
@@ -103,8 +137,7 @@
     agg = jnp.concatenate(
         [jnp.where(odd == 0, sums[0], sums[1]), jnp.where(odd == 0, sums[1], sums[0])], axis=1
     )
-    scaled = (features_ref[...].astype(jnp.float32) * inv_root).astype(jnp.bfloat16)
-    mixed = ((agg + scaled.astype(jnp.float32)) * inv_root).astype(jnp.bfloat16)
+    mixed = ((agg + scaled_ref[...].astype(jnp.float32)) * inv_root).astype(jnp.bfloat16)
     pre = jnp.dot(mixed, weight_ref[...], preferred_element_type=jnp.float32) + bias_ref[...]
     square = pre * pre
     bent = jnp.tanh(GELU_C * (pre + 0.044715 * (square * pre)))
@@ -173,10 +206,10 @@
     bf16, f32 = jnp.bfloat16, jnp.float32
     half = jax.ShapeDtypeStruct((row_count, width // 2), bf16)
 
-    outgoing = pl.pallas_call(
-        lambda *refs: scale_kernel(sections, *refs),
-        out_shape=(half, half), in_specs=[VMEM, VMEM], out_specs=(VMEM, VMEM), name="scale",
-    )(features, degree_row)
+    outgoing = local_call(
+        lambda *refs: scale_kernel(sections, *refs), "scale",
+        (features, degree_row), [VMEM] * 2, (half, half),
+    )
     arrived = []
     for flip, part in enumerate(outgoing):
         moves = []
@@ -187,67 +220,62 @@
                 moves.append((dom * rep_size + rep, target * rep_size + (plane ^ flip)))
         arrived.append(lax.ppermute(part, ("dom", "rep"), moves))
 
-    tiles = pl.pallas_call(
-        cast_kernel,
-        out_shape=jax.ShapeDtypeStruct((sections * slots, block, block), bf16),
-        in_specs=[VMEM], out_specs=VMEM, compiler_params=PARAMS, name="cast",
-    )(tile_count)
-    codes = tile_row * block_count + tile_col
+    tiles, codes, scaled, inv_root = local_call(
+        lambda *refs: prepare_kernel(block_count, *refs), "prepare",
+        (tile_count, tile_row, tile_col, features, degree_row), [VMEM, SMEM, SMEM, VMEM, VMEM],
+        (
+            jax.ShapeDtypeStruct((sections * slots, block, block), bf16),
+            jax.ShapeDtypeStruct(tile_row.shape, jnp.int32),
+            jax.ShapeDtypeStruct((row_count, width), bf16),
+            jax.ShapeDtypeStruct((row_count, width // 2), f32),
+        ),
+    )
     pair = xor_pairs(rep_size, 1)
     their_codes = lax.ppermute(codes, "rep", pair)
     their_tiles = lax.ppermute(tiles, "rep", pair)
+    arrived, their_codes = lax.optimization_barrier((arrived, their_codes))
 
     pieces = [None] * dom_size
-    pieces[0] = pl.pallas_call(
-        join_kernel,
-        out_shape=jax.ShapeDtypeStruct((2 * row_count, width // 2), bf16),
-        in_specs=[VMEM, VMEM], out_specs=VMEM, name="join",
-    )(*arrived)
+    pieces[0] = local_call(
+        join_kernel, "join", arrived, [VMEM] * 2,
+        jax.ShapeDtypeStruct((2 * row_count, width // 2), bf16),
+    )
     for mask in range(2, dom_size, 2):
         pieces[mask] = lax.ppermute(pieces[0], "dom", xor_pairs(dom_size, mask))
     for mask in range(0, dom_size, 2):
         pieces[mask + 1] = lax.ppermute(pieces[mask], "dom", xor_pairs(dom_size, 1))
 
-    held_shape = (dom_size * 2 * row_count // block, block, width // 2)
-    partials = pl.pallas_call(
-        lambda *refs: aggregate_kernel(dom_size, rep_size, sections, *refs),
-        out_shape=(half,) * rep_size,
-        in_specs=[SMEM, SMEM] + [VMEM] * (2 + dom_size),
-        out_specs=(VMEM,) * rep_size,
-        scratch_shapes=[
-            pltpu.VMEM(held_shape, bf16),
-            pltpu.VMEM((block_count, block, width // 2), f32),
-        ],
-        compiler_params=PARAMS,
-        name="aggregate",
-    )(codes, their_codes, tiles, their_tiles, *pieces)
+    partials = local_call(
+        lambda *refs: aggregate_kernel(dom_size, rep_size, sections, *refs), "aggregate",
+        (codes, their_codes, tiles, their_tiles, *pieces), [SMEM] * 2 + [VMEM] * (2 + dom_size),
+        (half,) * rep_size,
+        (
+            jax.ShapeDtypeStruct((dom_size * 2 * row_count // block, block, width // 2), bf16),
+            jax.ShapeDtypeStruct((block_count, block, width // 2), f32),
+        ),
+    )
 
     parts = [partials[0]]
     for mask in range(1, rep_size):
         parts.append(lax.ppermute(partials[mask], "rep", xor_pairs(rep_size, mask)))
 
     share = jax.ShapeDtypeStruct((width // 2 + 16, width), f32)
-    outcome, keep, send = pl.pallas_call(
-        lambda *refs: dense_kernel(rep_size, *refs),
-        out_shape=(jax.ShapeDtypeStruct((row_count, width), bf16), share, share),
-        in_specs=[VMEM] * (rep_size + 5),
-        out_specs=(VMEM,) * 3,
-        compiler_params=PARAMS,
-        name="dense",
-    )(*parts, features, degree_row, weight, bias.reshape(1, width), cotangent)
+    outcome, keep, send = local_call(
+        lambda *refs: dense_kernel(rep_size, *refs), "dense",
+        (*parts, scaled, inv_root, weight, bias.reshape(1, width), cotangent),
+        [VMEM] * (rep_size + 5),
+        (jax.ShapeDtypeStruct((row_count, width), bf16), share, share),
+    )
 
     swap = xor_pairs(dom_size, 1)
     mine = (keep + lax.ppermute(send, "dom", swap)).astype(bf16)
     mine = exchange_sum(mine, "dom", bits_of(dom_size)[1:])
     mine = exchange_sum(mine, "rep", bits_of(rep_size))
     other = lax.ppermute(mine, "dom", swap)
-    weight_grad, bias_grad = pl.pallas_call(
-        finish_kernel,
-        out_shape=(
-            jax.ShapeDtypeStruct((width, width), f32), jax.ShapeDtypeStruct((1, width), f32),
-        ),
-        in_specs=[VMEM, VMEM], out_specs=(VMEM, VMEM), name="finish",
-    )(mine, other)
+    weight_grad, bias_grad = local_call(
+        finish_kernel, "finish", (mine, other), [VMEM] * 2,
+        (jax.ShapeDtypeStruct((width, width), f32), jax.ShapeDtypeStruct((1, width), f32)),
+    )
     return (outcome, weight_grad, bias_grad.reshape(width))
 
 

time: 63.5 us -> 59.5 us (0.937)
  Pallas kernels: 7.01 us -> 4.18 us
  starting transfers between devices: 27 us -> 24.8 us
  waiting for transfers between devices: 24.4 us -> 26.1 us
    ppermute x3, waiting for transfers between devices: 0.73 us -> 4.69 us  [on_device(): pieces[mask] = lax.ppermute(pieces[0], 'dom', xor_pairs(dom_size, mask))]
    ppermute x2, waiting for transfers between devices: 3.35 us -> 0.01 us  [on_device(): arrived.append(lax.ppermute(part, ('dom', 'rep'), moves))]
    pallas_call x6, Pallas kernels: 7.01 us -> 4.18 us  [local_call(): pl.pallas_call(kernel, out_shape=out_shape, in_specs=in_specs, out_specs=...]
    ppermute x3, starting transfers between devices: 5.08 us -> 3.74 us  [on_device(): pieces[mask] = lax.ppermute(pieces[0], 'dom', xor_pairs(dom_size, mask))]
    ppermute x1, starting transfers between devices: 1.38 us -> 0.07 us  [on_device(): their_codes = lax.ppermute(codes, 'rep', pair)]
    ppermute x1, waiting for transfers between devices: 2.25 us -> 3.56 us  [on_device(): their_codes = lax.ppermute(codes, 'rep', pair)]
    ppermute x2, starting transfers between devices: 3.41 us -> 4.41 us  [exchange_sum(): third = lax.ppermute(value, axis, xor_pairs(size, now[0] ^ now[1]))]
    ppermute x1, starting transfers between devices: 0.07 us -> 1.04 us  [on_device(): their_tiles = lax.ppermute(tiles, 'rep', pair)]
  transfers between devices with their start and end apart: 22 -> 22, of which waited for: 13 -> 14; matrix products, arithmetic and copies ran while one was open for 0% -> 0% of each run, Pallas kernels for 3% -> 2%
where the time goes in v3:
time: 59.5 us; the launch traced here: 59.2 us
  waiting for transfers between devices  26.1 us (44%)
  starting transfers between devices  24.8 us (42%)
  Pallas kernels  4.18 us (7%)
  local copies, waits for them, and re-layouts  3.3 us (6%)
  between operations  0.8 us (1%)
    ppermute x2, starting transfers between devices, on_device(): arrived.append(lax.ppermute(part, ('dom', 'rep'), moves))  7.39 us
    ppermute x3, waiting for transfers between devices, on_device(): parts.append(lax.ppermute(partials[mask], 'rep', xor_pairs(rep_size, mask)))  5.27 us
    ppermute x3, waiting for transfers between devices, on_device(): pieces[mask] = lax.ppermute(pieces[0], 'dom', xor_pairs(dom_size, mask))  4.69 us
    ppermute x3, starting transfers between devices, on_device(): parts.append(lax.ppermute(partials[mask], 'rep', xor_pairs(rep_size, mask)))  4.45 us
    ppermute x2, waiting for transfers between devices, exchange_sum(): second = lax.ppermute(value, axis, xor_pairs(size, now[1]))  4.44 us
    ppermute x2, starting transfers between devices, exchange_sum(): third = lax.ppermute(value, axis, xor_pairs(size, now[0] ^ now[1]))  4.41 us
    pallas_call x6, Pallas kernels, local_call(): pl.pallas_call(kernel, out_shape=out_shape, in_specs=in_specs, out_specs=...  4.18 us
    ppermute x2, waiting for transfers between devices, exchange_sum(): third = lax.ppermute(value, axis, xor_pairs(size, now[0] ^ now[1]))  4.09 us
  transfers between devices with their start and end apart: 22, of which 14 were waited for; matrix products, arithmetic and copies ran while one was open for 0% of the time, Pallas kernels for 2%

profile of v3, /device:TPU:0, one launch (start us, length us, event | category | flops | bytes accessed | tf_op | source)
XLA Modules:
  0.0 59.2 jit_solution(8094472073591926730)
XLA Ops:
  0.6 0.7 %copy-done.5 = s32[256]{0:T(256)S(1)} copy-done((s32[256]{0:T(256)S(1)}, s32[256]{0:T(256)}, u32[]{:S(2)}) %copy-start.5) | copy-done | bytes 1048
  1.3 0.9 %copy-done.1 = bf16[256,256]{1,0:T(8,128)(2,1)S(1)} copy-done((bf16[256,256]{1,0:T(8,128)(2,1)S(1)}, bf16[256,256]{1,0:T(8,128)(2,1)}, u32[]{:S(2)}) %copy-start.1) | copy-done | bytes 131096
  2.4 3.0 %collective-permute-start = (bf16[256,128]{1,0:T(8,128)(2,1)S(1)}, bf16[256,128]{1,0:T(8,128)(2,1)S(1)}, u32[]{:S(2)}, u32[]{:S(2)}) collective-permute-start(bf16[256,128]{1,0:T(8,128)(2,1)S(1)} %get-tuple-element.22), channel_id=1, source_target_pairs={{0,8},{1,0},{2,16},{3,24},{4,12},{5,4},{6,20},{7,28},{8,25},{9,17}... | collective-permute-start | bytes 196616 | tf_op jit(solution)/shard_map/ppermute | solution.py:221
  5.3 4.4 %collective-permute-start.1 = (bf16[256,128]{1,0:T(8,128)(2,1)S(1)}, bf16[256,128]{1,0:T(8,128)(2,1)S(1)}, u32[]{:S(2)}, u32[]{:S(2)}) collective-permute-start(bf16[256,128]{1,0:T(8,128)(2,1)S(1)} %get-tuple-element.23), channel_id=1, source_target_pairs={{0,9},{1,1},{2,17},{3,25},{4,13},{5,5},{6,21},{7,29},{8,24},{9,16}... | collective-permute-start | bytes 196616 | tf_op jit(solution)/shard_map/ppermute | solution.py:221
  9.8 1.0 %copy-done = s32[1,2,4,128,128]{4,3,2,1,0:T(8,128)S(1)} copy-done((s32[1,2,4,128,128]{4,3,2,1,0:T(8,128)S(1)}, s32[1,2,4,128,128]{4,3,2,1,0:T(8,128)}, u32[]{:S(2)}) %copy-start) | copy-done | bytes 524312
  10.8 1.3 %prepare.1 = (bf16[8,128,128]{2,1,0:T(8,128)(2,1)S(1)}, s32[1,2,4]{2,1,0:T(2,128)S(1)}, bf16[256,256]{1,0:T(8,128)(2,1)S(1)}, f32[256,128]{1,0:T(8,128)S(1)}) custom-call(s32[1,2,4,128,128]{4,3,2,1,0:T(8,128)S(1)} %copy-done, s32[1,2,4]{2,1,0:T(2,128)S(1)} %copy-done.6, s32[1,2,4]{2,1,0:T(2,128)S(1)} %copy-done.7, bf16[256,256]{1,0:T(8,128)(2,1)S(1)} %copy-done.2, ...), custom_call_target="tpu_custom_call" | custom-call | tf_op jit(solution)/shard_map/prepare/pallas_call | solution.py:35
  12.2 3.6 %collective-permute-done.2.refs_1_ = s32[1,2,4]{2,1,0:T(2,128)S(1)} collective-permute-done((s32[1,2,4]{2,1,0:T(2,128)S(1)}, s32[1,2,4]{2,1,0:T(2,128)S(1)}, u32[]{:S(2)}, u32[]{:S(2)}) %collective-permute-start.2) | collective-permute-done | bytes 64 | tf_op jit(solution)/shard_map/ppermute | solution.py:234
  15.8 2.6 %collective-permute-start.9 = (bf16[512,128]{1,0:T(8,128)(2,1)S(1)}, bf16[512,128]{1,0:T(8,128)(2,1)S(1)}, u32[]{:S(2)}, u32[]{:S(2)}) collective-permute-start(bf16[512,128]{1,0:T(8,128)(2,1)S(1)} %join.1.refs_4_), channel_id=1, source_target_pairs={{0,24},{4,28},{8,16},{12,20},{16,8},{20,12},{24,0},{28,4},{1,25},{... | collective-permute-start | bytes 393224 | tf_op jit(solution)/shard_map/ppermute | solution.py:244
  18.4 1.0 %collective-permute-start.3 = (bf16[8,128,128]{2,1,0:T(8,128)(2,1)S(1)}, bf16[8,128,128]{2,1,0:T(8,128)(2,1)S(1)}, u32[]{:S(2)}, u32[]{:S(2)}) collective-permute-start(bf16[8,128,128]{2,1,0:T(8,128)(2,1)S(1)} %get-tuple-element.25.refs_2_), channel_id=1, source_target_pairs={{0,1},{1,0},{2,3},{3,2},{4,5},{5,4},{6,7},{7,6},{8,9},{9,8},{10,11... | collective-permute-start | bytes 786440 | tf_op jit(solution)/shard_map/ppermute | solution.py:235
  19.4 0.9 %collective-permute-start.7 = (bf16[512,128]{1,0:T(8,128)(2,1)S(1)}, bf16[512,128]{1,0:T(8,128)(2,1)S(1)}, u32[]{:S(2)}, u32[]{:S(2)}) collective-permute-start(bf16[512,128]{1,0:T(8,128)(2,1)S(1)} %join.1.refs_4_), channel_id=1, source_target_pairs={{0,16},{4,20},{8,24},{12,28},{16,0},{20,4},{24,8},{28,12},{1,17},{... | collective-permute-start | bytes 393224 | tf_op jit(solution)/shard_map/ppermute | solution.py:244
  20.6 1.8 %collective-permute-done.9.refs_10_ = bf16[512,128]{1,0:T(8,128)(2,1)S(1)} collective-permute-done((bf16[512,128]{1,0:T(8,128)(2,1)S(1)}, bf16[512,128]{1,0:T(8,128)(2,1)S(1)}, u32[]{:S(2)}, u32[]{:S(2)}) %collective-permute-start.9) | collective-permute-done | bytes 131104 | tf_op jit(solution)/shard_map/ppermute | solution.py:244
  22.3 2.0 %collective-permute-done.7.refs_8_ = bf16[512,128]{1,0:T(8,128)(2,1)S(1)} collective-permute-done((bf16[512,128]{1,0:T(8,128)(2,1)S(1)}, bf16[512,128]{1,0:T(8,128)(2,1)S(1)}, u32[]{:S(2)}, u32[]{:S(2)}) %collective-permute-start.7) | collective-permute-done | bytes 131104 | tf_op jit(solution)/shard_map/ppermute | solution.py:244
  24.4 0.9 %collective-permute-done.5.refs_6_ = bf16[512,128]{1,0:T(8,128)(2,1)S(1)} collective-permute-done((bf16[512,128]{1,0:T(8,128)(2,1)S(1)}, bf16[512,128]{1,0:T(8,128)(2,1)S(1)}, u32[]{:S(2)}, u32[]{:S(2)}) %collective-permute-start.5) | collective-permute-done | bytes 131104 | tf_op jit(solution)/shard_map/ppermute | solution.py:244
  25.7 0.9 %collective-permute-done.6.refs_7_ = bf16[512,128]{1,0:T(8,128)(2,1)S(1)} collective-permute-done((bf16[512,128]{1,0:T(8,128)(2,1)S(1)}, bf16[512,128]{1,0:T(8,128)(2,1)S(1)}, u32[]{:S(2)}, u32[]{:S(2)}) %collective-permute-start.6) | collective-permute-done | bytes 131104 | tf_op jit(solution)/shard_map/ppermute | solution.py:246
  26.6 1.0 %aggregate.1 = (bf16[256,128]{1,0:T(8,128)(2,1)S(1)}, bf16[256,128]{1,0:T(8,128)(2,1)S(1)}, bf16[256,128]{1,0:T(8,128)(2,1)S(1)}, bf16[256,128]{1,0:T(8,128)(2,1)S(1)}) custom-call(s32[1,2,4]{2,1,0:T(2,128)S(1)} %get-tuple-element.21.refs_0_, s32[1,2,4]{2,1,0:T(2,128)S(1)} %collective-permute-done.2.refs_1_, ...), custom_call_target="tpu_custom_call" | custom-call | tf_op jit(solution)/shard_map/aggregate/pallas_call | solution.py:35
  27.7 1.7 %collective-permute-start.11 = (bf16[256,128]{1,0:T(8,128)(2,1)S(1)}, bf16[256,128]{1,0:T(8,128)(2,1)S(1)}, u32[]{:S(2)}, u32[]{:S(2)}) collective-permute-start(bf16[256,128]{1,0:T(8,128)(2,1)S(1)} %get-tuple-element.29), channel_id=1, source_target_pairs={{0,1},{1,0},{2,3},{3,2},{4,5},{5,4},{6,7},{7,6},{8,9},{9,8},{10,11... | collective-permute-start | bytes 196616 | tf_op jit(solution)/shard_map/ppermute | solution.py:260
  29.4 1.0 %collective-permute-start.12 = (bf16[256,128]{1,0:T(8,128)(2,1)S(1)}, bf16[256,128]{1,0:T(8,128)(2,1)S(1)}, u32[]{:S(2)}, u32[]{:S(2)}) collective-permute-start(bf16[256,128]{1,0:T(8,128)(2,1)S(1)} %get-tuple-element.30), channel_id=1, source_target_pairs={{0,2},{1,3},{2,0},{3,1},{4,6},{5,7},{6,4},{7,5},{8,10},{9,11},{10,... | collective-permute-start | bytes 196616 | tf_op jit(solution)/shard_map/ppermute | solution.py:260
  30.4 1.8 %collective-permute-start.13 = (bf16[256,128]{1,0:T(8,128)(2,1)S(1)}, bf16[256,128]{1,0:T(8,128)(2,1)S(1)}, u32[]{:S(2)}, u32[]{:S(2)}) collective-permute-start(bf16[256,128]{1,0:T(8,128)(2,1)S(1)} %get-tuple-element.31), channel_id=1, source_target_pairs={{0,3},{1,2},{2,1},{3,0},{4,7},{5,6},{6,5},{7,4},{8,11},{9,10},{10,... | collective-permute-start | bytes 196616 | tf_op jit(solution)/shard_map/ppermute | solution.py:260
  32.1 5.3 %collective-permute-done.12.refs_2_ = bf16[256,128]{1,0:T(8,128)(2,1)S(1)} collective-permute-done((bf16[256,128]{1,0:T(8,128)(2,1)S(1)}, bf16[256,128]{1,0:T(8,128)(2,1)S(1)}, u32[]{:S(2)}, u32[]{:S(2)}) %collective-permute-start.12) | collective-permute-done | bytes 65568 | tf_op jit(solution)/shard_map/ppermute | solution.py:260
  38.1 1.0 %dense.1 = (bf16[256,256]{1,0:T(8,128)(2,1)}, f32[144,256]{1,0:T(8,128)S(1)}, f32[144,256]{1,0:T(8,128)S(1)}) custom-call(bf16[256,128]{1,0:T(8,128)(2,1)S(1)} %get-tuple-element.28.refs_0_, bf16[256,128]{1,0:T(8,128)(2,1)S(1)} %collective-permute-done.11.refs_1_, bf16[256,128]{1,0:T(8,128)(2,1)S(1)} %collective-permute-done.12.refs_2_, ...), custom_call_target="tpu_custom_call" | custom-call | tf_op jit(solution)/shard_map/dense/pallas_call | solution.py:35
  39.1 1.4 %collective-permute-done.14 = f32[144,256]{1,0:T(8,128)S(1)} collective-permute-done((f32[144,256]{1,0:T(8,128)S(1)}, f32[144,256]{1,0:T(8,128)S(1)}, u32[]{:S(2)}, u32[]{:S(2)}) %collective-permute-start.14) | collective-permute-done | bytes 147488 | tf_op jit(solution)/shard_map/ppermute | solution.py:271
  40.5 2.1 %collective-permute-start.17 = (bf16[144,256]{1,0:T(8,128)(2,1)S(1)}, bf16[144,256]{1,0:T(8,128)(2,1)S(1)}, u32[]{:S(2)}, u32[]{:S(2)}) collective-permute-start(bf16[144,256]{1,0:T(8,128)(2,1)S(1)} %add_convert_fusion.2), channel_id=1, source_target_pairs={{0,24},{4,28},{8,16},{12,20},{16,8},{20,12},{24,0},{28,4},{1,25},{... | collective-permute-start | bytes 221192 | tf_op jit(solution)/shard_map/ppermute | solution.py:188
  43.1 0.9 %collective-permute-start.15 = (bf16[144,256]{1,0:T(8,128)(2,1)S(1)}, bf16[144,256]{1,0:T(8,128)(2,1)S(1)}, u32[]{:S(2)}, u32[]{:S(2)}) collective-permute-start(bf16[144,256]{1,0:T(8,128)(2,1)S(1)} %add_convert_fusion.2), channel_id=1, source_target_pairs={{0,8},{4,12},{8,0},{12,4},{16,24},{20,28},{24,16},{28,20},{1,9},{5... | collective-permute-start | bytes 221192 | tf_op jit(solution)/shard_map/ppermute | solution.py:183
  44.0 1.8 %collective-permute-done.17 = bf16[144,256]{1,0:T(8,128)(2,1)S(1)} collective-permute-done((bf16[144,256]{1,0:T(8,128)(2,1)S(1)}, bf16[144,256]{1,0:T(8,128)(2,1)S(1)}, u32[]{:S(2)}, u32[]{:S(2)}) %collective-permute-start.17) | collective-permute-done | bytes 73760 | tf_op jit(solution)/shard_map/ppermute | solution.py:188
  45.9 1.5 %collective-permute-done.16 = bf16[144,256]{1,0:T(8,128)(2,1)S(1)} collective-permute-done((bf16[144,256]{1,0:T(8,128)(2,1)S(1)}, bf16[144,256]{1,0:T(8,128)(2,1)S(1)}, u32[]{:S(2)}, u32[]{:S(2)}) %collective-permute-start.16) | collective-permute-done | bytes 73760 | tf_op jit(solution)/shard_map/ppermute | solution.py:187
  47.5 2.3 %collective-permute-start.20 = (bf16[144,256]{1,0:T(8,128)(2,1)S(1)}, bf16[144,256]{1,0:T(8,128)(2,1)S(1)}, u32[]{:S(2)}, u32[]{:S(2)}) collective-permute-start(bf16[144,256]{1,0:T(8,128)(2,1)S(1)} %add_convert_fusion.1), channel_id=1, source_target_pairs={{0,3},{1,2},{2,1},{3,0},{4,7},{5,6},{6,5},{7,4},{8,11},{9,10},{10,... | collective-permute-start | bytes 221192 | tf_op jit(solution)/shard_map/ppermute | solution.py:188
  49.8 0.8 %collective-permute-start.19 = (bf16[144,256]{1,0:T(8,128)(2,1)S(1)}, bf16[144,256]{1,0:T(8,128)(2,1)S(1)}, u32[]{:S(2)}, u32[]{:S(2)}) collective-permute-start(bf16[144,256]{1,0:T(8,128)(2,1)S(1)} %add_convert_fusion.1), channel_id=1, source_target_pairs={{0,2},{1,3},{2,0},{3,1},{4,6},{5,7},{6,4},{7,5},{8,10},{9,11},{10,... | collective-permute-start | bytes 221192 | tf_op jit(solution)/shard_map/ppermute | solution.py:187
  50.6 1.3 %collective-permute-start.18 = (bf16[144,256]{1,0:T(8,128)(2,1)S(1)}, bf16[144,256]{1,0:T(8,128)(2,1)S(1)}, u32[]{:S(2)}, u32[]{:S(2)}) collective-permute-start(bf16[144,256]{1,0:T(8,128)(2,1)S(1)} %add_convert_fusion.1), channel_id=1, source_target_pairs={{0,1},{1,0},{2,3},{3,2},{4,5},{5,4},{6,7},{7,6},{8,9},{9,8},{10,11... | collective-permute-start | bytes 221192 | tf_op jit(solution)/shard_map/ppermute | solution.py:183
  51.9 2.3 %collective-permute-done.20 = bf16[144,256]{1,0:T(8,128)(2,1)S(1)} collective-permute-done((bf16[144,256]{1,0:T(8,128)(2,1)S(1)}, bf16[144,256]{1,0:T(8,128)(2,1)S(1)}, u32[]{:S(2)}, u32[]{:S(2)}) %collective-permute-start.20) | collective-permute-done | bytes 73760 | tf_op jit(solution)/shard_map/ppermute | solution.py:188
  54.2 2.9 %collective-permute-done.19 = bf16[144,256]{1,0:T(8,128)(2,1)S(1)} collective-permute-done((bf16[144,256]{1,0:T(8,128)(2,1)S(1)}, bf16[144,256]{1,0:T(8,128)(2,1)S(1)}, u32[]{:S(2)}, u32[]{:S(2)}) %collective-permute-start.19) | collective-permute-done | bytes 73760 | tf_op jit(solution)/shard_map/ppermute | solution.py:187
  57.2 1.3 %collective-permute-done.21.other_ref = bf16[144,256]{1,0:T(8,128)(2,1)S(1)} collective-permute-done((bf16[144,256]{1,0:T(8,128)(2,1)S(1)}, bf16[144,256]{1,0:T(8,128)(2,1)S(1)}, u32[]{:S(2)}, u32[]{:S(2)}) %collective-permute-start.21) | collective-permute-done | bytes 73760 | tf_op jit(solution)/shard_map/ppermute | solution.py:274
  58.5 0.7 %finish.1 = (f32[256,256]{1,0:T(8,128)}, f32[1,256]{1,0:T(1,128)}) custom-call(bf16[144,256]{1,0:T(8,128)(2,1)S(1)} %add_convert_fusion.mine_ref, bf16[144,256]{1,0:T(8,128)(2,1)S(1)} %collective-permute-done.21.other_ref), custom_call_target="tpu_custom_call" | custom-call | tf_op jit(solution)/shard_map/finish/pallas_call | solution.py:35
  (39 shorter events, 2.3 us)
Async XLA Ops:
  0.6 0.7 %copy-start.5 = (s32[256]{0:T(256)S(1)}, s32[256]{0:T(256)}, u32[]{:S(2)}) copy-start(s32[256]{0:T(256)} %param.10) | copy-start | bytes 3076
  1.3 0.9 %copy-start.1 = (bf16[256,256]{1,0:T(8,128)(2,1)S(1)}, bf16[256,256]{1,0:T(8,128)(2,1)}, u32[]{:S(2)}) copy-start(bf16[256,256]{1,0:T(8,128)(2,1)} %refs_0_.3) | copy-start | bytes 393220
  2.2 7.5 %copy-start.2 = (bf16[256,256]{1,0:T(8,128)(2,1)S(1)}, bf16[256,256]{1,0:T(8,128)(2,1)}, u32[]{:S(2)}) copy-start(bf16[256,256]{1,0:T(8,128)(2,1)} %refs_0_.3) | copy-start | bytes 393220
  2.3 7.4 %copy-start.7 = (s32[1,2,4]{2,1,0:T(2,128)S(1)}, s32[1,2,4]{2,1,0:T(2,128)}, u32[]{:S(2)}) copy-start(s32[1,2,4]{2,1,0:T(2,128)} %refs_2_.1) | copy-start | bytes 100
  2.3 7.4 %copy-start.6 = (s32[1,2,4]{2,1,0:T(2,128)S(1)}, s32[1,2,4]{2,1,0:T(2,128)}, u32[]{:S(2)}) copy-start(s32[1,2,4]{2,1,0:T(2,128)} %refs_1_.1) | copy-start | bytes 100
  2.4 13.4 %collective-permute-start = (bf16[256,128]{1,0:T(8,128)(2,1)S(1)}, bf16[256,128]{1,0:T(8,128)(2,1)S(1)}, u32[]{:S(2)}, u32[]{:S(2)}) collective-permute-start(bf16[256,128]{1,0:T(8,128)(2,1)S(1)} %get-tuple-element.22), channel_id=1, source_target_pairs={{0,8},{1,0},{2,16},{3,24},{4,12},{5,4},{6,20},{7,28},{8,25},{9,17}... | collective-permute-start | bytes 196616 | tf_op jit(solution)/shard_map/ppermute | solution.py:221
  5.3 10.4 %collective-permute-start.1 = (bf16[256,128]{1,0:T(8,128)(2,1)S(1)}, bf16[256,128]{1,0:T(8,128)(2,1)S(1)}, u32[]{:S(2)}, u32[]{:S(2)}) collective-permute-start(bf16[256,128]{1,0:T(8,128)(2,1)S(1)} %get-tuple-element.23), channel_id=1, source_target_pairs={{0,9},{1,1},{2,17},{3,25},{4,13},{5,5},{6,21},{7,29},{8,24},{9,16}... | collective-permute-start | bytes 196616 | tf_op jit(solution)/shard_map/ppermute | solution.py:221
  9.8 1.0 %copy-start = (s32[1,2,4,128,128]{4,3,2,1,0:T(8,128)S(1)}, s32[1,2,4,128,128]{4,3,2,1,0:T(8,128)}, u32[]{:S(2)}) copy-start(s32[1,2,4,128,128]{4,3,2,1,0:T(8,128)} %refs_0_.2) | copy-start | bytes 1572868
  12.1 3.6 %collective-permute-start.2 = (s32[1,2,4]{2,1,0:T(2,128)S(1)}, s32[1,2,4]{2,1,0:T(2,128)S(1)}, u32[]{:S(2)}, u32[]{:S(2)}) collective-permute-start(s32[1,2,4]{2,1,0:T(2,128)S(1)} %get-tuple-element.21.refs_0_), channel_id=1, source_target_pairs={{0,1},{1,0},{2,3},{3,2},{4,5},{5,4},{6,7},{7,6},{8,9},{9,8},{10,11... | collective-permute-start | bytes 104 | tf_op jit(solution)/shard_map/ppermute | solution.py:234
  15.8 6.6 %collective-permute-start.9 = (bf16[512,128]{1,0:T(8,128)(2,1)S(1)}, bf16[512,128]{1,0:T(8,128)(2,1)S(1)}, u32[]{:S(2)}, u32[]{:S(2)}) collective-permute-start(bf16[512,128]{1,0:T(8,128)(2,1)S(1)} %join.1.refs_4_), channel_id=1, source_target_pairs={{0,24},{4,28},{8,16},{12,20},{16,8},{20,12},{24,0},{28,4},{1,25},{... | collective-permute-start | bytes 393224 | tf_op jit(solution)/shard_map/ppermute | solution.py:244
  18.4 19.0 %copy-start.3 = (bf16[256,256]{1,0:T(8,128)(2,1)S(1)}, bf16[256,256]{1,0:T(8,128)(2,1)}, u32[]{:S(2)}) copy-start(bf16[256,256]{1,0:T(8,128)(2,1)} %refs_6_.1) | copy-start | bytes 393220
  18.4 19.0 %copy-start.4 = (bf16[256,256]{1,0:T(8,128)(2,1)S(1)}, bf16[256,256]{1,0:T(8,128)(2,1)}, u32[]{:S(2)}) copy-start(bf16[256,256]{1,0:T(8,128)(2,1)} %refs_8_.1) | copy-start | bytes 393220
  18.4 6.9 %collective-permute-start.3 = (bf16[8,128,128]{2,1,0:T(8,128)(2,1)S(1)}, bf16[8,128,128]{2,1,0:T(8,128)(2,1)S(1)}, u32[]{:S(2)}, u32[]{:S(2)}) collective-permute-start(bf16[8,128,128]{2,1,0:T(8,128)(2,1)S(1)} %get-tuple-element.25.refs_2_), channel_id=1, source_target_pairs={{0,1},{1,0},{2,3},{3,2},{4,5},{5,4},{6,7},{7,6},{8,9},{9,8},{10,11... | collective-permute-start | bytes 786440 | tf_op jit(solution)/shard_map/ppermute | solution.py:235
  19.4 5.0 %collective-permute-start.7 = (bf16[512,128]{1,0:T(8,128)(2,1)S(1)}, bf16[512,128]{1,0:T(8,128)(2,1)S(1)}, u32[]{:S(2)}, u32[]{:S(2)}) collective-permute-start(bf16[512,128]{1,0:T(8,128)(2,1)S(1)} %join.1.refs_4_), channel_id=1, source_target_pairs={{0,16},{4,20},{8,24},{12,28},{16,0},{20,4},{24,8},{28,12},{1,17},{... | collective-permute-start | bytes 393224 | tf_op jit(solution)/shard_map/ppermute | solution.py:244
  20.3 5.0 %collective-permute-start.5 = (bf16[512,128]{1,0:T(8,128)(2,1)S(1)}, bf16[512,128]{1,0:T(8,128)(2,1)S(1)}, u32[]{:S(2)}, u32[]{:S(2)}) collective-permute-start(bf16[512,128]{1,0:T(8,128)(2,1)S(1)} %join.1.refs_4_), channel_id=1, source_target_pairs={{0,8},{4,12},{8,0},{12,4},{16,24},{20,28},{24,16},{28,20},{1,9},{5... | collective-permute-start | bytes 393224 | tf_op jit(solution)/shard_map/ppermute | solution.py:244
  20.6 4.7 %collective-permute-start.4 = (bf16[512,128]{1,0:T(8,128)(2,1)S(1)}, bf16[512,128]{1,0:T(8,128)(2,1)S(1)}, u32[]{:S(2)}, u32[]{:S(2)}) collective-permute-start(bf16[512,128]{1,0:T(8,128)(2,1)S(1)} %join.1.refs_4_), channel_id=1, source_target_pairs={{0,4},{4,0},{8,12},{12,8},{16,20},{20,16},{24,28},{28,24},{1,5},{5... | collective-permute-start | bytes 393224 | tf_op jit(solution)/shard_map/ppermute | solution.py:246
  22.3 2.9 %collective-permute-start.10 = (bf16[512,128]{1,0:T(8,128)(2,1)S(1)}, bf16[512,128]{1,0:T(8,128)(2,1)S(1)}, u32[]{:S(2)}, u32[]{:S(2)}) collective-permute-start(bf16[512,128]{1,0:T(8,128)(2,1)S(1)} %collective-permute-done.9.refs_10_), channel_id=1, source_target_pairs={{0,4},{4,0},{8,12},{12,8},{16,20},{20,16},{24,28},{28,24},{1,5},{5... | collective-permute-start | bytes 393224 | tf_op jit(solution)/shard_map/ppermute | solution.py:246
  24.4 1.3 %collective-permute-start.8 = (bf16[512,128]{1,0:T(8,128)(2,1)S(1)}, bf16[512,128]{1,0:T(8,128)(2,1)S(1)}, u32[]{:S(2)}, u32[]{:S(2)}) collective-permute-start(bf16[512,128]{1,0:T(8,128)(2,1)S(1)} %collective-permute-done.7.refs_8_), channel_id=1, source_target_pairs={{0,4},{4,0},{8,12},{12,8},{16,20},{20,16},{24,28},{28,24},{1,5},{5... | collective-permute-start | bytes 393224 | tf_op jit(solution)/shard_map/ppermute | solution.py:246
  25.3 1.3 %collective-permute-start.6 = (bf16[512,128]{1,0:T(8,128)(2,1)S(1)}, bf16[512,128]{1,0:T(8,128)(2,1)S(1)}, u32[]{:S(2)}, u32[]{:S(2)}) collective-permute-start(bf16[512,128]{1,0:T(8,128)(2,1)S(1)} %collective-permute-done.5.refs_6_), channel_id=1, source_target_pairs={{0,4},{4,0},{8,12},{12,8},{16,20},{20,16},{24,28},{28,24},{1,5},{5... | collective-permute-start | bytes 393224 | tf_op jit(solution)/shard_map/ppermute | solution.py:246
  27.7 4.5 %collective-permute-start.11 = (bf16[256,128]{1,0:T(8,128)(2,1)S(1)}, bf16[256,128]{1,0:T(8,128)(2,1)S(1)}, u32[]{:S(2)}, u32[]{:S(2)}) collective-permute-start(bf16[256,128]{1,0:T(8,128)(2,1)S(1)} %get-tuple-element.29), channel_id=1, source_target_pairs={{0,1},{1,0},{2,3},{3,2},{4,5},{5,4},{6,7},{7,6},{8,9},{9,8},{10,11... | collective-permute-start | bytes 196616 | tf_op jit(solution)/shard_map/ppermute | solution.py:260
  29.4 8.0 %collective-permute-start.12 = (bf16[256,128]{1,0:T(8,128)(2,1)S(1)}, bf16[256,128]{1,0:T(8,128)(2,1)S(1)}, u32[]{:S(2)}, u32[]{:S(2)}) collective-permute-start(bf16[256,128]{1,0:T(8,128)(2,1)S(1)} %get-tuple-element.30), channel_id=1, source_target_pairs={{0,2},{1,3},{2,0},{3,1},{4,6},{5,7},{6,4},{7,5},{8,10},{9,11},{10,... | collective-permute-start | bytes 196616 | tf_op jit(solution)/shard_map/ppermute | solution.py:260
  30.4 7.0 %collective-permute-start.13 = (bf16[256,128]{1,0:T(8,128)(2,1)S(1)}, bf16[256,128]{1,0:T(8,128)(2,1)S(1)}, u32[]{:S(2)}, u32[]{:S(2)}) collective-permute-start(bf16[256,128]{1,0:T(8,128)(2,1)S(1)} %get-tuple-element.31), channel_id=1, source_target_pairs={{0,3},{1,2},{2,1},{3,0},{4,7},{5,6},{6,5},{7,4},{8,11},{9,10},{10,... | collective-permute-start | bytes 196616 | tf_op jit(solution)/shard_map/ppermute | solution.py:260
  37.4 0.7 %copy-start.8 = (f32[256]{0:T(256)S(1)}, f32[256]{0:T(256)}, u32[]{:S(2)}) copy-start(f32[256]{0:T(256)} %param.15) | copy-start | bytes 3076
  39.1 1.4 %collective-permute-start.14 = (f32[144,256]{1,0:T(8,128)S(1)}, f32[144,256]{1,0:T(8,128)S(1)}, u32[]{:S(2)}, u32[]{:S(2)}) collective-permute-start(f32[144,256]{1,0:T(8,128)S(1)} %get-tuple-element.36), channel_id=1, source_target_pairs={{0,4},{4,0},{8,12},{12,8},{16,20},{20,16},{24,28},{28,24},{1,5},{5... | collective-permute-start | bytes 442376 | tf_op jit(solution)/shard_map/ppermute | solution.py:271
  40.5 5.4 %collective-permute-start.17 = (bf16[144,256]{1,0:T(8,128)(2,1)S(1)}, bf16[144,256]{1,0:T(8,128)(2,1)S(1)}, u32[]{:S(2)}, u32[]{:S(2)}) collective-permute-start(bf16[144,256]{1,0:T(8,128)(2,1)S(1)} %add_convert_fusion.2), channel_id=1, source_target_pairs={{0,24},{4,28},{8,16},{12,20},{16,8},{20,12},{24,0},{28,4},{1,25},{... | collective-permute-start | bytes 221192 | tf_op jit(solution)/shard_map/ppermute | solution.py:188
  42.6 4.8 %collective-permute-start.16 = (bf16[144,256]{1,0:T(8,128)(2,1)S(1)}, bf16[144,256]{1,0:T(8,128)(2,1)S(1)}, u32[]{:S(2)}, u32[]{:S(2)}) collective-permute-start(bf16[144,256]{1,0:T(8,128)(2,1)S(1)} %add_convert_fusion.2), channel_id=1, source_target_pairs={{0,16},{4,20},{8,24},{12,28},{16,0},{20,4},{24,8},{28,12},{1,17},{... | collective-permute-start | bytes 221192 | tf_op jit(solution)/shard_map/ppermute | solution.py:187
  43.1 4.4 %collective-permute-start.15 = (bf16[144,256]{1,0:T(8,128)(2,1)S(1)}, bf16[144,256]{1,0:T(8,128)(2,1)S(1)}, u32[]{:S(2)}, u32[]{:S(2)}) collective-permute-start(bf16[144,256]{1,0:T(8,128)(2,1)S(1)} %add_convert_fusion.2), channel_id=1, source_target_pairs={{0,8},{4,12},{8,0},{12,4},{16,24},{20,28},{24,16},{28,20},{1,9},{5... | collective-permute-start | bytes 221192 | tf_op jit(solution)/shard_map/ppermute | solution.py:183
  47.5 6.7 %collective-permute-start.20 = (bf16[144,256]{1,0:T(8,128)(2,1)S(1)}, bf16[144,256]{1,0:T(8,128)(2,1)S(1)}, u32[]{:S(2)}, u32[]{:S(2)}) collective-permute-start(bf16[144,256]{1,0:T(8,128)(2,1)S(1)} %add_convert_fusion.1), channel_id=1, source_target_pairs={{0,3},{1,2},{2,1},{3,0},{4,7},{5,6},{6,5},{7,4},{8,11},{9,10},{10,... | collective-permute-start | bytes 221192 | tf_op jit(solution)/shard_map/ppermute | solution.py:188
  49.8 7.4 %collective-permute-start.19 = (bf16[144,256]{1,0:T(8,128)(2,1)S(1)}, bf16[144,256]{1,0:T(8,128)(2,1)S(1)}, u32[]{:S(2)}, u32[]{:S(2)}) collective-permute-start(bf16[144,256]{1,0:T(8,128)(2,1)S(1)} %add_convert_fusion.1), channel_id=1, source_target_pairs={{0,2},{1,3},{2,0},{3,1},{4,6},{5,7},{6,4},{7,5},{8,10},{9,11},{10,... | collective-permute-start | bytes 221192 | tf_op jit(solution)/shard_map/ppermute | solution.py:187
  50.6 6.5 %collective-permute-start.18 = (bf16[144,256]{1,0:T(8,128)(2,1)S(1)}, bf16[144,256]{1,0:T(8,128)(2,1)S(1)}, u32[]{:S(2)}, u32[]{:S(2)}) collective-permute-start(bf16[144,256]{1,0:T(8,128)(2,1)S(1)} %add_convert_fusion.1), channel_id=1, source_target_pairs={{0,1},{1,0},{2,3},{3,2},{4,5},{5,4},{6,7},{7,6},{8,9},{9,8},{10,11... | collective-permute-start | bytes 221192 | tf_op jit(solution)/shard_map/ppermute | solution.py:183
  57.2 1.3 %collective-permute-start.21 = (bf16[144,256]{1,0:T(8,128)(2,1)S(1)}, bf16[144,256]{1,0:T(8,128)(2,1)S(1)}, u32[]{:S(2)}, u32[]{:S(2)}) collective-permute-start(bf16[144,256]{1,0:T(8,128)(2,1)S(1)} %add_convert_fusion.mine_ref), channel_id=1, source_target_pairs={{0,4},{4,0},{8,12},{12,8},{16,20},{20,16},{24,28},{28,24},{1,5},{5... | collective-permute-start | bytes 221192 | tf_op jit(solution)/shard_map/ppermute | solution.py:274

commit v4 on v3

--- a/solution.py
+++ b/solution.py
@@ -9,25 +9,27 @@
 
 VMEM = pl.BlockSpec(memory_space=pltpu.VMEM)
 SMEM = pl.BlockSpec(memory_space=pltpu.SMEM)
+HBM = pl.BlockSpec(memory_space=pltpu.MemorySpace.HBM)
+CODE_ROWS = 16
 GELU_C = 0.7978845608028654
 
 
-LATIN = ((1, 0, 2, 3), (3, 2, 0, 1), (0, 1, 3, 2), (2, 3, 1, 0))
-LATIN_BITS = sum(
-    to << (2 * (4 * plane + rep)) for plane, row in enumerate(LATIN) for rep, to in enumerate(row)
+ASIDE = ((3, 1, 2, 0), (1, 3, 2, 0), (0, 1, 3, 2), (0, 2, 1, 3))
+ASIDE_BITS = sum(
+    to << (2 * (4 * plane + rep)) for plane, row in enumerate(ASIDE) for rep, to in enumerate(row)
 )
 
 
-def chip_of(plane, rep, rep_size):
+def chip_of(source, plane, rep, rep_size):
     if rep_size != 4:
-        return plane ^ rep
+        return source ^ rep
     if isinstance(plane, int):
-        return LATIN[plane][rep]
-    bits = jnp.int32(LATIN_BITS - (1 << 32) if LATIN_BITS >> 31 else LATIN_BITS)
-    return lax.shift_right_logical(bits, 2 * (4 * plane + rep)) & 3
-
-
-def local_call(kernel, name, inputs, in_specs, out_shape, scratch=()):
+        return source ^ ASIDE[plane][rep]
+    bits = jnp.int32(ASIDE_BITS - (1 << 32) if ASIDE_BITS >> 31 else ASIDE_BITS)
+    return source ^ (lax.shift_right_logical(bits, 2 * (4 * plane + rep)) & 3)
+
+
+def local_call(kernel, name, inputs, in_specs, out_shape, scratch=(), small=(), spare=4):
     size = sum(
         math.prod(each.shape) * each.dtype.itemsize
         for each in (*inputs, *jax.tree.leaves(out_shape), *scratch)
@@ -36,9 +38,9 @@
         kernel,
         out_shape=out_shape,
         in_specs=in_specs,
-        out_specs=jax.tree.map(lambda each: SMEM if each.dtype == jnp.int32 else VMEM, out_shape),
-        scratch_shapes=[pltpu.VMEM(each.shape, each.dtype) for each in scratch],
-        compiler_params=pltpu.CompilerParams(vmem_limit_bytes=size + 4 * 1024 * 1024),
+        out_specs=jax.tree.map(lambda each: VMEM, out_shape),
+        scratch_shapes=[pltpu.VMEM(each.shape, each.dtype) for each in scratch] + list(small),
+        compiler_params=pltpu.CompilerParams(vmem_limit_bytes=size + spare * 1024 * 1024),
         name=name,
     )(*inputs)
 
@@ -47,9 +49,18 @@
     return jnp.transpose(jnp.broadcast_to(row, (width, row.shape[1])))
 
 
-def scale_kernel(sections, features_ref, degree_ref, *out_refs):
+def scale_kernel(sections, features_hbm, degree_hbm, *refs):
+    out_refs, (features_ref, degree_ref, sems) = refs[:2], refs[2:]
+    copies = [
+        pltpu.make_async_copy(degree_hbm, degree_ref, sems.at[0]),
+        pltpu.make_async_copy(features_hbm, features_ref, sems.at[1]),
+    ]
+    for copy in copies:
+        copy.start()
+    copies[0].wait()
     width = features_ref.shape[1] // 2
     inv_root = column_of(lax.rsqrt(degree_ref[...].astype(jnp.float32)), width)
+    copies[1].wait()
     halves = []
     for half in range(2):
         part = features_ref[:, half * width : (half + 1) * width].astype(jnp.float32)
@@ -60,25 +71,29 @@
 
 
 def prepare_kernel(
-    block_count, count_ref, row_ref, col_ref, features_ref, degree_ref,
-    tiles_ref, codes_ref, scaled_ref, inv_ref,
+    block_count, count_ref, row_ref, col_ref, features_ref, degree_ref, bias_ref,
+    tiles_ref, scaled_ref, inv_ref, bias_out_ref,
 ):
-    tiles_ref[...] = count_ref[0].reshape(tiles_ref.shape).astype(jnp.float32).astype(jnp.bfloat16)
-    sections, slots = codes_ref.shape[1:]
-
-    def code_step(at, carry):
+    _, sections, slots, block, _ = count_ref.shape
+    for at in range(sections * slots):
+        tile = count_ref[0, at // slots, at % slots].astype(jnp.float32)
+        tiles_ref[at * block : (at + 1) * block, :] = tile.astype(jnp.bfloat16)
+    lane = lax.broadcasted_iota(jnp.int32, (CODE_ROWS, block), 1)
+
+    def code_step(at, codes):
         section, slot = at // slots, at % slots
         code = row_ref[0, section, slot] * block_count + col_ref[0, section, slot]
-        codes_ref[0, section, slot] = code
-        return carry
-
-    lax.fori_loop(0, sections * slots, code_step, 0)
+        return jnp.where(lane == at, code, codes)
+
+    codes = lax.fori_loop(0, sections * slots, code_step, jnp.zeros_like(lane))
+    tiles_ref[sections * slots * block :, :] = codes.astype(jnp.float32).astype(jnp.bfloat16)
     width = inv_ref.shape[1]
     inv_root = column_of(lax.rsqrt(degree_ref[...].astype(jnp.float32)), width)
     inv_ref[...] = inv_root
     for at in range(0, features_ref.shape[1], width):
         part = features_ref[:, at : at + width].astype(jnp.float32)
         scaled_ref[:, at : at + width] = (part * inv_root).astype(jnp.bfloat16)
+    bias_out_ref[...] = bias_ref[...]
 
 
 def join_kernel(first_ref, second_ref, out_ref):
@@ -87,37 +102,51 @@
     out_ref[rows:, :] = second_ref[...]
 
 
-def aggregate_kernel(dom_size, rep_size, sections, *refs):
-    code_refs, tile_refs, refs = refs[:2], refs[2:4], refs[4:]
-    piece_refs, refs = refs[:dom_size], refs[dom_size:]
+def aggregate_kernel(dom_size, rep_size, sections, slots, *refs):
+    row_ref, col_ref, *tile_refs = refs[:4]
+    piece_refs, refs = refs[4 : 4 + dom_size], refs[4 + dom_size :]
     out_refs, (held, acc) = refs[:rep_size], refs[rep_size:]
-    slots, block = tile_refs[0].shape[0] // sections, tile_refs[0].shape[1]
+    block = tile_refs[0].shape[1]
+    tile_rows = sections * slots * block
     block_count = acc.shape[0]
     per_piece = piece_refs[0].shape[0] // block
     per_slice = per_piece // 2
+    code_rows = tile_refs[1][tile_rows:, :].astype(jnp.float32)
+    lane = lax.broadcasted_iota(jnp.int32, code_rows.shape, 1)
+    dom, rep = lax.axis_index("dom"), lax.axis_index("rep")
+
+    def code_of(at):
+        return jnp.max(jnp.where(lane == at, code_rows, 0.0)).astype(jnp.int32)
+
+    def add_slot(which, at, row, col):
+        chip = chip_of(rep ^ which, rep, col // per_slice, rep_size)
+        mask = (chip * sections + at // slots) ^ dom
+        rows = held[mask * per_piece + which * per_slice + col % per_slice]
+        tile = tile_refs[which][pl.ds(at * block, block), :]
+        acc[row] += jnp.dot(tile, rows, preferred_element_type=jnp.float32)
+
+    def own_step(at, carry):
+        section, slot = at // slots, at % slots
+        add_slot(0, at, row_ref[0, section, slot], col_ref[0, section, slot])
+        return carry
+
+    def their_step(at, carry):
+        code = code_of(at)
+        add_slot(1, at, code // block_count, code % block_count)
+        return carry
+
+    few = sections * slots <= 8
+    codes = [code_of(at) for at in range(sections * slots)] if few else None
     for mask, piece_ref in enumerate(piece_refs):
         for at in range(per_piece):
             held[mask * per_piece + at] = piece_ref[at * block : (at + 1) * block, :]
     acc[...] = jnp.zeros_like(acc)
-    dom, rep = lax.axis_index("dom"), lax.axis_index("rep")
-
-    for which in range(2):
-        code_ref, tile_ref = code_refs[which], tile_refs[which]
-
-        def slot_step(at):
-            section, slot = at // slots, at % slots
-            code = code_ref[0, section, slot]
-            row, col = code // block_count, code % block_count
-            chip = chip_of(rep ^ which, col // per_slice, rep_size)
-            mask = (chip * sections + section) ^ dom
-            rows = held[mask * per_piece + which * per_slice + col % per_slice]
-            acc[row] += jnp.dot(tile_ref[at], rows, preferred_element_type=jnp.float32)
-
-        if sections * slots <= 8:
-            for at in range(sections * slots):
-                slot_step(at)
-        else:
-            lax.fori_loop(0, sections * slots, lambda at, c: (slot_step(at), c)[1], 0)
+    lax.fori_loop(0, sections * slots, own_step, 0, unroll=few)
+    if few:
+        for at, code in enumerate(codes):
+            add_slot(1, at, code // block_count, code % block_count)
+    else:
+        lax.fori_loop(0, sections * slots, their_step, 0)
 
     for mask, out_ref in enumerate(out_refs):
         for at in range(per_slice):
@@ -208,7 +237,8 @@
 
     outgoing = local_call(
         lambda *refs: scale_kernel(sections, *refs), "scale",
-        (features, degree_row), [VMEM] * 2, (half, half),
+        (features, degree_row), [HBM] * 2, (half, half), (features, degree_row),
+        [pltpu.SemaphoreType.DMA((2,))], 58,
     )
     arrived = []
     for flip, part in enumerate(outgoing):
@@ -216,24 +246,22 @@
         for dom in range(dom_size):
             plane = dom // sections
             for rep in range(rep_size):
-                target = chip_of(plane, rep, rep_size) * sections + dom % sections
+                target = chip_of(plane, plane ^ flip, rep, rep_size) * sections + dom % sections
                 moves.append((dom * rep_size + rep, target * rep_size + (plane ^ flip)))
         arrived.append(lax.ppermute(part, ("dom", "rep"), moves))
 
-    tiles, codes, scaled, inv_root = local_call(
+    tiles, scaled, inv_root, bias_row = local_call(
         lambda *refs: prepare_kernel(block_count, *refs), "prepare",
-        (tile_count, tile_row, tile_col, features, degree_row), [VMEM, SMEM, SMEM, VMEM, VMEM],
+        (tile_count, tile_row, tile_col, features, degree_row, bias.reshape(1, width)),
+        [VMEM, SMEM, SMEM, VMEM, VMEM, VMEM],
         (
-            jax.ShapeDtypeStruct((sections * slots, block, block), bf16),
-            jax.ShapeDtypeStruct(tile_row.shape, jnp.int32),
+            jax.ShapeDtypeStruct((sections * slots * block + CODE_ROWS, block), bf16),
             jax.ShapeDtypeStruct((row_count, width), bf16),
             jax.ShapeDtypeStruct((row_count, width // 2), f32),
+            jax.ShapeDtypeStruct((1, width), f32),
         ),
     )
-    pair = xor_pairs(rep_size, 1)
-    their_codes = lax.ppermute(codes, "rep", pair)
-    their_tiles = lax.ppermute(tiles, "rep", pair)
-    arrived, their_codes = lax.optimization_barrier((arrived, their_codes))
+    their_tiles = lax.ppermute(tiles, "rep", xor_pairs(rep_size, 1))
 
     pieces = [None] * dom_size
     pieces[0] = local_call(
@@ -246,8 +274,8 @@
         pieces[mask + 1] = lax.ppermute(pieces[mask], "dom", xor_pairs(dom_size, 1))
 
     partials = local_call(
-        lambda *refs: aggregate_kernel(dom_size, rep_size, sections, *refs), "aggregate",
-        (codes, their_codes, tiles, their_tiles, *pieces), [SMEM] * 2 + [VMEM] * (2 + dom_size),
+        lambda *refs: aggregate_kernel(dom_size, rep_size, sections, slots, *refs), "aggregate",
+        (tile_row, tile_col, tiles, their_tiles, *pieces), [SMEM] * 2 + [VMEM] * (2 + dom_size),
         (half,) * rep_size,
         (
             jax.ShapeDtypeStruct((dom_size * 2 * row_count // block, block, width // 2), bf16),
@@ -262,7 +290,7 @@
     share = jax.ShapeDtypeStruct((width // 2 + 16, width), f32)
     outcome, keep, send = local_call(
         lambda *refs: dense_kernel(rep_size, *refs), "dense",
-        (*parts, scaled, inv_root, weight, bias.reshape(1, width), cotangent),
+        (*parts, scaled, inv_root, weight, bias_row, cotangent),
         [VMEM] * (rep_size + 5),
         (jax.ShapeDtypeStruct((row_count, width), bf16), share, share),
     )

time: 59.5 us -> 56.1 us (0.943)
  waiting for transfers between devices: 26.1 us -> 23.3 us
  local copies, waits for them, and re-layouts: 3.3 us -> 1.07 us
  Pallas kernels: 4.18 us -> 5.23 us
  starting transfers between devices: 24.8 us -> 25.4 us
    ppermute x2 -> x1, waiting for transfers between devices: 3.56 us -> 0.01 us  [on_device(): their_tiles = lax.ppermute(tiles, 'rep', xor_pairs(rep_size, 1))]
    unnamed x18 -> x16, local copies, waits for them, and re-layouts: 3.3 us -> 1.07 us
    ppermute x2, starting transfers between devices: 7.39 us -> 5.49 us  [on_device(): arrived.append(lax.ppermute(part, ('dom', 'rep'), moves))]
    ppermute x2 -> x1, starting transfers between devices: 1.11 us -> 2.63 us  [on_device(): their_tiles = lax.ppermute(tiles, 'rep', xor_pairs(rep_size, 1))]
    pallas_call x6, Pallas kernels: 4.18 us -> 5.23 us  [local_call(): pl.pallas_call(kernel, out_shape=out_shape, in_specs=in_specs, out_specs=...]
    ppermute x2, starting transfers between devices: 4.41 us -> 3.45 us  [exchange_sum(): third = lax.ppermute(value, axis, xor_pairs(size, now[0] ^ now[1]))]
    ppermute x2, starting transfers between devices: 2.27 us -> 3.2 us  [exchange_sum(): first = lax.ppermute(value, axis, xor_pairs(size, now[0]))]
    ppermute x2, waiting for transfers between devices: 4.44 us -> 3.7 us  [exchange_sum(): second = lax.ppermute(value, axis, xor_pairs(size, now[1]))]
  transfers between devices with their start and end apart: 22 -> 21, of which waited for: 14 -> 13; matrix products, arithmetic and copies ran while one was open for 0% -> 0% of each run, Pallas kernels for 2% -> 1%
where the time goes in v4:
time: 56.1 us; the launch traced here: 55.9 us
  starting transfers between devices  25.4 us (45%)
  waiting for transfers between devices  23.3 us (42%)
  Pallas kernels  5.23 us (9%)
  local copies, waits for them, and re-layouts  1.07 us (2%)
  between operations  0.75 us (1%)
    ppermute x2, starting transfers between devices, on_device(): arrived.append(lax.ppermute(part, ('dom', 'rep'), moves))  5.49 us
    ppermute x3, waiting for transfers between devices, on_device(): pieces[mask] = lax.ppermute(pieces[0], 'dom', xor_pairs(dom_size, mask))  5.33 us
    ppermute x3, waiting for transfers between devices, on_device(): parts.append(lax.ppermute(partials[mask], 'rep', xor_pairs(rep_size, mask)))  5.26 us
    pallas_call x6, Pallas kernels, local_call(): pl.pallas_call(kernel, out_shape=out_shape, in_specs=in_specs, out_specs=...  5.23 us
    ppermute x2, waiting for transfers between devices, exchange_sum(): third = lax.ppermute(value, axis, xor_pairs(size, now[0] ^ now[1]))  4.81 us
    ppermute x3, starting transfers between devices, on_device(): parts.append(lax.ppermute(partials[mask], 'rep', xor_pairs(rep_size, mask)))  4.45 us
    ppermute x3, starting transfers between devices, on_device(): pieces[mask] = lax.ppermute(pieces[0], 'dom', xor_pairs(dom_size, mask))  4.24 us
    ppermute x2, waiting for transfers between devices, exchange_sum(): second = lax.ppermute(value, axis, xor_pairs(size, now[1]))  3.7 us
  transfers between devices with their start and end apart: 21, of which 13 were waited for; matrix products, arithmetic and copies ran while one was open for 0% of the time, Pallas kernels for 1%

profile of v4, /device:TPU:0, one launch (start us, length us, event | category | flops | bytes accessed | tf_op | source)
XLA Modules:
  0.0 55.9 jit_solution(13098047973772941581)
XLA Ops:
  0.6 1.7 %scale.1 = (bf16[256,128]{1,0:T(8,128)(2,1)}, bf16[256,128]{1,0:T(8,128)(2,1)}) custom-call(bf16[256,256]{1,0:T(8,128)(2,1)} %refs_0_.4, s32[1,256]{1,0:T(1,128)} %bitcast.3), custom_call_target="tpu_custom_call" | custom-call | tf_op jit(solution)/shard_map/scale/pallas_call | solution.py:37
  2.3 3.9 %collective-permute-start.1 = (bf16[256,128]{1,0:T(8,128)(2,1)}, bf16[256,128]{1,0:T(8,128)(2,1)S(1)}, u32[]{:S(2)}, u32[]{:S(2)}) collective-permute-start(bf16[256,128]{1,0:T(8,128)(2,1)} %get-tuple-element.19), channel_id=1, source_target_pairs={{0,24},{1,8},{2,16},{3,0},{4,28},{5,12},{6,20},{7,4},{8,1},{9,17},... | collective-permute-start | bytes 196616 | tf_op jit(solution)/shard_map/ppermute | solution.py:251
  6.3 1.5 %collective-permute-start.2 = (bf16[256,128]{1,0:T(8,128)(2,1)}, bf16[256,128]{1,0:T(8,128)(2,1)S(1)}, u32[]{:S(2)}, u32[]{:S(2)}) collective-permute-start(bf16[256,128]{1,0:T(8,128)(2,1)} %get-tuple-element.20), channel_id=1, source_target_pairs={{0,9},{1,25},{2,17},{3,1},{4,13},{5,29},{6,21},{7,5},{8,16},{9,0},... | collective-permute-start | bytes 196616 | tf_op jit(solution)/shard_map/ppermute | solution.py:251
  7.9 1.0 %copy-done = s32[1,2,4,128,128]{4,3,2,1,0:T(8,128)S(1)} copy-done((s32[1,2,4,128,128]{4,3,2,1,0:T(8,128)S(1)}, s32[1,2,4,128,128]{4,3,2,1,0:T(8,128)}, u32[]{:S(2)}) %copy-start) | copy-done | bytes 524312
  8.9 0.8 %prepare.1 = (bf16[1040,128]{1,0:T(8,128)(2,1)S(1)}, bf16[256,256]{1,0:T(8,128)(2,1)S(1)}, f32[256,128]{1,0:T(8,128)S(1)}, f32[1,256]{1,0:T(1,128)S(1)}) custom-call(s32[1,2,4,128,128]{4,3,2,1,0:T(8,128)S(1)} %copy-done, s32[1,2,4]{2,1,0:T(2,128)S(1)} %copy-done.5, s32[1,2,4]{2,1,0:T(2,128)S(1)} %copy-done.6, bf16[256,256]{1,0:T(8,128)(2,1)S(1)} %copy-done.1, ...), custom_call_target="tpu_custom_call" | custom-call | tf_op jit(solution)/shard_map/prepare/pallas_call | solution.py:37
  9.7 2.6 %collective-permute-start = (bf16[1040,128]{1,0:T(8,128)(2,1)S(1)}, bf16[1040,128]{1,0:T(8,128)(2,1)S(1)}, u32[]{:S(2)}, u32[]{:S(2)}) collective-permute-start(bf16[1040,128]{1,0:T(8,128)(2,1)S(1)} %get-tuple-element.18.refs_2_), channel_id=1, source_target_pairs={{0,1},{1,0},{2,3},{3,2},{4,5},{5,4},{6,7},{7,6},{8,9},{9,8},{10,11... | collective-permute-start | bytes 798728 | tf_op jit(solution)/shard_map/ppermute | solution.py:264
  12.3 0.6 %collective-permute-done.2.second_ref = bf16[256,128]{1,0:T(8,128)(2,1)S(1)} collective-permute-done((bf16[256,128]{1,0:T(8,128)(2,1)}, bf16[256,128]{1,0:T(8,128)(2,1)S(1)}, u32[]{:S(2)}, u32[]{:S(2)}) %collective-permute-start.2) | collective-permute-done | bytes 65568 | tf_op jit(solution)/shard_map/ppermute | solution.py:251
  13.0 3.6 %collective-permute-start.8 = (bf16[512,128]{1,0:T(8,128)(2,1)S(1)}, bf16[512,128]{1,0:T(8,128)(2,1)S(1)}, u32[]{:S(2)}, u32[]{:S(2)}) collective-permute-start(bf16[512,128]{1,0:T(8,128)(2,1)S(1)} %join.1.refs_4_), channel_id=1, source_target_pairs={{0,24},{4,28},{8,16},{12,20},{16,8},{20,12},{24,0},{28,4},{1,25},{... | collective-permute-start | bytes 393224 | tf_op jit(solution)/shard_map/ppermute | solution.py:272
  16.6 0.6 %collective-permute-start.4 = (bf16[512,128]{1,0:T(8,128)(2,1)S(1)}, bf16[512,128]{1,0:T(8,128)(2,1)S(1)}, u32[]{:S(2)}, u32[]{:S(2)}) collective-permute-start(bf16[512,128]{1,0:T(8,128)(2,1)S(1)} %join.1.refs_4_), channel_id=1, source_target_pairs={{0,8},{4,12},{8,0},{12,4},{16,24},{20,28},{24,16},{28,20},{1,9},{5... | collective-permute-start | bytes 393224 | tf_op jit(solution)/shard_map/ppermute | solution.py:272
  17.2 3.2 %collective-permute-done.8.refs_10_ = bf16[512,128]{1,0:T(8,128)(2,1)S(1)} collective-permute-done((bf16[512,128]{1,0:T(8,128)(2,1)S(1)}, bf16[512,128]{1,0:T(8,128)(2,1)S(1)}, u32[]{:S(2)}, u32[]{:S(2)}) %collective-permute-start.8) | collective-permute-done | bytes 131104 | tf_op jit(solution)/shard_map/ppermute | solution.py:272
  20.4 2.1 %collective-permute-done.6.refs_8_ = bf16[512,128]{1,0:T(8,128)(2,1)S(1)} collective-permute-done((bf16[512,128]{1,0:T(8,128)(2,1)S(1)}, bf16[512,128]{1,0:T(8,128)(2,1)S(1)}, u32[]{:S(2)}, u32[]{:S(2)}) %collective-permute-start.6) | collective-permute-done | bytes 131104 | tf_op jit(solution)/shard_map/ppermute | solution.py:272
  22.5 0.5 collective-permute-start.5
  23.1 0.8 %collective-permute-done.7.refs_9_ = bf16[512,128]{1,0:T(8,128)(2,1)S(1)} collective-permute-done((bf16[512,128]{1,0:T(8,128)(2,1)S(1)}, bf16[512,128]{1,0:T(8,128)(2,1)S(1)}, u32[]{:S(2)}, u32[]{:S(2)}) %collective-permute-start.7) | collective-permute-done | bytes 131104 | tf_op jit(solution)/shard_map/ppermute | solution.py:274
  24.1 1.0 %aggregate.1 = (bf16[256,128]{1,0:T(8,128)(2,1)S(1)}, bf16[256,128]{1,0:T(8,128)(2,1)S(1)}, bf16[256,128]{1,0:T(8,128)(2,1)S(1)}, bf16[256,128]{1,0:T(8,128)(2,1)S(1)}) custom-call(s32[1,2,4]{2,1,0:T(2,128)S(1)} %copy-done.5, s32[1,2,4]{2,1,0:T(2,128)S(1)} %copy-done.6, bf16[1040,128]{1,0:T(8,128)(2,1)S(1)} %get-tuple-element.18.refs_2_, ...), custom_call_target="tpu_custom_call" | custom-call | tf_op jit(solution)/shard_map/aggregate/pallas_call | solution.py:37
  25.1 1.1 %collective-permute-start.10 = (bf16[256,128]{1,0:T(8,128)(2,1)S(1)}, bf16[256,128]{1,0:T(8,128)(2,1)S(1)}, u32[]{:S(2)}, u32[]{:S(2)}) collective-permute-start(bf16[256,128]{1,0:T(8,128)(2,1)S(1)} %get-tuple-element.22), channel_id=1, source_target_pairs={{0,1},{1,0},{2,3},{3,2},{4,5},{5,4},{6,7},{7,6},{8,9},{9,8},{10,11... | collective-permute-start | bytes 196616 | tf_op jit(solution)/shard_map/ppermute | solution.py:288
  26.2 2.5 %collective-permute-start.11 = (bf16[256,128]{1,0:T(8,128)(2,1)S(1)}, bf16[256,128]{1,0:T(8,128)(2,1)S(1)}, u32[]{:S(2)}, u32[]{:S(2)}) collective-permute-start(bf16[256,128]{1,0:T(8,128)(2,1)S(1)} %get-tuple-element.23), channel_id=1, source_target_pairs={{0,2},{1,3},{2,0},{3,1},{4,6},{5,7},{6,4},{7,5},{8,10},{9,11},{10,... | collective-permute-start | bytes 196616 | tf_op jit(solution)/shard_map/ppermute | solution.py:288
  28.7 0.9 %collective-permute-start.12 = (bf16[256,128]{1,0:T(8,128)(2,1)S(1)}, bf16[256,128]{1,0:T(8,128)(2,1)S(1)}, u32[]{:S(2)}, u32[]{:S(2)}) collective-permute-start(bf16[256,128]{1,0:T(8,128)(2,1)S(1)} %get-tuple-element.24), channel_id=1, source_target_pairs={{0,3},{1,2},{2,1},{3,0},{4,7},{5,6},{6,5},{7,4},{8,11},{9,10},{10,... | collective-permute-start | bytes 196616 | tf_op jit(solution)/shard_map/ppermute | solution.py:288
  29.6 4.2 %collective-permute-done.11.refs_2_ = bf16[256,128]{1,0:T(8,128)(2,1)S(1)} collective-permute-done((bf16[256,128]{1,0:T(8,128)(2,1)S(1)}, bf16[256,128]{1,0:T(8,128)(2,1)S(1)}, u32[]{:S(2)}, u32[]{:S(2)}) %collective-permute-start.11) | collective-permute-done | bytes 65568 | tf_op jit(solution)/shard_map/ppermute | solution.py:288
  33.8 1.0 %collective-permute-done.12.refs_3_ = bf16[256,128]{1,0:T(8,128)(2,1)S(1)} collective-permute-done((bf16[256,128]{1,0:T(8,128)(2,1)S(1)}, bf16[256,128]{1,0:T(8,128)(2,1)S(1)}, u32[]{:S(2)}, u32[]{:S(2)}) %collective-permute-start.12) | collective-permute-done | bytes 65568 | tf_op jit(solution)/shard_map/ppermute | solution.py:288
  34.8 1.0 %dense.1 = (bf16[256,256]{1,0:T(8,128)(2,1)}, f32[144,256]{1,0:T(8,128)S(1)}, f32[144,256]{1,0:T(8,128)S(1)}) custom-call(bf16[256,128]{1,0:T(8,128)(2,1)S(1)} %get-tuple-element.21.refs_0_, bf16[256,128]{1,0:T(8,128)(2,1)S(1)} %collective-permute-done.10.refs_1_, bf16[256,128]{1,0:T(8,128)(2,1)S(1)} %collective-permute-done.11.refs_2_, ...), custom_call_target="tpu_custom_call" | custom-call | tf_op jit(solution)/shard_map/dense/pallas_call | solution.py:37
  35.8 1.4 %collective-permute-done.13 = f32[144,256]{1,0:T(8,128)S(1)} collective-permute-done((f32[144,256]{1,0:T(8,128)S(1)}, f32[144,256]{1,0:T(8,128)S(1)}, u32[]{:S(2)}, u32[]{:S(2)}) %collective-permute-start.13) | collective-permute-done | bytes 147488 | tf_op jit(solution)/shard_map/ppermute | solution.py:299
  37.2 1.2 %collective-permute-start.16 = (bf16[144,256]{1,0:T(8,128)(2,1)S(1)}, bf16[144,256]{1,0:T(8,128)(2,1)S(1)}, u32[]{:S(2)}, u32[]{:S(2)}) collective-permute-start(bf16[144,256]{1,0:T(8,128)(2,1)S(1)} %add_convert_fusion.2), channel_id=1, source_target_pairs={{0,24},{4,28},{8,16},{12,20},{16,8},{20,12},{24,0},{28,4},{1,25},{... | collective-permute-start | bytes 221192 | tf_op jit(solution)/shard_map/ppermute | solution.py:217
  38.4 1.0 %collective-permute-start.15 = (bf16[144,256]{1,0:T(8,128)(2,1)S(1)}, bf16[144,256]{1,0:T(8,128)(2,1)S(1)}, u32[]{:S(2)}, u32[]{:S(2)}) collective-permute-start(bf16[144,256]{1,0:T(8,128)(2,1)S(1)} %add_convert_fusion.2), channel_id=1, source_target_pairs={{0,16},{4,20},{8,24},{12,28},{16,0},{20,4},{24,8},{28,12},{1,17},{... | collective-permute-start | bytes 221192 | tf_op jit(solution)/shard_map/ppermute | solution.py:216
  39.4 1.4 %collective-permute-start.14 = (bf16[144,256]{1,0:T(8,128)(2,1)S(1)}, bf16[144,256]{1,0:T(8,128)(2,1)S(1)}, u32[]{:S(2)}, u32[]{:S(2)}) collective-permute-start(bf16[144,256]{1,0:T(8,128)(2,1)S(1)} %add_convert_fusion.2), channel_id=1, source_target_pairs={{0,8},{4,12},{8,0},{12,4},{16,24},{20,28},{24,16},{28,20},{1,9},{5... | collective-permute-start | bytes 221192 | tf_op jit(solution)/shard_map/ppermute | solution.py:212
  40.8 2.2 %collective-permute-done.16 = bf16[144,256]{1,0:T(8,128)(2,1)S(1)} collective-permute-done((bf16[144,256]{1,0:T(8,128)(2,1)S(1)}, bf16[144,256]{1,0:T(8,128)(2,1)S(1)}, u32[]{:S(2)}, u32[]{:S(2)}) %collective-permute-start.16) | collective-permute-done | bytes 73760 | tf_op jit(solution)/shard_map/ppermute | solution.py:217
  43.0 1.0 %collective-permute-done.15 = bf16[144,256]{1,0:T(8,128)(2,1)S(1)} collective-permute-done((bf16[144,256]{1,0:T(8,128)(2,1)S(1)}, bf16[144,256]{1,0:T(8,128)(2,1)S(1)}, u32[]{:S(2)}, u32[]{:S(2)}) %collective-permute-start.15) | collective-permute-done | bytes 73760 | tf_op jit(solution)/shard_map/ppermute | solution.py:216
  44.1 2.2 %collective-permute-start.19 = (bf16[144,256]{1,0:T(8,128)(2,1)S(1)}, bf16[144,256]{1,0:T(8,128)(2,1)S(1)}, u32[]{:S(2)}, u32[]{:S(2)}) collective-permute-start(bf16[144,256]{1,0:T(8,128)(2,1)S(1)} %add_convert_fusion.1), channel_id=1, source_target_pairs={{0,3},{1,2},{2,1},{3,0},{4,7},{5,6},{6,5},{7,4},{8,11},{9,10},{10,... | collective-permute-start | bytes 221192 | tf_op jit(solution)/shard_map/ppermute | solution.py:217
  46.7 1.8 %collective-permute-start.17 = (bf16[144,256]{1,0:T(8,128)(2,1)S(1)}, bf16[144,256]{1,0:T(8,128)(2,1)S(1)}, u32[]{:S(2)}, u32[]{:S(2)}) collective-permute-start(bf16[144,256]{1,0:T(8,128)(2,1)S(1)} %add_convert_fusion.1), channel_id=1, source_target_pairs={{0,1},{1,0},{2,3},{3,2},{4,5},{5,4},{6,7},{7,6},{8,9},{9,8},{10,11... | collective-permute-start | bytes 221192 | tf_op jit(solution)/shard_map/ppermute | solution.py:212
  48.6 2.6 %collective-permute-done.19 = bf16[144,256]{1,0:T(8,128)(2,1)S(1)} collective-permute-done((bf16[144,256]{1,0:T(8,128)(2,1)S(1)}, bf16[144,256]{1,0:T(8,128)(2,1)S(1)}, u32[]{:S(2)}, u32[]{:S(2)}) %collective-permute-start.19) | collective-permute-done | bytes 73760 | tf_op jit(solution)/shard_map/ppermute | solution.py:217
  51.1 2.7 %collective-permute-done.18 = bf16[144,256]{1,0:T(8,128)(2,1)S(1)} collective-permute-done((bf16[144,256]{1,0:T(8,128)(2,1)S(1)}, bf16[144,256]{1,0:T(8,128)(2,1)S(1)}, u32[]{:S(2)}, u32[]{:S(2)}) %collective-permute-start.18) | collective-permute-done | bytes 73760 | tf_op jit(solution)/shard_map/ppermute | solution.py:216
  53.9 1.3 %collective-permute-done.20.other_ref = bf16[144,256]{1,0:T(8,128)(2,1)S(1)} collective-permute-done((bf16[144,256]{1,0:T(8,128)(2,1)S(1)}, bf16[144,256]{1,0:T(8,128)(2,1)S(1)}, u32[]{:S(2)}, u32[]{:S(2)}) %collective-permute-start.20) | collective-permute-done | bytes 73760 | tf_op jit(solution)/shard_map/ppermute | solution.py:302
  55.2 0.7 %finish.1 = (f32[256,256]{1,0:T(8,128)}, f32[1,256]{1,0:T(1,128)}) custom-call(bf16[144,256]{1,0:T(8,128)(2,1)S(1)} %add_convert_fusion.mine_ref, bf16[144,256]{1,0:T(8,128)(2,1)S(1)} %collective-permute-done.20.other_ref), custom_call_target="tpu_custom_call" | custom-call | tf_op jit(solution)/shard_map/finish/pallas_call | solution.py:37
  (35 shorter events, 0.8 us)
Async XLA Ops:
  0.6 7.2 %copy-start.1 = (bf16[256,256]{1,0:T(8,128)(2,1)S(1)}, bf16[256,256]{1,0:T(8,128)(2,1)}, u32[]{:S(2)}) copy-start(bf16[256,256]{1,0:T(8,128)(2,1)} %refs_0_.4) | copy-start | bytes 393220
  2.3 5.5 %copy-start.7 = (f32[256]{0:T(256)S(1)}, f32[256]{0:T(256)}, u32[]{:S(2)}) copy-start(f32[256]{0:T(256)} %param.15) | copy-start | bytes 3076
  2.3 10.0 %collective-permute-start.1 = (bf16[256,128]{1,0:T(8,128)(2,1)}, bf16[256,128]{1,0:T(8,128)(2,1)S(1)}, u32[]{:S(2)}, u32[]{:S(2)}) collective-permute-start(bf16[256,128]{1,0:T(8,128)(2,1)} %get-tuple-element.19), channel_id=1, source_target_pairs={{0,24},{1,8},{2,16},{3,0},{4,28},{5,12},{6,20},{7,4},{8,1},{9,17},... | collective-permute-start | bytes 196616 | tf_op jit(solution)/shard_map/ppermute | solution.py:251
  6.3 1.6 %copy-start.5 = (s32[1,2,4]{2,1,0:T(2,128)S(1)}, s32[1,2,4]{2,1,0:T(2,128)}, u32[]{:S(2)}) copy-start(s32[1,2,4]{2,1,0:T(2,128)} %refs_0_.5) | copy-start | bytes 100
  6.3 1.6 %copy-start.6 = (s32[1,2,4]{2,1,0:T(2,128)S(1)}, s32[1,2,4]{2,1,0:T(2,128)}, u32[]{:S(2)}) copy-start(s32[1,2,4]{2,1,0:T(2,128)} %refs_1_.3) | copy-start | bytes 100
  6.3 1.6 %copy-start.4 = (s32[256]{0:T(256)S(1)}, s32[256]{0:T(256)}, u32[]{:S(2)}) copy-start(s32[256]{0:T(256)} %param.10) | copy-start | bytes 3076
  6.3 6.6 %collective-permute-start.2 = (bf16[256,128]{1,0:T(8,128)(2,1)}, bf16[256,128]{1,0:T(8,128)(2,1)S(1)}, u32[]{:S(2)}, u32[]{:S(2)}) collective-permute-start(bf16[256,128]{1,0:T(8,128)(2,1)} %get-tuple-element.20), channel_id=1, source_target_pairs={{0,9},{1,25},{2,17},{3,1},{4,13},{5,29},{6,21},{7,5},{8,16},{9,0},... | collective-permute-start | bytes 196616 | tf_op jit(solution)/shard_map/ppermute | solution.py:251
  7.9 1.0 %copy-start = (s32[1,2,4,128,128]{4,3,2,1,0:T(8,128)S(1)}, s32[1,2,4,128,128]{4,3,2,1,0:T(8,128)}, u32[]{:S(2)}) copy-start(s32[1,2,4,128,128]{4,3,2,1,0:T(8,128)} %refs_0_.3) | copy-start | bytes 1572868
  9.7 13.4 %collective-permute-start = (bf16[1040,128]{1,0:T(8,128)(2,1)S(1)}, bf16[1040,128]{1,0:T(8,128)(2,1)S(1)}, u32[]{:S(2)}, u32[]{:S(2)}) collective-permute-start(bf16[1040,128]{1,0:T(8,128)(2,1)S(1)} %get-tuple-element.18.refs_2_), channel_id=1, source_target_pairs={{0,1},{1,0},{2,3},{3,2},{4,5},{5,4},{6,7},{7,6},{8,9},{9,8},{10,11... | collective-permute-start | bytes 798728 | tf_op jit(solution)/shard_map/ppermute | solution.py:264
  12.9 21.9 %copy-start.2 = (bf16[256,256]{1,0:T(8,128)(2,1)S(1)}, bf16[256,256]{1,0:T(8,128)(2,1)}, u32[]{:S(2)}) copy-start(bf16[256,256]{1,0:T(8,128)(2,1)} %refs_6_.1) | copy-start | bytes 393220
  12.9 21.9 %copy-start.3 = (bf16[256,256]{1,0:T(8,128)(2,1)S(1)}, bf16[256,256]{1,0:T(8,128)(2,1)}, u32[]{:S(2)}) copy-start(bf16[256,256]{1,0:T(8,128)(2,1)} %refs_8_.1) | copy-start | bytes 393220
  13.0 7.5 %collective-permute-start.8 = (bf16[512,128]{1,0:T(8,128)(2,1)S(1)}, bf16[512,128]{1,0:T(8,128)(2,1)S(1)}, u32[]{:S(2)}, u32[]{:S(2)}) collective-permute-start(bf16[512,128]{1,0:T(8,128)(2,1)S(1)} %join.1.refs_4_), channel_id=1, source_target_pairs={{0,24},{4,28},{8,16},{12,20},{16,8},{20,12},{24,0},{28,4},{1,25},{... | collective-permute-start | bytes 393224 | tf_op jit(solution)/shard_map/ppermute | solution.py:272
  16.5 6.0 %collective-permute-start.6 = (bf16[512,128]{1,0:T(8,128)(2,1)S(1)}, bf16[512,128]{1,0:T(8,128)(2,1)S(1)}, u32[]{:S(2)}, u32[]{:S(2)}) collective-permute-start(bf16[512,128]{1,0:T(8,128)(2,1)S(1)} %join.1.refs_4_), channel_id=1, source_target_pairs={{0,16},{4,20},{8,24},{12,28},{16,0},{20,4},{24,8},{28,12},{1,17},{... | collective-permute-start | bytes 393224 | tf_op jit(solution)/shard_map/ppermute | solution.py:272
  16.6 6.0 %collective-permute-start.4 = (bf16[512,128]{1,0:T(8,128)(2,1)S(1)}, bf16[512,128]{1,0:T(8,128)(2,1)S(1)}, u32[]{:S(2)}, u32[]{:S(2)}) collective-permute-start(bf16[512,128]{1,0:T(8,128)(2,1)S(1)} %join.1.refs_4_), channel_id=1, source_target_pairs={{0,8},{4,12},{8,0},{12,4},{16,24},{20,28},{24,16},{28,20},{1,9},{5... | collective-permute-start | bytes 393224 | tf_op jit(solution)/shard_map/ppermute | solution.py:272
  17.2 5.9 %collective-permute-start.3 = (bf16[512,128]{1,0:T(8,128)(2,1)S(1)}, bf16[512,128]{1,0:T(8,128)(2,1)S(1)}, u32[]{:S(2)}, u32[]{:S(2)}) collective-permute-start(bf16[512,128]{1,0:T(8,128)(2,1)S(1)} %join.1.refs_4_), channel_id=1, source_target_pairs={{0,4},{4,0},{8,12},{12,8},{16,20},{20,16},{24,28},{28,24},{1,5},{5... | collective-permute-start | bytes 393224 | tf_op jit(solution)/shard_map/ppermute | solution.py:274
  20.4 2.6 %collective-permute-start.9 = (bf16[512,128]{1,0:T(8,128)(2,1)S(1)}, bf16[512,128]{1,0:T(8,128)(2,1)S(1)}, u32[]{:S(2)}, u32[]{:S(2)}) collective-permute-start(bf16[512,128]{1,0:T(8,128)(2,1)S(1)} %collective-permute-done.8.refs_10_), channel_id=1, source_target_pairs={{0,4},{4,0},{8,12},{12,8},{16,20},{20,16},{24,28},{28,24},{1,5},{5... | collective-permute-start | bytes 393224 | tf_op jit(solution)/shard_map/ppermute | solution.py:274
  22.5 1.3 %collective-permute-start.7 = (bf16[512,128]{1,0:T(8,128)(2,1)S(1)}, bf16[512,128]{1,0:T(8,128)(2,1)S(1)}, u32[]{:S(2)}, u32[]{:S(2)}) collective-permute-start(bf16[512,128]{1,0:T(8,128)(2,1)S(1)} %collective-permute-done.6.refs_8_), channel_id=1, source_target_pairs={{0,4},{4,0},{8,12},{12,8},{16,20},{20,16},{24,28},{28,24},{1,5},{5... | collective-permute-start | bytes 393224 | tf_op jit(solution)/shard_map/ppermute | solution.py:274
  22.5 1.5 %collective-permute-start.5 = (bf16[512,128]{1,0:T(8,128)(2,1)S(1)}, bf16[512,128]{1,0:T(8,128)(2,1)S(1)}, u32[]{:S(2)}, u32[]{:S(2)}) collective-permute-start(bf16[512,128]{1,0:T(8,128)(2,1)S(1)} %collective-permute-done.4.refs_6_), channel_id=1, source_target_pairs={{0,4},{4,0},{8,12},{12,8},{16,20},{20,16},{24,28},{28,24},{1,5},{5... | collective-permute-start | bytes 393224 | tf_op jit(solution)/shard_map/ppermute | solution.py:274
  25.1 4.5 %collective-permute-start.10 = (bf16[256,128]{1,0:T(8,128)(2,1)S(1)}, bf16[256,128]{1,0:T(8,128)(2,1)S(1)}, u32[]{:S(2)}, u32[]{:S(2)}) collective-permute-start(bf16[256,128]{1,0:T(8,128)(2,1)S(1)} %get-tuple-element.22), channel_id=1, source_target_pairs={{0,1},{1,0},{2,3},{3,2},{4,5},{5,4},{6,7},{7,6},{8,9},{9,8},{10,11... | collective-permute-start | bytes 196616 | tf_op jit(solution)/shard_map/ppermute | solution.py:288
  26.2 7.6 %collective-permute-start.11 = (bf16[256,128]{1,0:T(8,128)(2,1)S(1)}, bf16[256,128]{1,0:T(8,128)(2,1)S(1)}, u32[]{:S(2)}, u32[]{:S(2)}) collective-permute-start(bf16[256,128]{1,0:T(8,128)(2,1)S(1)} %get-tuple-element.23), channel_id=1, source_target_pairs={{0,2},{1,3},{2,0},{3,1},{4,6},{5,7},{6,4},{7,5},{8,10},{9,11},{10,... | collective-permute-start | bytes 196616 | tf_op jit(solution)/shard_map/ppermute | solution.py:288
  28.7 6.1 %collective-permute-start.12 = (bf16[256,128]{1,0:T(8,128)(2,1)S(1)}, bf16[256,128]{1,0:T(8,128)(2,1)S(1)}, u32[]{:S(2)}, u32[]{:S(2)}) collective-permute-start(bf16[256,128]{1,0:T(8,128)(2,1)S(1)} %get-tuple-element.24), channel_id=1, source_target_pairs={{0,3},{1,2},{2,1},{3,0},{4,7},{5,6},{6,5},{7,4},{8,11},{9,10},{10,... | collective-permute-start | bytes 196616 | tf_op jit(solution)/shard_map/ppermute | solution.py:288
  35.8 1.4 %collective-permute-start.13 = (f32[144,256]{1,0:T(8,128)S(1)}, f32[144,256]{1,0:T(8,128)S(1)}, u32[]{:S(2)}, u32[]{:S(2)}) collective-permute-start(f32[144,256]{1,0:T(8,128)S(1)} %get-tuple-element.30), channel_id=1, source_target_pairs={{0,4},{4,0},{8,12},{12,8},{16,20},{20,16},{24,28},{28,24},{1,5},{5... | collective-permute-start | bytes 442376 | tf_op jit(solution)/shard_map/ppermute | solution.py:299
  37.2 5.8 %collective-permute-start.16 = (bf16[144,256]{1,0:T(8,128)(2,1)S(1)}, bf16[144,256]{1,0:T(8,128)(2,1)S(1)}, u32[]{:S(2)}, u32[]{:S(2)}) collective-permute-start(bf16[144,256]{1,0:T(8,128)(2,1)S(1)} %add_convert_fusion.2), channel_id=1, source_target_pairs={{0,24},{4,28},{8,16},{12,20},{16,8},{20,12},{24,0},{28,4},{1,25},{... | collective-permute-start | bytes 221192 | tf_op jit(solution)/shard_map/ppermute | solution.py:217
  38.4 5.6 %collective-permute-start.15 = (bf16[144,256]{1,0:T(8,128)(2,1)S(1)}, bf16[144,256]{1,0:T(8,128)(2,1)S(1)}, u32[]{:S(2)}, u32[]{:S(2)}) collective-permute-start(bf16[144,256]{1,0:T(8,128)(2,1)S(1)} %add_convert_fusion.2), channel_id=1, source_target_pairs={{0,16},{4,20},{8,24},{12,28},{16,0},{20,4},{24,8},{28,12},{1,17},{... | collective-permute-start | bytes 221192 | tf_op jit(solution)/shard_map/ppermute | solution.py:216
  39.4 4.7 %collective-permute-start.14 = (bf16[144,256]{1,0:T(8,128)(2,1)S(1)}, bf16[144,256]{1,0:T(8,128)(2,1)S(1)}, u32[]{:S(2)}, u32[]{:S(2)}) collective-permute-start(bf16[144,256]{1,0:T(8,128)(2,1)S(1)} %add_convert_fusion.2), channel_id=1, source_target_pairs={{0,8},{4,12},{8,0},{12,4},{16,24},{20,28},{24,16},{28,20},{1,9},{5... | collective-permute-start | bytes 221192 | tf_op jit(solution)/shard_map/ppermute | solution.py:212
  44.1 7.0 %collective-permute-start.19 = (bf16[144,256]{1,0:T(8,128)(2,1)S(1)}, bf16[144,256]{1,0:T(8,128)(2,1)S(1)}, u32[]{:S(2)}, u32[]{:S(2)}) collective-permute-start(bf16[144,256]{1,0:T(8,128)(2,1)S(1)} %add_convert_fusion.1), channel_id=1, source_target_pairs={{0,3},{1,2},{2,1},{3,0},{4,7},{5,6},{6,5},{7,4},{8,11},{9,10},{10,... | collective-permute-start | bytes 221192 | tf_op jit(solution)/shard_map/ppermute | solution.py:217
  46.3 7.5 %collective-permute-start.18 = (bf16[144,256]{1,0:T(8,128)(2,1)S(1)}, bf16[144,256]{1,0:T(8,128)(2,1)S(1)}, u32[]{:S(2)}, u32[]{:S(2)}) collective-permute-start(bf16[144,256]{1,0:T(8,128)(2,1)S(1)} %add_convert_fusion.1), channel_id=1, source_target_pairs={{0,2},{1,3},{2,0},{3,1},{4,6},{5,7},{6,4},{7,5},{8,10},{9,11},{10,... | collective-permute-start | bytes 221192 | tf_op jit(solution)/shard_map/ppermute | solution.py:216
  46.7 7.1 %collective-permute-start.17 = (bf16[144,256]{1,0:T(8,128)(2,1)S(1)}, bf16[144,256]{1,0:T(8,128)(2,1)S(1)}, u32[]{:S(2)}, u32[]{:S(2)}) collective-permute-start(bf16[144,256]{1,0:T(8,128)(2,1)S(1)} %add_convert_fusion.1), channel_id=1, source_target_pairs={{0,1},{1,0},{2,3},{3,2},{4,5},{5,4},{6,7},{7,6},{8,9},{9,8},{10,11... | collective-permute-start | bytes 221192 | tf_op jit(solution)/shard_map/ppermute | solution.py:212
  53.8 1.3 %collective-permute-start.20 = (bf16[144,256]{1,0:T(8,128)(2,1)S(1)}, bf16[144,256]{1,0:T(8,128)(2,1)S(1)}, u32[]{:S(2)}, u32[]{:S(2)}) collective-permute-start(bf16[144,256]{1,0:T(8,128)(2,1)S(1)} %add_convert_fusion.mine_ref), channel_id=1, source_target_pairs={{0,4},{4,0},{8,12},{12,8},{16,20},{20,16},{24,28},{28,24},{1,5},{5... | collective-permute-start | bytes 221192 | tf_op jit(solution)/shard_map/ppermute | solution.py:302

commit v5 on v4

--- a/solution.py
+++ b/solution.py
@@ -103,50 +103,46 @@
 
 
 def aggregate_kernel(dom_size, rep_size, sections, slots, *refs):
-    row_ref, col_ref, *tile_refs = refs[:4]
-    piece_refs, refs = refs[4 : 4 + dom_size], refs[4 + dom_size :]
+    tile_refs, refs = refs[:2], refs[2:]
+    piece_refs, refs = refs[:dom_size], refs[dom_size:]
     out_refs, (held, acc) = refs[:rep_size], refs[rep_size:]
     block = tile_refs[0].shape[1]
     tile_rows = sections * slots * block
     block_count = acc.shape[0]
     per_piece = piece_refs[0].shape[0] // block
     per_slice = per_piece // 2
-    code_rows = tile_refs[1][tile_rows:, :].astype(jnp.float32)
-    lane = lax.broadcasted_iota(jnp.int32, code_rows.shape, 1)
+    code_rows = [tile_ref[tile_rows:, :].astype(jnp.float32) for tile_ref in tile_refs]
+    lane = lax.broadcasted_iota(jnp.int32, code_rows[0].shape, 1)
     dom, rep = lax.axis_index("dom"), lax.axis_index("rep")
 
-    def code_of(at):
-        return jnp.max(jnp.where(lane == at, code_rows, 0.0)).astype(jnp.int32)
-
-    def add_slot(which, at, row, col):
+    def code_of(which, at):
+        return jnp.max(jnp.where(lane == at, code_rows[which], 0.0)).astype(jnp.int32)
+
+    def add_slot(which, at, code):
+        row, col = code // block_count, code % block_count
         chip = chip_of(rep ^ which, rep, col // per_slice, rep_size)
         mask = (chip * sections + at // slots) ^ dom
         rows = held[mask * per_piece + which * per_slice + col % per_slice]
         tile = tile_refs[which][pl.ds(at * block, block), :]
         acc[row] += jnp.dot(tile, rows, preferred_element_type=jnp.float32)
 
-    def own_step(at, carry):
-        section, slot = at // slots, at % slots
-        add_slot(0, at, row_ref[0, section, slot], col_ref[0, section, slot])
+    def both_step(at, carry):
+        for which in range(2):
+            add_slot(which, at, code_of(which, at))
         return carry
 
-    def their_step(at, carry):
-        code = code_of(at)
-        add_slot(1, at, code // block_count, code % block_count)
-        return carry
-
     few = sections * slots <= 8
-    codes = [code_of(at) for at in range(sections * slots)] if few else None
+    order = [(which, at) for which in range(2) for at in range(sections * slots)]
+    codes = [code_of(*each) for each in order] if few else None
     for mask, piece_ref in enumerate(piece_refs):
         for at in range(per_piece):
             held[mask * per_piece + at] = piece_ref[at * block : (at + 1) * block, :]
     acc[...] = jnp.zeros_like(acc)
-    lax.fori_loop(0, sections * slots, own_step, 0, unroll=few)
     if few:
-        for at, code in enumerate(codes):
-            add_slot(1, at, code // block_count, code % block_count)
+        for (which, at), code in zip(order, codes):
+            add_slot(which, at, code)
     else:
-        lax.fori_loop(0, sections * slots, their_step, 0)
+        lax.fori_loop(0, sections * slots, both_step, 0)
 
     for mask, out_ref in enumerate(out_refs):
         for at in range(per_slice):
@@ -191,7 +187,7 @@
     send_ref[kept:, :] = extra
 
 
-def finish_kernel(mine_ref, other_ref, weight_ref, bias_ref):
+def finish_kernel(mine_ref, other_ref, outcome_ref, weight_ref, bias_ref, out_ref):
     kept = weight_ref.shape[0] // 2
     first = lax.axis_index("dom") % 2 == 0
     mine = mine_ref[...].astype(jnp.float32)
@@ -199,6 +195,7 @@
     weight_ref[:kept, :] = jnp.where(first, mine[:kept], other[:kept])
     weight_ref[kept:, :] = jnp.where(first, other[:kept], mine[:kept])
     bias_ref[...] = mine[kept : kept + 1]
+    out_ref[...] = outcome_ref[...]
 
 
 def xor_pairs(size, mask):
@@ -275,7 +272,7 @@
 
     partials = local_call(
         lambda *refs: aggregate_kernel(dom_size, rep_size, sections, slots, *refs), "aggregate",
-        (tile_row, tile_col, tiles, their_tiles, *pieces), [SMEM] * 2 + [VMEM] * (2 + dom_size),
+        (tiles, their_tiles, *pieces), [VMEM] * (2 + dom_size),
         (half,) * rep_size,
         (
             jax.ShapeDtypeStruct((dom_size * 2 * row_count // block, block, width // 2), bf16),
@@ -300,9 +297,13 @@
     mine = exchange_sum(mine, "dom", bits_of(dom_size)[1:])
     mine = exchange_sum(mine, "rep", bits_of(rep_size))
     other = lax.ppermute(mine, "dom", swap)
-    weight_grad, bias_grad = local_call(
-        finish_kernel, "finish", (mine, other), [VMEM] * 2,
-        (jax.ShapeDtypeStruct((width, width), f32), jax.ShapeDtypeStruct((1, width), f32)),
+    weight_grad, bias_grad, outcome = local_call(
+        finish_kernel, "finish", (mine, other, outcome), [VMEM] * 3,
+        (
+            jax.ShapeDtypeStruct((width, width), f32),
+            jax.ShapeDtypeStruct((1, width), f32),
+            jax.ShapeDtypeStruct((row_count, width), bf16),
+        ),
     )
     return (outcome, weight_grad, bias_grad.reshape(width))
 

time: 56.1 us -> 55.3 us (0.986)
  Pallas kernels: 5.23 us -> 4.34 us
    pallas_call x6, Pallas kernels: 5.23 us -> 4.34 us  [local_call(): pl.pallas_call(kernel, out_shape=out_shape, in_specs=in_specs, out_specs=...]
where the time goes in v5:
time: 55.3 us; the launch traced here: 55.1 us
  starting transfers between devices  25.5 us (46%)
  waiting for transfers between devices  23.3 us (42%)
  Pallas kernels  4.34 us (8%)
  local copies, waits for them, and re-layouts  1.07 us (2%)
  between operations  0.77 us (1%)
    ppermute x2, starting transfers between devices, on_device(): arrived.append(lax.ppermute(part, ('dom', 'rep'), moves))  5.49 us
    ppermute x3, waiting for transfers between devices, on_device(): pieces[mask] = lax.ppermute(pieces[0], 'dom', xor_pairs(dom_size, mask))  5.33 us
    ppermute x3, waiting for transfers between devices, on_device(): parts.append(lax.ppermute(partials[mask], 'rep', xor_pairs(rep_size, mask)))  5.25 us
    ppermute x2, waiting for transfers between devices, exchange_sum(): third = lax.ppermute(value, axis, xor_pairs(size, now[0] ^ now[1]))  4.82 us
    ppermute x3, starting transfers between devices, on_device(): parts.append(lax.ppermute(partials[mask], 'rep', xor_pairs(rep_size, mask)))  4.45 us
    pallas_call x6, Pallas kernels, local_call(): pl.pallas_call(kernel, out_shape=out_shape, in_specs=in_specs, out_specs=...  4.34 us
    ppermute x3, starting transfers between devices, on_device(): pieces[mask] = lax.ppermute(pieces[0], 'dom', xor_pairs(dom_size, mask))  4.24 us
    ppermute x2, waiting for transfers between devices, exchange_sum(): second = lax.ppermute(value, axis, xor_pairs(size, now[1]))  3.7 us
  transfers between devices with their start and end apart: 21, of which 13 were waited for; matrix products, arithmetic and copies ran while one was open for 0% of the time, Pallas kernels for 1%

profile of v5, /device:TPU:0, one launch (start us, length us, event | category | flops | bytes accessed | tf_op | source)
XLA Modules:
  0.0 55.1 jit_solution(10431607308964367372)
XLA Ops:
  0.6 1.7 %scale.1 = (bf16[256,128]{1,0:T(8,128)(2,1)}, bf16[256,128]{1,0:T(8,128)(2,1)}) custom-call(bf16[256,256]{1,0:T(8,128)(2,1)} %refs_0_.3, s32[1,256]{1,0:T(1,128)} %bitcast.3), custom_call_target="tpu_custom_call" | custom-call | tf_op jit(solution)/shard_map/scale/pallas_call | solution.py:37
  2.3 3.9 %collective-permute-start.1 = (bf16[256,128]{1,0:T(8,128)(2,1)}, bf16[256,128]{1,0:T(8,128)(2,1)S(1)}, u32[]{:S(2)}, u32[]{:S(2)}) collective-permute-start(bf16[256,128]{1,0:T(8,128)(2,1)} %get-tuple-element.20), channel_id=1, source_target_pairs={{0,24},{1,8},{2,16},{3,0},{4,28},{5,12},{6,20},{7,4},{8,1},{9,17},... | collective-permute-start | bytes 196616 | tf_op jit(solution)/shard_map/ppermute | solution.py:248
  6.3 1.5 %collective-permute-start.2 = (bf16[256,128]{1,0:T(8,128)(2,1)}, bf16[256,128]{1,0:T(8,128)(2,1)S(1)}, u32[]{:S(2)}, u32[]{:S(2)}) collective-permute-start(bf16[256,128]{1,0:T(8,128)(2,1)} %get-tuple-element.21), channel_id=1, source_target_pairs={{0,9},{1,25},{2,17},{3,1},{4,13},{5,29},{6,21},{7,5},{8,16},{9,0},... | collective-permute-start | bytes 196616 | tf_op jit(solution)/shard_map/ppermute | solution.py:248
  7.9 1.0 %copy-done = s32[1,2,4,128,128]{4,3,2,1,0:T(8,128)S(1)} copy-done((s32[1,2,4,128,128]{4,3,2,1,0:T(8,128)S(1)}, s32[1,2,4,128,128]{4,3,2,1,0:T(8,128)}, u32[]{:S(2)}) %copy-start) | copy-done | bytes 524312
  8.9 0.8 %prepare.1 = (bf16[1040,128]{1,0:T(8,128)(2,1)S(1)}, bf16[256,256]{1,0:T(8,128)(2,1)S(1)}, f32[256,128]{1,0:T(8,128)S(1)}, f32[1,256]{1,0:T(1,128)S(1)}) custom-call(s32[1,2,4,128,128]{4,3,2,1,0:T(8,128)S(1)} %copy-done, s32[1,2,4]{2,1,0:T(2,128)S(1)} %copy-done.5, s32[1,2,4]{2,1,0:T(2,128)S(1)} %copy-done.6, bf16[256,256]{1,0:T(8,128)(2,1)S(1)} %copy-done.1, ...), custom_call_target="tpu_custom_call" | custom-call | tf_op jit(solution)/shard_map/prepare/pallas_call | solution.py:37
  9.7 2.6 %collective-permute-start = (bf16[1040,128]{1,0:T(8,128)(2,1)S(1)}, bf16[1040,128]{1,0:T(8,128)(2,1)S(1)}, u32[]{:S(2)}, u32[]{:S(2)}) collective-permute-start(bf16[1040,128]{1,0:T(8,128)(2,1)S(1)} %get-tuple-element.19.refs_0_), channel_id=1, source_target_pairs={{0,1},{1,0},{2,3},{3,2},{4,5},{5,4},{6,7},{7,6},{8,9},{9,8},{10,11... | collective-permute-start | bytes 798728 | tf_op jit(solution)/shard_map/ppermute | solution.py:261
  12.3 0.6 %collective-permute-done.2.second_ref = bf16[256,128]{1,0:T(8,128)(2,1)S(1)} collective-permute-done((bf16[256,128]{1,0:T(8,128)(2,1)}, bf16[256,128]{1,0:T(8,128)(2,1)S(1)}, u32[]{:S(2)}, u32[]{:S(2)}) %collective-permute-start.2) | collective-permute-done | bytes 65568 | tf_op jit(solution)/shard_map/ppermute | solution.py:248
  13.0 3.6 %collective-permute-start.8 = (bf16[512,128]{1,0:T(8,128)(2,1)S(1)}, bf16[512,128]{1,0:T(8,128)(2,1)S(1)}, u32[]{:S(2)}, u32[]{:S(2)}) collective-permute-start(bf16[512,128]{1,0:T(8,128)(2,1)S(1)} %join.1.refs_2_), channel_id=1, source_target_pairs={{0,24},{4,28},{8,16},{12,20},{16,8},{20,12},{24,0},{28,4},{1,25},{... | collective-permute-start | bytes 393224 | tf_op jit(solution)/shard_map/ppermute | solution.py:269
  16.6 0.6 %collective-permute-start.4 = (bf16[512,128]{1,0:T(8,128)(2,1)S(1)}, bf16[512,128]{1,0:T(8,128)(2,1)S(1)}, u32[]{:S(2)}, u32[]{:S(2)}) collective-permute-start(bf16[512,128]{1,0:T(8,128)(2,1)S(1)} %join.1.refs_2_), channel_id=1, source_target_pairs={{0,8},{4,12},{8,0},{12,4},{16,24},{20,28},{24,16},{28,20},{1,9},{5... | collective-permute-start | bytes 393224 | tf_op jit(solution)/shard_map/ppermute | solution.py:269
  17.2 3.2 %collective-permute-done.8.refs_8_ = bf16[512,128]{1,0:T(8,128)(2,1)S(1)} collective-permute-done((bf16[512,128]{1,0:T(8,128)(2,1)S(1)}, bf16[512,128]{1,0:T(8,128)(2,1)S(1)}, u32[]{:S(2)}, u32[]{:S(2)}) %collective-permute-start.8) | collective-permute-done | bytes 131104 | tf_op jit(solution)/shard_map/ppermute | solution.py:269
  20.4 2.1 %collective-permute-done.6.refs_6_ = bf16[512,128]{1,0:T(8,128)(2,1)S(1)} collective-permute-done((bf16[512,128]{1,0:T(8,128)(2,1)S(1)}, bf16[512,128]{1,0:T(8,128)(2,1)S(1)}, u32[]{:S(2)}, u32[]{:S(2)}) %collective-permute-start.6) | collective-permute-done | bytes 131104 | tf_op jit(solution)/shard_map/ppermute | solution.py:269
  22.5 0.5 collective-permute-start.5
  23.1 0.8 %collective-permute-done.7.refs_7_ = bf16[512,128]{1,0:T(8,128)(2,1)S(1)} collective-permute-done((bf16[512,128]{1,0:T(8,128)(2,1)S(1)}, bf16[512,128]{1,0:T(8,128)(2,1)S(1)}, u32[]{:S(2)}, u32[]{:S(2)}) %collective-permute-start.7) | collective-permute-done | bytes 131104 | tf_op jit(solution)/shard_map/ppermute | solution.py:271
  24.1 0.6 %aggregate.1 = (bf16[256,128]{1,0:T(8,128)(2,1)S(1)}, bf16[256,128]{1,0:T(8,128)(2,1)S(1)}, bf16[256,128]{1,0:T(8,128)(2,1)S(1)}, bf16[256,128]{1,0:T(8,128)(2,1)S(1)}) custom-call(bf16[1040,128]{1,0:T(8,128)(2,1)S(1)} %get-tuple-element.19.refs_0_, bf16[1040,128]{1,0:T(8,128)(2,1)S(1)} %collective-permute-done.refs_1_, bf16[512,128]{1,0:T(8,128)(2,1)S(1)} %join.1.refs_2_, ...), custom_call_target="tpu_custom_call" | custom-call | tf_op jit(solution)/shard_map/aggregate/pallas_call | solution.py:37
  24.6 1.1 %collective-permute-start.10 = (bf16[256,128]{1,0:T(8,128)(2,1)S(1)}, bf16[256,128]{1,0:T(8,128)(2,1)S(1)}, u32[]{:S(2)}, u32[]{:S(2)}) collective-permute-start(bf16[256,128]{1,0:T(8,128)(2,1)S(1)} %get-tuple-element.23), channel_id=1, source_target_pairs={{0,1},{1,0},{2,3},{3,2},{4,5},{5,4},{6,7},{7,6},{8,9},{9,8},{10,11... | collective-permute-start | bytes 196616 | tf_op jit(solution)/shard_map/ppermute | solution.py:285
  25.7 2.5 %collective-permute-start.11 = (bf16[256,128]{1,0:T(8,128)(2,1)S(1)}, bf16[256,128]{1,0:T(8,128)(2,1)S(1)}, u32[]{:S(2)}, u32[]{:S(2)}) collective-permute-start(bf16[256,128]{1,0:T(8,128)(2,1)S(1)} %get-tuple-element.24), channel_id=1, source_target_pairs={{0,2},{1,3},{2,0},{3,1},{4,6},{5,7},{6,4},{7,5},{8,10},{9,11},{10,... | collective-permute-start | bytes 196616 | tf_op jit(solution)/shard_map/ppermute | solution.py:285
  28.2 0.9 %collective-permute-start.12 = (bf16[256,128]{1,0:T(8,128)(2,1)S(1)}, bf16[256,128]{1,0:T(8,128)(2,1)S(1)}, u32[]{:S(2)}, u32[]{:S(2)}) collective-permute-start(bf16[256,128]{1,0:T(8,128)(2,1)S(1)} %get-tuple-element.25), channel_id=1, source_target_pairs={{0,3},{1,2},{2,1},{3,0},{4,7},{5,6},{6,5},{7,4},{8,11},{9,10},{10,... | collective-permute-start | bytes 196616 | tf_op jit(solution)/shard_map/ppermute | solution.py:285
  29.1 4.2 %collective-permute-done.11.refs_2_ = bf16[256,128]{1,0:T(8,128)(2,1)S(1)} collective-permute-done((bf16[256,128]{1,0:T(8,128)(2,1)S(1)}, bf16[256,128]{1,0:T(8,128)(2,1)S(1)}, u32[]{:S(2)}, u32[]{:S(2)}) %collective-permute-start.11) | collective-permute-done | bytes 65568 | tf_op jit(solution)/shard_map/ppermute | solution.py:285
  33.3 1.0 %collective-permute-done.12.refs_3_ = bf16[256,128]{1,0:T(8,128)(2,1)S(1)} collective-permute-done((bf16[256,128]{1,0:T(8,128)(2,1)S(1)}, bf16[256,128]{1,0:T(8,128)(2,1)S(1)}, u32[]{:S(2)}, u32[]{:S(2)}) %collective-permute-start.12) | collective-permute-done | bytes 65568 | tf_op jit(solution)/shard_map/ppermute | solution.py:285
  34.3 0.5 dense.1
  35.0 1.4 %collective-permute-done.13 = f32[144,256]{1,0:T(8,128)S(1)} collective-permute-done((f32[144,256]{1,0:T(8,128)S(1)}, f32[144,256]{1,0:T(8,128)S(1)}, u32[]{:S(2)}, u32[]{:S(2)}) %collective-permute-start.13) | collective-permute-done | bytes 147488 | tf_op jit(solution)/shard_map/ppermute | solution.py:296
  36.4 1.2 %collective-permute-start.16 = (bf16[144,256]{1,0:T(8,128)(2,1)S(1)}, bf16[144,256]{1,0:T(8,128)(2,1)S(1)}, u32[]{:S(2)}, u32[]{:S(2)}) collective-permute-start(bf16[144,256]{1,0:T(8,128)(2,1)S(1)} %add_convert_fusion.2), channel_id=1, source_target_pairs={{0,24},{4,28},{8,16},{12,20},{16,8},{20,12},{24,0},{28,4},{1,25},{... | collective-permute-start | bytes 221192 | tf_op jit(solution)/shard_map/ppermute | solution.py:214
  37.6 1.0 %collective-permute-start.15 = (bf16[144,256]{1,0:T(8,128)(2,1)S(1)}, bf16[144,256]{1,0:T(8,128)(2,1)S(1)}, u32[]{:S(2)}, u32[]{:S(2)}) collective-permute-start(bf16[144,256]{1,0:T(8,128)(2,1)S(1)} %add_convert_fusion.2), channel_id=1, source_target_pairs={{0,16},{4,20},{8,24},{12,28},{16,0},{20,4},{24,8},{28,12},{1,17},{... | collective-permute-start | bytes 221192 | tf_op jit(solution)/shard_map/ppermute | solution.py:213
  38.5 1.4 %collective-permute-start.14 = (bf16[144,256]{1,0:T(8,128)(2,1)S(1)}, bf16[144,256]{1,0:T(8,128)(2,1)S(1)}, u32[]{:S(2)}, u32[]{:S(2)}) collective-permute-start(bf16[144,256]{1,0:T(8,128)(2,1)S(1)} %add_convert_fusion.2), channel_id=1, source_target_pairs={{0,8},{4,12},{8,0},{12,4},{16,24},{20,28},{24,16},{28,20},{1,9},{5... | collective-permute-start | bytes 221192 | tf_op jit(solution)/shard_map/ppermute | solution.py:209
  39.9 2.2 %collective-permute-done.16 = bf16[144,256]{1,0:T(8,128)(2,1)S(1)} collective-permute-done((bf16[144,256]{1,0:T(8,128)(2,1)S(1)}, bf16[144,256]{1,0:T(8,128)(2,1)S(1)}, u32[]{:S(2)}, u32[]{:S(2)}) %collective-permute-start.16) | collective-permute-done | bytes 73760 | tf_op jit(solution)/shard_map/ppermute | solution.py:214
  42.1 1.1 %collective-permute-done.15 = bf16[144,256]{1,0:T(8,128)(2,1)S(1)} collective-permute-done((bf16[144,256]{1,0:T(8,128)(2,1)S(1)}, bf16[144,256]{1,0:T(8,128)(2,1)S(1)}, u32[]{:S(2)}, u32[]{:S(2)}) %collective-permute-start.15) | collective-permute-done | bytes 73760 | tf_op jit(solution)/shard_map/ppermute | solution.py:213
  43.2 2.2 %collective-permute-start.19 = (bf16[144,256]{1,0:T(8,128)(2,1)S(1)}, bf16[144,256]{1,0:T(8,128)(2,1)S(1)}, u32[]{:S(2)}, u32[]{:S(2)}) collective-permute-start(bf16[144,256]{1,0:T(8,128)(2,1)S(1)} %add_convert_fusion.1), channel_id=1, source_target_pairs={{0,3},{1,2},{2,1},{3,0},{4,7},{5,6},{6,5},{7,4},{8,11},{9,10},{10,... | collective-permute-start | bytes 221192 | tf_op jit(solution)/shard_map/ppermute | solution.py:214
  45.9 1.8 %collective-permute-start.17 = (bf16[144,256]{1,0:T(8,128)(2,1)S(1)}, bf16[144,256]{1,0:T(8,128)(2,1)S(1)}, u32[]{:S(2)}, u32[]{:S(2)}) collective-permute-start(bf16[144,256]{1,0:T(8,128)(2,1)S(1)} %add_convert_fusion.1), channel_id=1, source_target_pairs={{0,1},{1,0},{2,3},{3,2},{4,5},{5,4},{6,7},{7,6},{8,9},{9,8},{10,11... | collective-permute-start | bytes 221192 | tf_op jit(solution)/shard_map/ppermute | solution.py:209
  47.7 2.6 %collective-permute-done.19 = bf16[144,256]{1,0:T(8,128)(2,1)S(1)} collective-permute-done((bf16[144,256]{1,0:T(8,128)(2,1)S(1)}, bf16[144,256]{1,0:T(8,128)(2,1)S(1)}, u32[]{:S(2)}, u32[]{:S(2)}) %collective-permute-start.19) | collective-permute-done | bytes 73760 | tf_op jit(solution)/shard_map/ppermute | solution.py:214
  50.3 2.6 %collective-permute-done.18 = bf16[144,256]{1,0:T(8,128)(2,1)S(1)} collective-permute-done((bf16[144,256]{1,0:T(8,128)(2,1)S(1)}, bf16[144,256]{1,0:T(8,128)(2,1)S(1)}, u32[]{:S(2)}, u32[]{:S(2)}) %collective-permute-start.18) | collective-permute-done | bytes 73760 | tf_op jit(solution)/shard_map/ppermute | solution.py:213
  53.1 1.3 %collective-permute-done.20.other_ref = bf16[144,256]{1,0:T(8,128)(2,1)S(1)} collective-permute-done((bf16[144,256]{1,0:T(8,128)(2,1)S(1)}, bf16[144,256]{1,0:T(8,128)(2,1)S(1)}, u32[]{:S(2)}, u32[]{:S(2)}) %collective-permute-start.20) | collective-permute-done | bytes 73760 | tf_op jit(solution)/shard_map/ppermute | solution.py:299
  54.3 0.8 %finish.1 = (f32[256,256]{1,0:T(8,128)}, f32[1,256]{1,0:T(1,128)}, bf16[256,256]{1,0:T(8,128)(2,1)}) custom-call(bf16[144,256]{1,0:T(8,128)(2,1)S(1)} %add_convert_fusion.mine_ref, bf16[144,256]{1,0:T(8,128)(2,1)S(1)} %collective-permute-done.20.other_ref, bf16[256,256]{1,0:T(8,128)(2,1)S(1)} %get-tuple-element.31.outcome_ref), custom_call_target="tpu_custom_call" | custom-call | tf_op jit(solution)/shard_map/finish/pallas_call | solution.py:37
  (35 shorter events, 0.9 us)
Async XLA Ops:
  0.6 7.2 %copy-start.1 = (bf16[256,256]{1,0:T(8,128)(2,1)S(1)}, bf16[256,256]{1,0:T(8,128)(2,1)}, u32[]{:S(2)}) copy-start(bf16[256,256]{1,0:T(8,128)(2,1)} %refs_0_.3) | copy-start | bytes 393220
  2.3 5.5 %copy-start.7 = (f32[256]{0:T(256)S(1)}, f32[256]{0:T(256)}, u32[]{:S(2)}) copy-start(f32[256]{0:T(256)} %param.15) | copy-start | bytes 3076
  2.3 10.0 %collective-permute-start.1 = (bf16[256,128]{1,0:T(8,128)(2,1)}, bf16[256,128]{1,0:T(8,128)(2,1)S(1)}, u32[]{:S(2)}, u32[]{:S(2)}) collective-permute-start(bf16[256,128]{1,0:T(8,128)(2,1)} %get-tuple-element.20), channel_id=1, source_target_pairs={{0,24},{1,8},{2,16},{3,0},{4,28},{5,12},{6,20},{7,4},{8,1},{9,17},... | collective-permute-start | bytes 196616 | tf_op jit(solution)/shard_map/ppermute | solution.py:248
  6.3 1.6 %copy-start.5 = (s32[1,2,4]{2,1,0:T(2,128)S(1)}, s32[1,2,4]{2,1,0:T(2,128)}, u32[]{:S(2)}) copy-start(s32[1,2,4]{2,1,0:T(2,128)} %refs_1_.1) | copy-start | bytes 100
  6.3 1.6 %copy-start.6 = (s32[1,2,4]{2,1,0:T(2,128)S(1)}, s32[1,2,4]{2,1,0:T(2,128)}, u32[]{:S(2)}) copy-start(s32[1,2,4]{2,1,0:T(2,128)} %refs_2_.1) | copy-start | bytes 100
  6.3 1.6 %copy-start.4 = (s32[256]{0:T(256)S(1)}, s32[256]{0:T(256)}, u32[]{:S(2)}) copy-start(s32[256]{0:T(256)} %param.10) | copy-start | bytes 3076
  6.3 6.6 %collective-permute-start.2 = (bf16[256,128]{1,0:T(8,128)(2,1)}, bf16[256,128]{1,0:T(8,128)(2,1)S(1)}, u32[]{:S(2)}, u32[]{:S(2)}) collective-permute-start(bf16[256,128]{1,0:T(8,128)(2,1)} %get-tuple-element.21), channel_id=1, source_target_pairs={{0,9},{1,25},{2,17},{3,1},{4,13},{5,29},{6,21},{7,5},{8,16},{9,0},... | collective-permute-start | bytes 196616 | tf_op jit(solution)/shard_map/ppermute | solution.py:248
  7.9 1.0 %copy-start = (s32[1,2,4,128,128]{4,3,2,1,0:T(8,128)S(1)}, s32[1,2,4,128,128]{4,3,2,1,0:T(8,128)}, u32[]{:S(2)}) copy-start(s32[1,2,4,128,128]{4,3,2,1,0:T(8,128)} %refs_0_.2) | copy-start | bytes 1572868
  9.7 13.4 %collective-permute-start = (bf16[1040,128]{1,0:T(8,128)(2,1)S(1)}, bf16[1040,128]{1,0:T(8,128)(2,1)S(1)}, u32[]{:S(2)}, u32[]{:S(2)}) collective-permute-start(bf16[1040,128]{1,0:T(8,128)(2,1)S(1)} %get-tuple-element.19.refs_0_), channel_id=1, source_target_pairs={{0,1},{1,0},{2,3},{3,2},{4,5},{5,4},{6,7},{7,6},{8,9},{9,8},{10,11... | collective-permute-start | bytes 798728 | tf_op jit(solution)/shard_map/ppermute | solution.py:261
  12.9 21.4 %copy-start.2 = (bf16[256,256]{1,0:T(8,128)(2,1)S(1)}, bf16[256,256]{1,0:T(8,128)(2,1)}, u32[]{:S(2)}) copy-start(bf16[256,256]{1,0:T(8,128)(2,1)} %refs_6_.1) | copy-start | bytes 393220
  12.9 21.4 %copy-start.3 = (bf16[256,256]{1,0:T(8,128)(2,1)S(1)}, bf16[256,256]{1,0:T(8,128)(2,1)}, u32[]{:S(2)}) copy-start(bf16[256,256]{1,0:T(8,128)(2,1)} %refs_8_.1) | copy-start | bytes 393220
  13.0 7.5 %collective-permute-start.8 = (bf16[512,128]{1,0:T(8,128)(2,1)S(1)}, bf16[512,128]{1,0:T(8,128)(2,1)S(1)}, u32[]{:S(2)}, u32[]{:S(2)}) collective-permute-start(bf16[512,128]{1,0:T(8,128)(2,1)S(1)} %join.1.refs_2_), channel_id=1, source_target_pairs={{0,24},{4,28},{8,16},{12,20},{16,8},{20,12},{24,0},{28,4},{1,25},{... | collective-permute-start | bytes 393224 | tf_op jit(solution)/shard_map/ppermute | solution.py:269
  16.5 6.0 %collective-permute-start.6 = (bf16[512,128]{1,0:T(8,128)(2,1)S(1)}, bf16[512,128]{1,0:T(8,128)(2,1)S(1)}, u32[]{:S(2)}, u32[]{:S(2)}) collective-permute-start(bf16[512,128]{1,0:T(8,128)(2,1)S(1)} %join.1.refs_2_), channel_id=1, source_target_pairs={{0,16},{4,20},{8,24},{12,28},{16,0},{20,4},{24,8},{28,12},{1,17},{... | collective-permute-start | bytes 393224 | tf_op jit(solution)/shard_map/ppermute | solution.py:269
  16.6 6.0 %collective-permute-start.4 = (bf16[512,128]{1,0:T(8,128)(2,1)S(1)}, bf16[512,128]{1,0:T(8,128)(2,1)S(1)}, u32[]{:S(2)}, u32[]{:S(2)}) collective-permute-start(bf16[512,128]{1,0:T(8,128)(2,1)S(1)} %join.1.refs_2_), channel_id=1, source_target_pairs={{0,8},{4,12},{8,0},{12,4},{16,24},{20,28},{24,16},{28,20},{1,9},{5... | collective-permute-start | bytes 393224 | tf_op jit(solution)/shard_map/ppermute | solution.py:269
  17.2 5.9 %collective-permute-start.3 = (bf16[512,128]{1,0:T(8,128)(2,1)S(1)}, bf16[512,128]{1,0:T(8,128)(2,1)S(1)}, u32[]{:S(2)}, u32[]{:S(2)}) collective-permute-start(bf16[512,128]{1,0:T(8,128)(2,1)S(1)} %join.1.refs_2_), channel_id=1, source_target_pairs={{0,4},{4,0},{8,12},{12,8},{16,20},{20,16},{24,28},{28,24},{1,5},{5... | collective-permute-start | bytes 393224 | tf_op jit(solution)/shard_map/ppermute | solution.py:271
  20.4 2.6 %collective-permute-start.9 = (bf16[512,128]{1,0:T(8,128)(2,1)S(1)}, bf16[512,128]{1,0:T(8,128)(2,1)S(1)}, u32[]{:S(2)}, u32[]{:S(2)}) collective-permute-start(bf16[512,128]{1,0:T(8,128)(2,1)S(1)} %collective-permute-done.8.refs_8_), channel_id=1, source_target_pairs={{0,4},{4,0},{8,12},{12,8},{16,20},{20,16},{24,28},{28,24},{1,5},{5... | collective-permute-start | bytes 393224 | tf_op jit(solution)/shard_map/ppermute | solution.py:271
  22.5 1.3 %collective-permute-start.7 = (bf16[512,128]{1,0:T(8,128)(2,1)S(1)}, bf16[512,128]{1,0:T(8,128)(2,1)S(1)}, u32[]{:S(2)}, u32[]{:S(2)}) collective-permute-start(bf16[512,128]{1,0:T(8,128)(2,1)S(1)} %collective-permute-done.6.refs_6_), channel_id=1, source_target_pairs={{0,4},{4,0},{8,12},{12,8},{16,20},{20,16},{24,28},{28,24},{1,5},{5... | collective-permute-start | bytes 393224 | tf_op jit(solution)/shard_map/ppermute | solution.py:271
  22.5 1.5 %collective-permute-start.5 = (bf16[512,128]{1,0:T(8,128)(2,1)S(1)}, bf16[512,128]{1,0:T(8,128)(2,1)S(1)}, u32[]{:S(2)}, u32[]{:S(2)}) collective-permute-start(bf16[512,128]{1,0:T(8,128)(2,1)S(1)} %collective-permute-done.4.refs_4_), channel_id=1, source_target_pairs={{0,4},{4,0},{8,12},{12,8},{16,20},{20,16},{24,28},{28,24},{1,5},{5... | collective-permute-start | bytes 393224 | tf_op jit(solution)/shard_map/ppermute | solution.py:271
  24.6 4.5 %collective-permute-start.10 = (bf16[256,128]{1,0:T(8,128)(2,1)S(1)}, bf16[256,128]{1,0:T(8,128)(2,1)S(1)}, u32[]{:S(2)}, u32[]{:S(2)}) collective-permute-start(bf16[256,128]{1,0:T(8,128)(2,1)S(1)} %get-tuple-element.23), channel_id=1, source_target_pairs={{0,1},{1,0},{2,3},{3,2},{4,5},{5,4},{6,7},{7,6},{8,9},{9,8},{10,11... | collective-permute-start | bytes 196616 | tf_op jit(solution)/shard_map/ppermute | solution.py:285
  25.7 7.6 %collective-permute-start.11 = (bf16[256,128]{1,0:T(8,128)(2,1)S(1)}, bf16[256,128]{1,0:T(8,128)(2,1)S(1)}, u32[]{:S(2)}, u32[]{:S(2)}) collective-permute-start(bf16[256,128]{1,0:T(8,128)(2,1)S(1)} %get-tuple-element.24), channel_id=1, source_target_pairs={{0,2},{1,3},{2,0},{3,1},{4,6},{5,7},{6,4},{7,5},{8,10},{9,11},{10,... | collective-permute-start | bytes 196616 | tf_op jit(solution)/shard_map/ppermute | solution.py:285
  28.2 6.1 %collective-permute-start.12 = (bf16[256,128]{1,0:T(8,128)(2,1)S(1)}, bf16[256,128]{1,0:T(8,128)(2,1)S(1)}, u32[]{:S(2)}, u32[]{:S(2)}) collective-permute-start(bf16[256,128]{1,0:T(8,128)(2,1)S(1)} %get-tuple-element.25), channel_id=1, source_target_pairs={{0,3},{1,2},{2,1},{3,0},{4,7},{5,6},{6,5},{7,4},{8,11},{9,10},{10,... | collective-permute-start | bytes 196616 | tf_op jit(solution)/shard_map/ppermute | solution.py:285
  34.9 1.4 %collective-permute-start.13 = (f32[144,256]{1,0:T(8,128)S(1)}, f32[144,256]{1,0:T(8,128)S(1)}, u32[]{:S(2)}, u32[]{:S(2)}) collective-permute-start(f32[144,256]{1,0:T(8,128)S(1)} %get-tuple-element.30), channel_id=1, source_target_pairs={{0,4},{4,0},{8,12},{12,8},{16,20},{20,16},{24,28},{28,24},{1,5},{5... | collective-permute-start | bytes 442376 | tf_op jit(solution)/shard_map/ppermute | solution.py:296
  36.4 5.8 %collective-permute-start.16 = (bf16[144,256]{1,0:T(8,128)(2,1)S(1)}, bf16[144,256]{1,0:T(8,128)(2,1)S(1)}, u32[]{:S(2)}, u32[]{:S(2)}) collective-permute-start(bf16[144,256]{1,0:T(8,128)(2,1)S(1)} %add_convert_fusion.2), channel_id=1, source_target_pairs={{0,24},{4,28},{8,16},{12,20},{16,8},{20,12},{24,0},{28,4},{1,25},{... | collective-permute-start | bytes 221192 | tf_op jit(solution)/shard_map/ppermute | solution.py:214
  37.6 5.6 %collective-permute-start.15 = (bf16[144,256]{1,0:T(8,128)(2,1)S(1)}, bf16[144,256]{1,0:T(8,128)(2,1)S(1)}, u32[]{:S(2)}, u32[]{:S(2)}) collective-permute-start(bf16[144,256]{1,0:T(8,128)(2,1)S(1)} %add_convert_fusion.2), channel_id=1, source_target_pairs={{0,16},{4,20},{8,24},{12,28},{16,0},{20,4},{24,8},{28,12},{1,17},{... | collective-permute-start | bytes 221192 | tf_op jit(solution)/shard_map/ppermute | solution.py:213
  38.5 4.7 %collective-permute-start.14 = (bf16[144,256]{1,0:T(8,128)(2,1)S(1)}, bf16[144,256]{1,0:T(8,128)(2,1)S(1)}, u32[]{:S(2)}, u32[]{:S(2)}) collective-permute-start(bf16[144,256]{1,0:T(8,128)(2,1)S(1)} %add_convert_fusion.2), channel_id=1, source_target_pairs={{0,8},{4,12},{8,0},{12,4},{16,24},{20,28},{24,16},{28,20},{1,9},{5... | collective-permute-start | bytes 221192 | tf_op jit(solution)/shard_map/ppermute | solution.py:209
  43.2 7.0 %collective-permute-start.19 = (bf16[144,256]{1,0:T(8,128)(2,1)S(1)}, bf16[144,256]{1,0:T(8,128)(2,1)S(1)}, u32[]{:S(2)}, u32[]{:S(2)}) collective-permute-start(bf16[144,256]{1,0:T(8,128)(2,1)S(1)} %add_convert_fusion.1), channel_id=1, source_target_pairs={{0,3},{1,2},{2,1},{3,0},{4,7},{5,6},{6,5},{7,4},{8,11},{9,10},{10,... | collective-permute-start | bytes 221192 | tf_op jit(solution)/shard_map/ppermute | solution.py:214
  45.5 7.5 %collective-permute-start.18 = (bf16[144,256]{1,0:T(8,128)(2,1)S(1)}, bf16[144,256]{1,0:T(8,128)(2,1)S(1)}, u32[]{:S(2)}, u32[]{:S(2)}) collective-permute-start(bf16[144,256]{1,0:T(8,128)(2,1)S(1)} %add_convert_fusion.1), channel_id=1, source_target_pairs={{0,2},{1,3},{2,0},{3,1},{4,6},{5,7},{6,4},{7,5},{8,10},{9,11},{10,... | collective-permute-start | bytes 221192 | tf_op jit(solution)/shard_map/ppermute | solution.py:213
  45.9 7.1 %collective-permute-start.17 = (bf16[144,256]{1,0:T(8,128)(2,1)S(1)}, bf16[144,256]{1,0:T(8,128)(2,1)S(1)}, u32[]{:S(2)}, u32[]{:S(2)}) collective-permute-start(bf16[144,256]{1,0:T(8,128)(2,1)S(1)} %add_convert_fusion.1), channel_id=1, source_target_pairs={{0,1},{1,0},{2,3},{3,2},{4,5},{5,4},{6,7},{7,6},{8,9},{9,8},{10,11... | collective-permute-start | bytes 221192 | tf_op jit(solution)/shard_map/ppermute | solution.py:209
  53.0 1.3 %collective-permute-start.20 = (bf16[144,256]{1,0:T(8,128)(2,1)S(1)}, bf16[144,256]{1,0:T(8,128)(2,1)S(1)}, u32[]{:S(2)}, u32[]{:S(2)}) collective-permute-start(bf16[144,256]{1,0:T(8,128)(2,1)S(1)} %add_convert_fusion.mine_ref), channel_id=1, source_target_pairs={{0,4},{4,0},{8,12},{12,8},{16,20},{20,16},{24,28},{28,24},{1,5},{5... | collective-permute-start | bytes 221192 | tf_op jit(solution)/shard_map/ppermute | solution.py:299

commit v6 on v5

--- a/solution.py
+++ b/solution.py
@@ -120,7 +120,7 @@
 
     def add_slot(which, at, code):
         row, col = code // block_count, code % block_count
-        chip = chip_of(rep ^ which, rep, col // per_slice, rep_size)
+        chip = chip_of(rep ^ (which * (rep_size - 1)), rep, col // per_slice, rep_size)
         mask = (chip * sections + at // slots) ^ dom
         rows = held[mask * per_piece + which * per_slice + col % per_slice]
         tile = tile_refs[which][pl.ds(at * block, block), :]
@@ -243,8 +243,8 @@
         for dom in range(dom_size):
             plane = dom // sections
             for rep in range(rep_size):
-                target = chip_of(plane, plane ^ flip, rep, rep_size) * sections + dom % sections
-                moves.append((dom * rep_size + rep, target * rep_size + (plane ^ flip)))
+                target = chip_of(plane, plane ^ (flip * (rep_size - 1)), rep, rep_size) * sections + dom % sections
+                moves.append((dom * rep_size + rep, target * rep_size + (plane ^ (flip * (rep_size - 1)))))
         arrived.append(lax.ppermute(part, ("dom", "rep"), moves))
 
     tiles, scaled, inv_root, bias_row = local_call(
@@ -258,7 +258,7 @@
             jax.ShapeDtypeStruct((1, width), f32),
         ),
     )
-    their_tiles = lax.ppermute(tiles, "rep", xor_pairs(rep_size, 1))
+    their_tiles = lax.ppermute(tiles, "rep", xor_pairs(rep_size, rep_size - 1))
 
     pieces = [None] * dom_size
     pieces[0] = local_call(

time: 55.3 us -> 53.6 us (0.969)
  waiting for transfers between devices: 23.3 us -> 22.3 us
  starting transfers between devices: 25.5 us -> 24.9 us
    ppermute x2, starting transfers between devices: 3.45 us -> 4.33 us  [exchange_sum(): third = lax.ppermute(value, axis, xor_pairs(size, now[0] ^ now[1]))]
    ppermute x2, waiting for transfers between devices: 4.82 us -> 3.94 us  [exchange_sum(): third = lax.ppermute(value, axis, xor_pairs(size, now[0] ^ now[1]))]
    ppermute x3, waiting for transfers between devices: 5.33 us -> 4.55 us  [on_device(): pieces[mask] = lax.ppermute(pieces[0], 'dom', xor_pairs(dom_size, mask))]
    ppermute x2, waiting for transfers between devices: 3.7 us -> 4.37 us  [exchange_sum(): second = lax.ppermute(value, axis, xor_pairs(size, now[1]))]
    ppermute x3, starting transfers between devices: 4.24 us -> 3.66 us  [on_device(): pieces[mask] = lax.ppermute(pieces[0], 'dom', xor_pairs(dom_size, mask))]
  transfers between devices with their start and end apart: 21 -> 21, of which waited for: 13 -> 13; matrix products, arithmetic and copies ran while one was open for 0% -> 0% of each run, Pallas kernels for 1% -> 2%
where the time goes in v6:
time: 53.6 us; the launch traced here: 53.4 us
  starting transfers between devices  24.9 us (46%)
  waiting for transfers between devices  22.3 us (42%)
  Pallas kernels  4.34 us (8%)
  local copies, waits for them, and re-layouts  1.07 us (2%)
  between operations  0.77 us (1%)
    ppermute x2, starting transfers between devices, on_device(): arrived.append(lax.ppermute(part, ('dom', 'rep'), moves))  5.2 us
    ppermute x3, waiting for transfers between devices, on_device(): parts.append(lax.ppermute(partials[mask], 'rep', xor_pairs(rep_size, mask)))  4.78 us
    ppermute x3, waiting for transfers between devices, on_device(): pieces[mask] = lax.ppermute(pieces[0], 'dom', xor_pairs(dom_size, mask))  4.55 us
    ppermute x3, starting transfers between devices, on_device(): parts.append(lax.ppermute(partials[mask], 'rep', xor_pairs(rep_size, mask)))  4.45 us
    ppermute x2, waiting for transfers between devices, exchange_sum(): second = lax.ppermute(value, axis, xor_pairs(size, now[1]))  4.37 us
    pallas_call x6, Pallas kernels, local_call(): pl.pallas_call(kernel, out_shape=out_shape, in_specs=in_specs, out_specs=...  4.34 us
    ppermute x2, starting transfers between devices, exchange_sum(): third = lax.ppermute(value, axis, xor_pairs(size, now[0] ^ now[1]))  4.33 us
    ppermute x2, waiting for transfers between devices, exchange_sum(): third = lax.ppermute(value, axis, xor_pairs(size, now[0] ^ now[1]))  3.94 us
  transfers between devices with their start and end apart: 21, of which 13 were waited for; matrix products, arithmetic and copies ran while one was open for 0% of the time, Pallas kernels for 2%

profile of v6, /device:TPU:0, one launch (start us, length us, event | category | flops | bytes accessed | tf_op | source)
XLA Modules:
  0.0 53.4 jit_solution(1594827120502071371)
XLA Ops:
  0.6 1.7 %scale.1 = (bf16[256,128]{1,0:T(8,128)(2,1)}, bf16[256,128]{1,0:T(8,128)(2,1)}) custom-call(bf16[256,256]{1,0:T(8,128)(2,1)} %refs_0_.3, s32[1,256]{1,0:T(1,128)} %bitcast.3), custom_call_target="tpu_custom_call" | custom-call | tf_op jit(solution)/shard_map/scale/pallas_call | solution.py:37
  2.3 3.9 %collective-permute-start.1 = (bf16[256,128]{1,0:T(8,128)(2,1)}, bf16[256,128]{1,0:T(8,128)(2,1)S(1)}, u32[]{:S(2)}, u32[]{:S(2)}) collective-permute-start(bf16[256,128]{1,0:T(8,128)(2,1)} %get-tuple-element.20), channel_id=1, source_target_pairs={{0,24},{1,8},{2,16},{3,0},{4,28},{5,12},{6,20},{7,4},{8,1},{9,17},... | collective-permute-start | bytes 196616 | tf_op jit(solution)/shard_map/ppermute | solution.py:248
  6.3 1.3 %collective-permute-start.2 = (bf16[256,128]{1,0:T(8,128)(2,1)}, bf16[256,128]{1,0:T(8,128)(2,1)S(1)}, u32[]{:S(2)}, u32[]{:S(2)}) collective-permute-start(bf16[256,128]{1,0:T(8,128)(2,1)} %get-tuple-element.21), channel_id=1, source_target_pairs={{0,3},{1,19},{2,11},{3,27},{4,7},{5,23},{6,15},{7,31},{8,10},{9,2}... | collective-permute-start | bytes 196616 | tf_op jit(solution)/shard_map/ppermute | solution.py:248
  7.6 1.0 %copy-done = s32[1,2,4,128,128]{4,3,2,1,0:T(8,128)S(1)} copy-done((s32[1,2,4,128,128]{4,3,2,1,0:T(8,128)S(1)}, s32[1,2,4,128,128]{4,3,2,1,0:T(8,128)}, u32[]{:S(2)}) %copy-start) | copy-done | bytes 524312
  8.6 0.8 %prepare.1 = (bf16[1040,128]{1,0:T(8,128)(2,1)S(1)}, bf16[256,256]{1,0:T(8,128)(2,1)S(1)}, f32[256,128]{1,0:T(8,128)S(1)}, f32[1,256]{1,0:T(1,128)S(1)}) custom-call(s32[1,2,4,128,128]{4,3,2,1,0:T(8,128)S(1)} %copy-done, s32[1,2,4]{2,1,0:T(2,128)S(1)} %copy-done.5, s32[1,2,4]{2,1,0:T(2,128)S(1)} %copy-done.6, bf16[256,256]{1,0:T(8,128)(2,1)S(1)} %copy-done.1, ...), custom_call_target="tpu_custom_call" | custom-call | tf_op jit(solution)/shard_map/prepare/pallas_call | solution.py:37
  9.4 2.9 %collective-permute-start = (bf16[1040,128]{1,0:T(8,128)(2,1)S(1)}, bf16[1040,128]{1,0:T(8,128)(2,1)S(1)}, u32[]{:S(2)}, u32[]{:S(2)}) collective-permute-start(bf16[1040,128]{1,0:T(8,128)(2,1)S(1)} %get-tuple-element.19.refs_0_), channel_id=1, source_target_pairs={{0,3},{1,2},{2,1},{3,0},{4,7},{5,6},{6,5},{7,4},{8,11},{9,10},{10,... | collective-permute-start | bytes 798728 | tf_op jit(solution)/shard_map/ppermute | solution.py:261
  12.3 1.0 %collective-permute-done.2.second_ref = bf16[256,128]{1,0:T(8,128)(2,1)S(1)} collective-permute-done((bf16[256,128]{1,0:T(8,128)(2,1)}, bf16[256,128]{1,0:T(8,128)(2,1)S(1)}, u32[]{:S(2)}, u32[]{:S(2)}) %collective-permute-start.2) | collective-permute-done | bytes 65568 | tf_op jit(solution)/shard_map/ppermute | solution.py:248
  13.3 3.0 %collective-permute-start.8 = (bf16[512,128]{1,0:T(8,128)(2,1)S(1)}, bf16[512,128]{1,0:T(8,128)(2,1)S(1)}, u32[]{:S(2)}, u32[]{:S(2)}) collective-permute-start(bf16[512,128]{1,0:T(8,128)(2,1)S(1)} %join.1.refs_2_), channel_id=1, source_target_pairs={{0,24},{4,28},{8,16},{12,20},{16,8},{20,12},{24,0},{28,4},{1,25},{... | collective-permute-start | bytes 393224 | tf_op jit(solution)/shard_map/ppermute | solution.py:269
  16.4 0.6 %collective-permute-start.4 = (bf16[512,128]{1,0:T(8,128)(2,1)S(1)}, bf16[512,128]{1,0:T(8,128)(2,1)S(1)}, u32[]{:S(2)}, u32[]{:S(2)}) collective-permute-start(bf16[512,128]{1,0:T(8,128)(2,1)S(1)} %join.1.refs_2_), channel_id=1, source_target_pairs={{0,8},{4,12},{8,0},{12,4},{16,24},{20,28},{24,16},{28,20},{1,9},{5... | collective-permute-start | bytes 393224 | tf_op jit(solution)/shard_map/ppermute | solution.py:269
  17.0 3.4 %collective-permute-done.8.refs_8_ = bf16[512,128]{1,0:T(8,128)(2,1)S(1)} collective-permute-done((bf16[512,128]{1,0:T(8,128)(2,1)S(1)}, bf16[512,128]{1,0:T(8,128)(2,1)S(1)}, u32[]{:S(2)}, u32[]{:S(2)}) %collective-permute-start.8) | collective-permute-done | bytes 131104 | tf_op jit(solution)/shard_map/ppermute | solution.py:269
  20.4 1.2 %collective-permute-done.6.refs_6_ = bf16[512,128]{1,0:T(8,128)(2,1)S(1)} collective-permute-done((bf16[512,128]{1,0:T(8,128)(2,1)S(1)}, bf16[512,128]{1,0:T(8,128)(2,1)S(1)}, u32[]{:S(2)}, u32[]{:S(2)}) %collective-permute-start.6) | collective-permute-done | bytes 131104 | tf_op jit(solution)/shard_map/ppermute | solution.py:269
  21.6 0.5 collective-permute-start.5
  22.1 0.8 %collective-permute-done.7.refs_7_ = bf16[512,128]{1,0:T(8,128)(2,1)S(1)} collective-permute-done((bf16[512,128]{1,0:T(8,128)(2,1)S(1)}, bf16[512,128]{1,0:T(8,128)(2,1)S(1)}, u32[]{:S(2)}, u32[]{:S(2)}) %collective-permute-start.7) | collective-permute-done | bytes 131104 | tf_op jit(solution)/shard_map/ppermute | solution.py:271
  23.1 0.6 %aggregate.1 = (bf16[256,128]{1,0:T(8,128)(2,1)S(1)}, bf16[256,128]{1,0:T(8,128)(2,1)S(1)}, bf16[256,128]{1,0:T(8,128)(2,1)S(1)}, bf16[256,128]{1,0:T(8,128)(2,1)S(1)}) custom-call(bf16[1040,128]{1,0:T(8,128)(2,1)S(1)} %get-tuple-element.19.refs_0_, bf16[1040,128]{1,0:T(8,128)(2,1)S(1)} %collective-permute-done.refs_1_, bf16[512,128]{1,0:T(8,128)(2,1)S(1)} %join.1.refs_2_, ...), custom_call_target="tpu_custom_call" | custom-call | tf_op jit(solution)/shard_map/aggregate/pallas_call | solution.py:37
  23.7 1.6 %collective-permute-start.10 = (bf16[256,128]{1,0:T(8,128)(2,1)S(1)}, bf16[256,128]{1,0:T(8,128)(2,1)S(1)}, u32[]{:S(2)}, u32[]{:S(2)}) collective-permute-start(bf16[256,128]{1,0:T(8,128)(2,1)S(1)} %get-tuple-element.23), channel_id=1, source_target_pairs={{0,1},{1,0},{2,3},{3,2},{4,5},{5,4},{6,7},{7,6},{8,9},{9,8},{10,11... | collective-permute-start | bytes 196616 | tf_op jit(solution)/shard_map/ppermute | solution.py:285
  25.2 1.0 %collective-permute-start.11 = (bf16[256,128]{1,0:T(8,128)(2,1)S(1)}, bf16[256,128]{1,0:T(8,128)(2,1)S(1)}, u32[]{:S(2)}, u32[]{:S(2)}) collective-permute-start(bf16[256,128]{1,0:T(8,128)(2,1)S(1)} %get-tuple-element.24), channel_id=1, source_target_pairs={{0,2},{1,3},{2,0},{3,1},{4,6},{5,7},{6,4},{7,5},{8,10},{9,11},{10,... | collective-permute-start | bytes 196616 | tf_op jit(solution)/shard_map/ppermute | solution.py:285
  26.2 1.9 %collective-permute-start.12 = (bf16[256,128]{1,0:T(8,128)(2,1)S(1)}, bf16[256,128]{1,0:T(8,128)(2,1)S(1)}, u32[]{:S(2)}, u32[]{:S(2)}) collective-permute-start(bf16[256,128]{1,0:T(8,128)(2,1)S(1)} %get-tuple-element.25), channel_id=1, source_target_pairs={{0,3},{1,2},{2,1},{3,0},{4,7},{5,6},{6,5},{7,4},{8,11},{9,10},{10,... | collective-permute-start | bytes 196616 | tf_op jit(solution)/shard_map/ppermute | solution.py:285
  28.1 0.6 %collective-permute-done.10.refs_1_ = bf16[256,128]{1,0:T(8,128)(2,1)S(1)} collective-permute-done((bf16[256,128]{1,0:T(8,128)(2,1)S(1)}, bf16[256,128]{1,0:T(8,128)(2,1)S(1)}, u32[]{:S(2)}, u32[]{:S(2)}) %collective-permute-start.10) | collective-permute-done | bytes 65568 | tf_op jit(solution)/shard_map/ppermute | solution.py:285
  28.8 4.1 %collective-permute-done.11.refs_2_ = bf16[256,128]{1,0:T(8,128)(2,1)S(1)} collective-permute-done((bf16[256,128]{1,0:T(8,128)(2,1)S(1)}, bf16[256,128]{1,0:T(8,128)(2,1)S(1)}, u32[]{:S(2)}, u32[]{:S(2)}) %collective-permute-start.11) | collective-permute-done | bytes 65568 | tf_op jit(solution)/shard_map/ppermute | solution.py:285
  32.9 0.5 %dense.1 = (bf16[256,256]{1,0:T(8,128)(2,1)S(1)}, f32[144,256]{1,0:T(8,128)S(1)}, f32[144,256]{1,0:T(8,128)S(1)}) custom-call(bf16[256,128]{1,0:T(8,128)(2,1)S(1)} %get-tuple-element.22.refs_0_, bf16[256,128]{1,0:T(8,128)(2,1)S(1)} %collective-permute-done.10.refs_1_, bf16[256,128]{1,0:T(8,128)(2,1)S(1)} %collective-permute-done.11.refs_2_, ...), custom_call_target="tpu_custom_call" | custom-call | tf_op jit(solution)/shard_map/dense/pallas_call | solution.py:37
  33.5 1.4 %collective-permute-done.13 = f32[144,256]{1,0:T(8,128)S(1)} collective-permute-done((f32[144,256]{1,0:T(8,128)S(1)}, f32[144,256]{1,0:T(8,128)S(1)}, u32[]{:S(2)}, u32[]{:S(2)}) %collective-permute-start.13) | collective-permute-done | bytes 147488 | tf_op jit(solution)/shard_map/ppermute | solution.py:296
  34.9 2.4 %collective-permute-start.16 = (bf16[144,256]{1,0:T(8,128)(2,1)S(1)}, bf16[144,256]{1,0:T(8,128)(2,1)S(1)}, u32[]{:S(2)}, u32[]{:S(2)}) collective-permute-start(bf16[144,256]{1,0:T(8,128)(2,1)S(1)} %add_convert_fusion.2), channel_id=1, source_target_pairs={{0,24},{4,28},{8,16},{12,20},{16,8},{20,12},{24,0},{28,4},{1,25},{... | collective-permute-start | bytes 221192 | tf_op jit(solution)/shard_map/ppermute | solution.py:214
  37.3 1.1 %collective-permute-start.14 = (bf16[144,256]{1,0:T(8,128)(2,1)S(1)}, bf16[144,256]{1,0:T(8,128)(2,1)S(1)}, u32[]{:S(2)}, u32[]{:S(2)}) collective-permute-start(bf16[144,256]{1,0:T(8,128)(2,1)S(1)} %add_convert_fusion.2), channel_id=1, source_target_pairs={{0,8},{4,12},{8,0},{12,4},{16,24},{20,28},{24,16},{28,20},{1,9},{5... | collective-permute-start | bytes 221192 | tf_op jit(solution)/shard_map/ppermute | solution.py:209
  38.5 1.8 %collective-permute-done.16 = bf16[144,256]{1,0:T(8,128)(2,1)S(1)} collective-permute-done((bf16[144,256]{1,0:T(8,128)(2,1)S(1)}, bf16[144,256]{1,0:T(8,128)(2,1)S(1)}, u32[]{:S(2)}, u32[]{:S(2)}) %collective-permute-start.16) | collective-permute-done | bytes 73760 | tf_op jit(solution)/shard_map/ppermute | solution.py:214
  40.3 1.5 %collective-permute-done.15 = bf16[144,256]{1,0:T(8,128)(2,1)S(1)} collective-permute-done((bf16[144,256]{1,0:T(8,128)(2,1)S(1)}, bf16[144,256]{1,0:T(8,128)(2,1)S(1)}, u32[]{:S(2)}, u32[]{:S(2)}) %collective-permute-start.15) | collective-permute-done | bytes 73760 | tf_op jit(solution)/shard_map/ppermute | solution.py:213
  41.9 1.9 %collective-permute-start.19 = (bf16[144,256]{1,0:T(8,128)(2,1)S(1)}, bf16[144,256]{1,0:T(8,128)(2,1)S(1)}, u32[]{:S(2)}, u32[]{:S(2)}) collective-permute-start(bf16[144,256]{1,0:T(8,128)(2,1)S(1)} %add_convert_fusion.1), channel_id=1, source_target_pairs={{0,3},{1,2},{2,1},{3,0},{4,7},{5,6},{6,5},{7,4},{8,11},{9,10},{10,... | collective-permute-start | bytes 221192 | tf_op jit(solution)/shard_map/ppermute | solution.py:214
  43.8 0.9 %collective-permute-start.18 = (bf16[144,256]{1,0:T(8,128)(2,1)S(1)}, bf16[144,256]{1,0:T(8,128)(2,1)S(1)}, u32[]{:S(2)}, u32[]{:S(2)}) collective-permute-start(bf16[144,256]{1,0:T(8,128)(2,1)S(1)} %add_convert_fusion.1), channel_id=1, source_target_pairs={{0,2},{1,3},{2,0},{3,1},{4,6},{5,7},{6,4},{7,5},{8,10},{9,11},{10,... | collective-permute-start | bytes 221192 | tf_op jit(solution)/shard_map/ppermute | solution.py:213
  44.6 1.7 %collective-permute-start.17 = (bf16[144,256]{1,0:T(8,128)(2,1)S(1)}, bf16[144,256]{1,0:T(8,128)(2,1)S(1)}, u32[]{:S(2)}, u32[]{:S(2)}) collective-permute-start(bf16[144,256]{1,0:T(8,128)(2,1)S(1)} %add_convert_fusion.1), channel_id=1, source_target_pairs={{0,1},{1,0},{2,3},{3,2},{4,5},{5,4},{6,7},{7,6},{8,9},{9,8},{10,11... | collective-permute-start | bytes 221192 | tf_op jit(solution)/shard_map/ppermute | solution.py:209
  46.3 2.1 %collective-permute-done.19 = bf16[144,256]{1,0:T(8,128)(2,1)S(1)} collective-permute-done((bf16[144,256]{1,0:T(8,128)(2,1)S(1)}, bf16[144,256]{1,0:T(8,128)(2,1)S(1)}, u32[]{:S(2)}, u32[]{:S(2)}) %collective-permute-start.19) | collective-permute-done | bytes 73760 | tf_op jit(solution)/shard_map/ppermute | solution.py:214
  48.4 2.8 %collective-permute-done.18 = bf16[144,256]{1,0:T(8,128)(2,1)S(1)} collective-permute-done((bf16[144,256]{1,0:T(8,128)(2,1)S(1)}, bf16[144,256]{1,0:T(8,128)(2,1)S(1)}, u32[]{:S(2)}, u32[]{:S(2)}) %collective-permute-start.18) | collective-permute-done | bytes 73760 | tf_op jit(solution)/shard_map/ppermute | solution.py:213
  51.4 1.3 %collective-permute-done.20.other_ref = bf16[144,256]{1,0:T(8,128)(2,1)S(1)} collective-permute-done((bf16[144,256]{1,0:T(8,128)(2,1)S(1)}, bf16[144,256]{1,0:T(8,128)(2,1)S(1)}, u32[]{:S(2)}, u32[]{:S(2)}) %collective-permute-start.20) | collective-permute-done | bytes 73760 | tf_op jit(solution)/shard_map/ppermute | solution.py:299
  52.7 0.8 %finish.1 = (f32[256,256]{1,0:T(8,128)}, f32[1,256]{1,0:T(1,128)}, bf16[256,256]{1,0:T(8,128)(2,1)}) custom-call(bf16[144,256]{1,0:T(8,128)(2,1)S(1)} %add_convert_fusion.mine_ref, bf16[144,256]{1,0:T(8,128)(2,1)S(1)} %collective-permute-done.20.other_ref, bf16[256,256]{1,0:T(8,128)(2,1)S(1)} %get-tuple-element.31.outcome_ref), custom_call_target="tpu_custom_call" | custom-call | tf_op jit(solution)/shard_map/finish/pallas_call | solution.py:37
  (35 shorter events, 0.5 us)
Async XLA Ops:
  0.6 6.9 %copy-start.1 = (bf16[256,256]{1,0:T(8,128)(2,1)S(1)}, bf16[256,256]{1,0:T(8,128)(2,1)}, u32[]{:S(2)}) copy-start(bf16[256,256]{1,0:T(8,128)(2,1)} %refs_0_.3) | copy-start | bytes 393220
  2.3 5.2 %copy-start.7 = (f32[256]{0:T(256)S(1)}, f32[256]{0:T(256)}, u32[]{:S(2)}) copy-start(f32[256]{0:T(256)} %param.15) | copy-start | bytes 3076
  2.3 10.0 %collective-permute-start.1 = (bf16[256,128]{1,0:T(8,128)(2,1)}, bf16[256,128]{1,0:T(8,128)(2,1)S(1)}, u32[]{:S(2)}, u32[]{:S(2)}) collective-permute-start(bf16[256,128]{1,0:T(8,128)(2,1)} %get-tuple-element.20), channel_id=1, source_target_pairs={{0,24},{1,8},{2,16},{3,0},{4,28},{5,12},{6,20},{7,4},{8,1},{9,17},... | collective-permute-start | bytes 196616 | tf_op jit(solution)/shard_map/ppermute | solution.py:248
  6.3 1.3 %copy-start.5 = (s32[1,2,4]{2,1,0:T(2,128)S(1)}, s32[1,2,4]{2,1,0:T(2,128)}, u32[]{:S(2)}) copy-start(s32[1,2,4]{2,1,0:T(2,128)} %refs_1_.1) | copy-start | bytes 100
  6.3 1.3 %copy-start.6 = (s32[1,2,4]{2,1,0:T(2,128)S(1)}, s32[1,2,4]{2,1,0:T(2,128)}, u32[]{:S(2)}) copy-start(s32[1,2,4]{2,1,0:T(2,128)} %refs_2_.1) | copy-start | bytes 100
  6.3 1.3 %copy-start.4 = (s32[256]{0:T(256)S(1)}, s32[256]{0:T(256)}, u32[]{:S(2)}) copy-start(s32[256]{0:T(256)} %param.10) | copy-start | bytes 3076
  6.3 7.0 %collective-permute-start.2 = (bf16[256,128]{1,0:T(8,128)(2,1)}, bf16[256,128]{1,0:T(8,128)(2,1)S(1)}, u32[]{:S(2)}, u32[]{:S(2)}) collective-permute-start(bf16[256,128]{1,0:T(8,128)(2,1)} %get-tuple-element.21), channel_id=1, source_target_pairs={{0,3},{1,19},{2,11},{3,27},{4,7},{5,23},{6,15},{7,31},{8,10},{9,2}... | collective-permute-start | bytes 196616 | tf_op jit(solution)/shard_map/ppermute | solution.py:248
  7.6 1.0 %copy-start = (s32[1,2,4,128,128]{4,3,2,1,0:T(8,128)S(1)}, s32[1,2,4,128,128]{4,3,2,1,0:T(8,128)}, u32[]{:S(2)}) copy-start(s32[1,2,4,128,128]{4,3,2,1,0:T(8,128)} %refs_0_.2) | copy-start | bytes 1572868
  9.4 12.7 %collective-permute-start = (bf16[1040,128]{1,0:T(8,128)(2,1)S(1)}, bf16[1040,128]{1,0:T(8,128)(2,1)S(1)}, u32[]{:S(2)}, u32[]{:S(2)}) collective-permute-start(bf16[1040,128]{1,0:T(8,128)(2,1)S(1)} %get-tuple-element.19.refs_0_), channel_id=1, source_target_pairs={{0,3},{1,2},{2,1},{3,0},{4,7},{5,6},{6,5},{7,4},{8,11},{9,10},{10,... | collective-permute-start | bytes 798728 | tf_op jit(solution)/shard_map/ppermute | solution.py:261
  13.3 19.6 %copy-start.2 = (bf16[256,256]{1,0:T(8,128)(2,1)S(1)}, bf16[256,256]{1,0:T(8,128)(2,1)}, u32[]{:S(2)}) copy-start(bf16[256,256]{1,0:T(8,128)(2,1)} %refs_6_.1) | copy-start | bytes 393220
  13.3 19.6 %copy-start.3 = (bf16[256,256]{1,0:T(8,128)(2,1)S(1)}, bf16[256,256]{1,0:T(8,128)(2,1)}, u32[]{:S(2)}) copy-start(bf16[256,256]{1,0:T(8,128)(2,1)} %refs_8_.1) | copy-start | bytes 393220
  13.3 7.0 %collective-permute-start.8 = (bf16[512,128]{1,0:T(8,128)(2,1)S(1)}, bf16[512,128]{1,0:T(8,128)(2,1)S(1)}, u32[]{:S(2)}, u32[]{:S(2)}) collective-permute-start(bf16[512,128]{1,0:T(8,128)(2,1)S(1)} %join.1.refs_2_), channel_id=1, source_target_pairs={{0,24},{4,28},{8,16},{12,20},{16,8},{20,12},{24,0},{28,4},{1,25},{... | collective-permute-start | bytes 393224 | tf_op jit(solution)/shard_map/ppermute | solution.py:269
  16.4 5.2 %collective-permute-start.6 = (bf16[512,128]{1,0:T(8,128)(2,1)S(1)}, bf16[512,128]{1,0:T(8,128)(2,1)S(1)}, u32[]{:S(2)}, u32[]{:S(2)}) collective-permute-start(bf16[512,128]{1,0:T(8,128)(2,1)S(1)} %join.1.refs_2_), channel_id=1, source_target_pairs={{0,16},{4,20},{8,24},{12,28},{16,0},{20,4},{24,8},{28,12},{1,17},{... | collective-permute-start | bytes 393224 | tf_op jit(solution)/shard_map/ppermute | solution.py:269
  16.4 5.2 %collective-permute-start.4 = (bf16[512,128]{1,0:T(8,128)(2,1)S(1)}, bf16[512,128]{1,0:T(8,128)(2,1)S(1)}, u32[]{:S(2)}, u32[]{:S(2)}) collective-permute-start(bf16[512,128]{1,0:T(8,128)(2,1)S(1)} %join.1.refs_2_), channel_id=1, source_target_pairs={{0,8},{4,12},{8,0},{12,4},{16,24},{20,28},{24,16},{28,20},{1,9},{5... | collective-permute-start | bytes 393224 | tf_op jit(solution)/shard_map/ppermute | solution.py:269
  17.0 5.1 %collective-permute-start.3 = (bf16[512,128]{1,0:T(8,128)(2,1)S(1)}, bf16[512,128]{1,0:T(8,128)(2,1)S(1)}, u32[]{:S(2)}, u32[]{:S(2)}) collective-permute-start(bf16[512,128]{1,0:T(8,128)(2,1)S(1)} %join.1.refs_2_), channel_id=1, source_target_pairs={{0,4},{4,0},{8,12},{12,8},{16,20},{20,16},{24,28},{28,24},{1,5},{5... | collective-permute-start | bytes 393224 | tf_op jit(solution)/shard_map/ppermute | solution.py:271
  20.4 1.7 %collective-permute-start.9 = (bf16[512,128]{1,0:T(8,128)(2,1)S(1)}, bf16[512,128]{1,0:T(8,128)(2,1)S(1)}, u32[]{:S(2)}, u32[]{:S(2)}) collective-permute-start(bf16[512,128]{1,0:T(8,128)(2,1)S(1)} %collective-permute-done.8.refs_8_), channel_id=1, source_target_pairs={{0,4},{4,0},{8,12},{12,8},{16,20},{20,16},{24,28},{28,24},{1,5},{5... | collective-permute-start | bytes 393224 | tf_op jit(solution)/shard_map/ppermute | solution.py:271
  21.6 1.3 %collective-permute-start.7 = (bf16[512,128]{1,0:T(8,128)(2,1)S(1)}, bf16[512,128]{1,0:T(8,128)(2,1)S(1)}, u32[]{:S(2)}, u32[]{:S(2)}) collective-permute-start(bf16[512,128]{1,0:T(8,128)(2,1)S(1)} %collective-permute-done.6.refs_6_), channel_id=1, source_target_pairs={{0,4},{4,0},{8,12},{12,8},{16,20},{20,16},{24,28},{28,24},{1,5},{5... | collective-permute-start | bytes 393224 | tf_op jit(solution)/shard_map/ppermute | solution.py:271
  21.6 1.5 %collective-permute-start.5 = (bf16[512,128]{1,0:T(8,128)(2,1)S(1)}, bf16[512,128]{1,0:T(8,128)(2,1)S(1)}, u32[]{:S(2)}, u32[]{:S(2)}) collective-permute-start(bf16[512,128]{1,0:T(8,128)(2,1)S(1)} %collective-permute-done.4.refs_4_), channel_id=1, source_target_pairs={{0,4},{4,0},{8,12},{12,8},{16,20},{20,16},{24,28},{28,24},{1,5},{5... | collective-permute-start | bytes 393224 | tf_op jit(solution)/shard_map/ppermute | solution.py:271
  23.7 5.1 %collective-permute-start.10 = (bf16[256,128]{1,0:T(8,128)(2,1)S(1)}, bf16[256,128]{1,0:T(8,128)(2,1)S(1)}, u32[]{:S(2)}, u32[]{:S(2)}) collective-permute-start(bf16[256,128]{1,0:T(8,128)(2,1)S(1)} %get-tuple-element.23), channel_id=1, source_target_pairs={{0,1},{1,0},{2,3},{3,2},{4,5},{5,4},{6,7},{7,6},{8,9},{9,8},{10,11... | collective-permute-start | bytes 196616 | tf_op jit(solution)/shard_map/ppermute | solution.py:285
  25.2 7.7 %collective-permute-start.11 = (bf16[256,128]{1,0:T(8,128)(2,1)S(1)}, bf16[256,128]{1,0:T(8,128)(2,1)S(1)}, u32[]{:S(2)}, u32[]{:S(2)}) collective-permute-start(bf16[256,128]{1,0:T(8,128)(2,1)S(1)} %get-tuple-element.24), channel_id=1, source_target_pairs={{0,2},{1,3},{2,0},{3,1},{4,6},{5,7},{6,4},{7,5},{8,10},{9,11},{10,... | collective-permute-start | bytes 196616 | tf_op jit(solution)/shard_map/ppermute | solution.py:285
  26.2 6.6 %collective-permute-start.12 = (bf16[256,128]{1,0:T(8,128)(2,1)S(1)}, bf16[256,128]{1,0:T(8,128)(2,1)S(1)}, u32[]{:S(2)}, u32[]{:S(2)}) collective-permute-start(bf16[256,128]{1,0:T(8,128)(2,1)S(1)} %get-tuple-element.25), channel_id=1, source_target_pairs={{0,3},{1,2},{2,1},{3,0},{4,7},{5,6},{6,5},{7,4},{8,11},{9,10},{10,... | collective-permute-start | bytes 196616 | tf_op jit(solution)/shard_map/ppermute | solution.py:285
  33.5 1.4 %collective-permute-start.13 = (f32[144,256]{1,0:T(8,128)S(1)}, f32[144,256]{1,0:T(8,128)S(1)}, u32[]{:S(2)}, u32[]{:S(2)}) collective-permute-start(f32[144,256]{1,0:T(8,128)S(1)} %get-tuple-element.30), channel_id=1, source_target_pairs={{0,4},{4,0},{8,12},{12,8},{16,20},{20,16},{24,28},{28,24},{1,5},{5... | collective-permute-start | bytes 442376 | tf_op jit(solution)/shard_map/ppermute | solution.py:296
  34.9 5.4 %collective-permute-start.16 = (bf16[144,256]{1,0:T(8,128)(2,1)S(1)}, bf16[144,256]{1,0:T(8,128)(2,1)S(1)}, u32[]{:S(2)}, u32[]{:S(2)}) collective-permute-start(bf16[144,256]{1,0:T(8,128)(2,1)S(1)} %add_convert_fusion.2), channel_id=1, source_target_pairs={{0,24},{4,28},{8,16},{12,20},{16,8},{20,12},{24,0},{28,4},{1,25},{... | collective-permute-start | bytes 221192 | tf_op jit(solution)/shard_map/ppermute | solution.py:214
  37.3 4.5 %collective-permute-start.15 = (bf16[144,256]{1,0:T(8,128)(2,1)S(1)}, bf16[144,256]{1,0:T(8,128)(2,1)S(1)}, u32[]{:S(2)}, u32[]{:S(2)}) collective-permute-start(bf16[144,256]{1,0:T(8,128)(2,1)S(1)} %add_convert_fusion.2), channel_id=1, source_target_pairs={{0,16},{4,20},{8,24},{12,28},{16,0},{20,4},{24,8},{28,12},{1,17},{... | collective-permute-start | bytes 221192 | tf_op jit(solution)/shard_map/ppermute | solution.py:213
  37.3 4.5 %collective-permute-start.14 = (bf16[144,256]{1,0:T(8,128)(2,1)S(1)}, bf16[144,256]{1,0:T(8,128)(2,1)S(1)}, u32[]{:S(2)}, u32[]{:S(2)}) collective-permute-start(bf16[144,256]{1,0:T(8,128)(2,1)S(1)} %add_convert_fusion.2), channel_id=1, source_target_pairs={{0,8},{4,12},{8,0},{12,4},{16,24},{20,28},{24,16},{28,20},{1,9},{5... | collective-permute-start | bytes 221192 | tf_op jit(solution)/shard_map/ppermute | solution.py:209
  41.9 6.6 %collective-permute-start.19 = (bf16[144,256]{1,0:T(8,128)(2,1)S(1)}, bf16[144,256]{1,0:T(8,128)(2,1)S(1)}, u32[]{:S(2)}, u32[]{:S(2)}) collective-permute-start(bf16[144,256]{1,0:T(8,128)(2,1)S(1)} %add_convert_fusion.1), channel_id=1, source_target_pairs={{0,3},{1,2},{2,1},{3,0},{4,7},{5,6},{6,5},{7,4},{8,11},{9,10},{10,... | collective-permute-start | bytes 221192 | tf_op jit(solution)/shard_map/ppermute | solution.py:214
  43.8 7.5 %collective-permute-start.18 = (bf16[144,256]{1,0:T(8,128)(2,1)S(1)}, bf16[144,256]{1,0:T(8,128)(2,1)S(1)}, u32[]{:S(2)}, u32[]{:S(2)}) collective-permute-start(bf16[144,256]{1,0:T(8,128)(2,1)S(1)} %add_convert_fusion.1), channel_id=1, source_target_pairs={{0,2},{1,3},{2,0},{3,1},{4,6},{5,7},{6,4},{7,5},{8,10},{9,11},{10,... | collective-permute-start | bytes 221192 | tf_op jit(solution)/shard_map/ppermute | solution.py:213
  44.6 6.6 %collective-permute-start.17 = (bf16[144,256]{1,0:T(8,128)(2,1)S(1)}, bf16[144,256]{1,0:T(8,128)(2,1)S(1)}, u32[]{:S(2)}, u32[]{:S(2)}) collective-permute-start(bf16[144,256]{1,0:T(8,128)(2,1)S(1)} %add_convert_fusion.1), channel_id=1, source_target_pairs={{0,1},{1,0},{2,3},{3,2},{4,5},{5,4},{6,7},{7,6},{8,9},{9,8},{10,11... | collective-permute-start | bytes 221192 | tf_op jit(solution)/shard_map/ppermute | solution.py:209
  51.3 1.3 %collective-permute-start.20 = (bf16[144,256]{1,0:T(8,128)(2,1)S(1)}, bf16[144,256]{1,0:T(8,128)(2,1)S(1)}, u32[]{:S(2)}, u32[]{:S(2)}) collective-permute-start(bf16[144,256]{1,0:T(8,128)(2,1)S(1)} %add_convert_fusion.mine_ref), channel_id=1, source_target_pairs={{0,4},{4,0},{8,12},{12,8},{16,20},{20,16},{24,28},{28,24},{1,5},{5... | collective-permute-start | bytes 221192 | tf_op jit(solution)/shard_map/ppermute | solution.py:299

commit v7 on v6

--- a/solution.py
+++ b/solution.py
@@ -14,7 +14,7 @@
 GELU_C = 0.7978845608028654
 
 
-ASIDE = ((3, 1, 2, 0), (1, 3, 2, 0), (0, 1, 3, 2), (0, 2, 1, 3))
+ASIDE = ((3, 2, 1, 0), (1, 3, 2, 0), (0, 1, 3, 2), (0, 1, 2, 3))
 ASIDE_BITS = sum(
     to << (2 * (4 * plane + rep)) for plane, row in enumerate(ASIDE) for rep, to in enumerate(row)
 )
@@ -181,10 +181,10 @@
     top, bottom = weight_term[:kept], weight_term[kept:]
     core = lax.axis_index("dom") % 2
     keep_ref[:kept, :] = jnp.where(core == 0, top, bottom)
-    send_ref[:kept, :] = jnp.where(core == 0, bottom, top)
+    send_ref[:kept, :] = jnp.where(core == 0, bottom, top).astype(jnp.bfloat16)
     extra = jnp.broadcast_to(bias_term, (keep_ref.shape[0] - kept, width))
     keep_ref[kept:, :] = extra
-    send_ref[kept:, :] = extra
+    send_ref[kept:, :] = extra.astype(jnp.bfloat16)
 
 
 def finish_kernel(mine_ref, other_ref, outcome_ref, weight_ref, bias_ref, out_ref):
@@ -284,16 +284,16 @@
     for mask in range(1, rep_size):
         parts.append(lax.ppermute(partials[mask], "rep", xor_pairs(rep_size, mask)))
 
-    share = jax.ShapeDtypeStruct((width // 2 + 16, width), f32)
+    share = [jax.ShapeDtypeStruct((width // 2 + 16, width), each) for each in (f32, bf16)]
     outcome, keep, send = local_call(
         lambda *refs: dense_kernel(rep_size, *refs), "dense",
         (*parts, scaled, inv_root, weight, bias_row, cotangent),
         [VMEM] * (rep_size + 5),
-        (jax.ShapeDtypeStruct((row_count, width), bf16), share, share),
+        (jax.ShapeDtypeStruct((row_count, width), bf16), *share),
     )
 
     swap = xor_pairs(dom_size, 1)
-    mine = (keep + lax.ppermute(send, "dom", swap)).astype(bf16)
+    mine = (keep + lax.ppermute(send, "dom", swap).astype(f32)).astype(bf16)
     mine = exchange_sum(mine, "dom", bits_of(dom_size)[1:])
     mine = exchange_sum(mine, "rep", bits_of(rep_size))
     other = lax.ppermute(mine, "dom", swap)

time: 53.6 us -> 53.2 us (level)
  waiting for transfers between devices: 22.3 us -> 21.5 us
    ppermute x2, waiting for transfers between devices: 4.37 us -> 3.46 us  [exchange_sum(): second = lax.ppermute(value, axis, xor_pairs(size, now[1]))]
    ppermute x2, waiting for transfers between devices: 3.94 us -> 4.63 us  [exchange_sum(): third = lax.ppermute(value, axis, xor_pairs(size, now[0] ^ now[1]))]
where the time goes in v7:
time: 53.2 us; the launch traced here: 53.1 us
  starting transfers between devices  25.3 us (48%)
  waiting for transfers between devices  21.5 us (40%)
  Pallas kernels  4.34 us (8%)
  local copies, waits for them, and re-layouts  1.07 us (2%)
  between operations  0.77 us (1%)
    ppermute x2, starting transfers between devices, on_device(): arrived.append(lax.ppermute(part, ('dom', 'rep'), moves))  5.2 us
    ppermute x2, waiting for transfers between devices, exchange_sum(): third = lax.ppermute(value, axis, xor_pairs(size, now[0] ^ now[1]))  4.63 us
    ppermute x3, waiting for transfers between devices, on_device(): parts.append(lax.ppermute(partials[mask], 'rep', xor_pairs(rep_size, mask)))  4.63 us
    ppermute x3, waiting for transfers between devices, on_device(): pieces[mask] = lax.ppermute(pieces[0], 'dom', xor_pairs(dom_size, mask))  4.58 us
    ppermute x2, starting transfers between devices, exchange_sum(): third = lax.ppermute(value, axis, xor_pairs(size, now[0] ^ now[1]))  4.54 us
    ppermute x3, starting transfers between devices, on_device(): parts.append(lax.ppermute(partials[mask], 'rep', xor_pairs(rep_size, mask)))  4.45 us
    pallas_call x6, Pallas kernels, local_call(): pl.pallas_call(kernel, out_shape=out_shape, in_specs=in_specs, out_specs=...  4.34 us
    ppermute x3, starting transfers between devices, on_device(): pieces[mask] = lax.ppermute(pieces[0], 'dom', xor_pairs(dom_size, mask))  4.03 us
  transfers between devices with their start and end apart: 21, of which 13 were waited for; matrix products, arithmetic and copies ran while one was open for 0% of the time, Pallas kernels for 2%

profile of v7, /device:TPU:0, one launch (start us, length us, event | category | flops | bytes accessed | tf_op | source)
XLA Modules:
  0.0 53.1 jit_solution(6237808745462870588)
XLA Ops:
  0.6 1.7 %scale.1 = (bf16[256,128]{1,0:T(8,128)(2,1)}, bf16[256,128]{1,0:T(8,128)(2,1)}) custom-call(bf16[256,256]{1,0:T(8,128)(2,1)} %refs_0_.3, s32[1,256]{1,0:T(1,128)} %bitcast.3), custom_call_target="tpu_custom_call" | custom-call | tf_op jit(solution)/shard_map/scale/pallas_call | solution.py:37
  2.3 3.9 %collective-permute-start.1 = (bf16[256,128]{1,0:T(8,128)(2,1)}, bf16[256,128]{1,0:T(8,128)(2,1)S(1)}, u32[]{:S(2)}, u32[]{:S(2)}) collective-permute-start(bf16[256,128]{1,0:T(8,128)(2,1)} %get-tuple-element.20), channel_id=1, source_target_pairs={{0,24},{1,16},{2,8},{3,0},{4,28},{5,20},{6,12},{7,4},{8,1},{9,17},... | collective-permute-start | bytes 196616 | tf_op jit(solution)/shard_map/ppermute | solution.py:248
  6.3 1.2 %collective-permute-start.2 = (bf16[256,128]{1,0:T(8,128)(2,1)}, bf16[256,128]{1,0:T(8,128)(2,1)S(1)}, u32[]{:S(2)}, u32[]{:S(2)}) collective-permute-start(bf16[256,128]{1,0:T(8,128)(2,1)} %get-tuple-element.21), channel_id=1, source_target_pairs={{0,3},{1,11},{2,19},{3,27},{4,7},{5,15},{6,23},{7,31},{8,10},{9,2}... | collective-permute-start | bytes 196616 | tf_op jit(solution)/shard_map/ppermute | solution.py:248
  7.6 1.0 %copy-done = s32[1,2,4,128,128]{4,3,2,1,0:T(8,128)S(1)} copy-done((s32[1,2,4,128,128]{4,3,2,1,0:T(8,128)S(1)}, s32[1,2,4,128,128]{4,3,2,1,0:T(8,128)}, u32[]{:S(2)}) %copy-start) | copy-done | bytes 524312
  8.6 0.8 %prepare.1 = (bf16[1040,128]{1,0:T(8,128)(2,1)S(1)}, bf16[256,256]{1,0:T(8,128)(2,1)S(1)}, f32[256,128]{1,0:T(8,128)S(1)}, f32[1,256]{1,0:T(1,128)S(1)}) custom-call(s32[1,2,4,128,128]{4,3,2,1,0:T(8,128)S(1)} %copy-done, s32[1,2,4]{2,1,0:T(2,128)S(1)} %copy-done.5, s32[1,2,4]{2,1,0:T(2,128)S(1)} %copy-done.6, bf16[256,256]{1,0:T(8,128)(2,1)S(1)} %copy-done.1, ...), custom_call_target="tpu_custom_call" | custom-call | tf_op jit(solution)/shard_map/prepare/pallas_call | solution.py:37
  9.4 2.9 %collective-permute-start = (bf16[1040,128]{1,0:T(8,128)(2,1)S(1)}, bf16[1040,128]{1,0:T(8,128)(2,1)S(1)}, u32[]{:S(2)}, u32[]{:S(2)}) collective-permute-start(bf16[1040,128]{1,0:T(8,128)(2,1)S(1)} %get-tuple-element.19.refs_0_), channel_id=1, source_target_pairs={{0,3},{1,2},{2,1},{3,0},{4,7},{5,6},{6,5},{7,4},{8,11},{9,10},{10,... | collective-permute-start | bytes 798728 | tf_op jit(solution)/shard_map/ppermute | solution.py:261
  12.3 0.6 %collective-permute-done.2.second_ref = bf16[256,128]{1,0:T(8,128)(2,1)S(1)} collective-permute-done((bf16[256,128]{1,0:T(8,128)(2,1)}, bf16[256,128]{1,0:T(8,128)(2,1)S(1)}, u32[]{:S(2)}, u32[]{:S(2)}) %collective-permute-start.2) | collective-permute-done | bytes 65568 | tf_op jit(solution)/shard_map/ppermute | solution.py:248
  13.0 3.4 %collective-permute-start.8 = (bf16[512,128]{1,0:T(8,128)(2,1)S(1)}, bf16[512,128]{1,0:T(8,128)(2,1)S(1)}, u32[]{:S(2)}, u32[]{:S(2)}) collective-permute-start(bf16[512,128]{1,0:T(8,128)(2,1)S(1)} %join.1.refs_2_), channel_id=1, source_target_pairs={{0,24},{4,28},{8,16},{12,20},{16,8},{20,12},{24,0},{28,4},{1,25},{... | collective-permute-start | bytes 393224 | tf_op jit(solution)/shard_map/ppermute | solution.py:269
  16.4 0.6 %collective-permute-start.4 = (bf16[512,128]{1,0:T(8,128)(2,1)S(1)}, bf16[512,128]{1,0:T(8,128)(2,1)S(1)}, u32[]{:S(2)}, u32[]{:S(2)}) collective-permute-start(bf16[512,128]{1,0:T(8,128)(2,1)S(1)} %join.1.refs_2_), channel_id=1, source_target_pairs={{0,8},{4,12},{8,0},{12,4},{16,24},{20,28},{24,16},{28,20},{1,9},{5... | collective-permute-start | bytes 393224 | tf_op jit(solution)/shard_map/ppermute | solution.py:269
  17.0 3.4 %collective-permute-done.8.refs_8_ = bf16[512,128]{1,0:T(8,128)(2,1)S(1)} collective-permute-done((bf16[512,128]{1,0:T(8,128)(2,1)S(1)}, bf16[512,128]{1,0:T(8,128)(2,1)S(1)}, u32[]{:S(2)}, u32[]{:S(2)}) %collective-permute-start.8) | collective-permute-done | bytes 131104 | tf_op jit(solution)/shard_map/ppermute | solution.py:269
  20.5 1.1 %collective-permute-done.6.refs_6_ = bf16[512,128]{1,0:T(8,128)(2,1)S(1)} collective-permute-done((bf16[512,128]{1,0:T(8,128)(2,1)S(1)}, bf16[512,128]{1,0:T(8,128)(2,1)S(1)}, u32[]{:S(2)}, u32[]{:S(2)}) %collective-permute-start.6) | collective-permute-done | bytes 131104 | tf_op jit(solution)/shard_map/ppermute | solution.py:269
  21.6 0.5 collective-permute-start.5
  22.1 0.8 %collective-permute-done.7.refs_7_ = bf16[512,128]{1,0:T(8,128)(2,1)S(1)} collective-permute-done((bf16[512,128]{1,0:T(8,128)(2,1)S(1)}, bf16[512,128]{1,0:T(8,128)(2,1)S(1)}, u32[]{:S(2)}, u32[]{:S(2)}) %collective-permute-start.7) | collective-permute-done | bytes 131104 | tf_op jit(solution)/shard_map/ppermute | solution.py:271
  23.1 0.6 %aggregate.1 = (bf16[256,128]{1,0:T(8,128)(2,1)S(1)}, bf16[256,128]{1,0:T(8,128)(2,1)S(1)}, bf16[256,128]{1,0:T(8,128)(2,1)S(1)}, bf16[256,128]{1,0:T(8,128)(2,1)S(1)}) custom-call(bf16[1040,128]{1,0:T(8,128)(2,1)S(1)} %get-tuple-element.19.refs_0_, bf16[1040,128]{1,0:T(8,128)(2,1)S(1)} %collective-permute-done.refs_1_, bf16[512,128]{1,0:T(8,128)(2,1)S(1)} %join.1.refs_2_, ...), custom_call_target="tpu_custom_call" | custom-call | tf_op jit(solution)/shard_map/aggregate/pallas_call | solution.py:37
  23.7 1.5 %collective-permute-start.10 = (bf16[256,128]{1,0:T(8,128)(2,1)S(1)}, bf16[256,128]{1,0:T(8,128)(2,1)S(1)}, u32[]{:S(2)}, u32[]{:S(2)}) collective-permute-start(bf16[256,128]{1,0:T(8,128)(2,1)S(1)} %get-tuple-element.23), channel_id=1, source_target_pairs={{0,1},{1,0},{2,3},{3,2},{4,5},{5,4},{6,7},{7,6},{8,9},{9,8},{10,11... | collective-permute-start | bytes 196616 | tf_op jit(solution)/shard_map/ppermute | solution.py:285
  25.2 1.1 %collective-permute-start.11 = (bf16[256,128]{1,0:T(8,128)(2,1)S(1)}, bf16[256,128]{1,0:T(8,128)(2,1)S(1)}, u32[]{:S(2)}, u32[]{:S(2)}) collective-permute-start(bf16[256,128]{1,0:T(8,128)(2,1)S(1)} %get-tuple-element.24), channel_id=1, source_target_pairs={{0,2},{1,3},{2,0},{3,1},{4,6},{5,7},{6,4},{7,5},{8,10},{9,11},{10,... | collective-permute-start | bytes 196616 | tf_op jit(solution)/shard_map/ppermute | solution.py:285
  26.3 1.9 %collective-permute-start.12 = (bf16[256,128]{1,0:T(8,128)(2,1)S(1)}, bf16[256,128]{1,0:T(8,128)(2,1)S(1)}, u32[]{:S(2)}, u32[]{:S(2)}) collective-permute-start(bf16[256,128]{1,0:T(8,128)(2,1)S(1)} %get-tuple-element.25), channel_id=1, source_target_pairs={{0,3},{1,2},{2,1},{3,0},{4,7},{5,6},{6,5},{7,4},{8,11},{9,10},{10,... | collective-permute-start | bytes 196616 | tf_op jit(solution)/shard_map/ppermute | solution.py:285
  28.2 0.6 %collective-permute-done.10.refs_1_ = bf16[256,128]{1,0:T(8,128)(2,1)S(1)} collective-permute-done((bf16[256,128]{1,0:T(8,128)(2,1)S(1)}, bf16[256,128]{1,0:T(8,128)(2,1)S(1)}, u32[]{:S(2)}, u32[]{:S(2)}) %collective-permute-start.10) | collective-permute-done | bytes 65568 | tf_op jit(solution)/shard_map/ppermute | solution.py:285
  28.8 4.0 %collective-permute-done.11.refs_2_ = bf16[256,128]{1,0:T(8,128)(2,1)S(1)} collective-permute-done((bf16[256,128]{1,0:T(8,128)(2,1)S(1)}, bf16[256,128]{1,0:T(8,128)(2,1)S(1)}, u32[]{:S(2)}, u32[]{:S(2)}) %collective-permute-start.11) | collective-permute-done | bytes 65568 | tf_op jit(solution)/shard_map/ppermute | solution.py:285
  32.8 0.5 %dense.1 = (bf16[256,256]{1,0:T(8,128)(2,1)S(1)}, f32[144,256]{1,0:T(8,128)S(1)}, bf16[144,256]{1,0:T(8,128)(2,1)S(1)}) custom-call(bf16[256,128]{1,0:T(8,128)(2,1)S(1)} %get-tuple-element.22.refs_0_, bf16[256,128]{1,0:T(8,128)(2,1)S(1)} %collective-permute-done.10.refs_1_, bf16[256,128]{1,0:T(8,128)(2,1)S(1)} %collective-permute-done.11.refs_2_, ...), custom_call_target="tpu_custom_call" | custom-call | tf_op jit(solution)/shard_map/dense/pallas_call | solution.py:37
  33.4 1.3 %collective-permute-done.13 = bf16[144,256]{1,0:T(8,128)(2,1)S(1)} collective-permute-done((bf16[144,256]{1,0:T(8,128)(2,1)S(1)}, bf16[144,256]{1,0:T(8,128)(2,1)S(1)}, u32[]{:S(2)}, u32[]{:S(2)}) %collective-permute-start.13) | collective-permute-done | bytes 73760 | tf_op jit(solution)/shard_map/ppermute | solution.py:296
  34.7 3.0 %collective-permute-start.16 = (bf16[144,256]{1,0:T(8,128)(2,1)S(1)}, bf16[144,256]{1,0:T(8,128)(2,1)S(1)}, u32[]{:S(2)}, u32[]{:S(2)}) collective-permute-start(bf16[144,256]{1,0:T(8,128)(2,1)S(1)} %add_convert_fusion.2), channel_id=1, source_target_pairs={{0,24},{4,28},{8,16},{12,20},{16,8},{20,12},{24,0},{28,4},{1,25},{... | collective-permute-start | bytes 221192 | tf_op jit(solution)/shard_map/ppermute | solution.py:214
  37.7 0.6 %collective-permute-start.14 = (bf16[144,256]{1,0:T(8,128)(2,1)S(1)}, bf16[144,256]{1,0:T(8,128)(2,1)S(1)}, u32[]{:S(2)}, u32[]{:S(2)}) collective-permute-start(bf16[144,256]{1,0:T(8,128)(2,1)S(1)} %add_convert_fusion.2), channel_id=1, source_target_pairs={{0,8},{4,12},{8,0},{12,4},{16,24},{20,28},{24,16},{28,20},{1,9},{5... | collective-permute-start | bytes 221192 | tf_op jit(solution)/shard_map/ppermute | solution.py:209
  38.3 2.0 %collective-permute-done.16 = bf16[144,256]{1,0:T(8,128)(2,1)S(1)} collective-permute-done((bf16[144,256]{1,0:T(8,128)(2,1)S(1)}, bf16[144,256]{1,0:T(8,128)(2,1)S(1)}, u32[]{:S(2)}, u32[]{:S(2)}) %collective-permute-start.16) | collective-permute-done | bytes 73760 | tf_op jit(solution)/shard_map/ppermute | solution.py:214
  40.3 1.7 %collective-permute-done.15 = bf16[144,256]{1,0:T(8,128)(2,1)S(1)} collective-permute-done((bf16[144,256]{1,0:T(8,128)(2,1)S(1)}, bf16[144,256]{1,0:T(8,128)(2,1)S(1)}, u32[]{:S(2)}, u32[]{:S(2)}) %collective-permute-start.15) | collective-permute-done | bytes 73760 | tf_op jit(solution)/shard_map/ppermute | solution.py:213
  42.1 1.6 %collective-permute-start.19 = (bf16[144,256]{1,0:T(8,128)(2,1)S(1)}, bf16[144,256]{1,0:T(8,128)(2,1)S(1)}, u32[]{:S(2)}, u32[]{:S(2)}) collective-permute-start(bf16[144,256]{1,0:T(8,128)(2,1)S(1)} %add_convert_fusion.1), channel_id=1, source_target_pairs={{0,3},{1,2},{2,1},{3,0},{4,7},{5,6},{6,5},{7,4},{8,11},{9,10},{10,... | collective-permute-start | bytes 221192 | tf_op jit(solution)/shard_map/ppermute | solution.py:214
  43.6 1.2 %collective-permute-start.18 = (bf16[144,256]{1,0:T(8,128)(2,1)S(1)}, bf16[144,256]{1,0:T(8,128)(2,1)S(1)}, u32[]{:S(2)}, u32[]{:S(2)}) collective-permute-start(bf16[144,256]{1,0:T(8,128)(2,1)S(1)} %add_convert_fusion.1), channel_id=1, source_target_pairs={{0,2},{1,3},{2,0},{3,1},{4,6},{5,7},{6,4},{7,5},{8,10},{9,11},{10,... | collective-permute-start | bytes 221192 | tf_op jit(solution)/shard_map/ppermute | solution.py:213
  44.9 1.7 %collective-permute-start.17 = (bf16[144,256]{1,0:T(8,128)(2,1)S(1)}, bf16[144,256]{1,0:T(8,128)(2,1)S(1)}, u32[]{:S(2)}, u32[]{:S(2)}) collective-permute-start(bf16[144,256]{1,0:T(8,128)(2,1)S(1)} %add_convert_fusion.1), channel_id=1, source_target_pairs={{0,1},{1,0},{2,3},{3,2},{4,5},{5,4},{6,7},{7,6},{8,9},{9,8},{10,11... | collective-permute-start | bytes 221192 | tf_op jit(solution)/shard_map/ppermute | solution.py:209
  46.5 2.6 %collective-permute-done.19 = bf16[144,256]{1,0:T(8,128)(2,1)S(1)} collective-permute-done((bf16[144,256]{1,0:T(8,128)(2,1)S(1)}, bf16[144,256]{1,0:T(8,128)(2,1)S(1)}, u32[]{:S(2)}, u32[]{:S(2)}) %collective-permute-start.19) | collective-permute-done | bytes 73760 | tf_op jit(solution)/shard_map/ppermute | solution.py:214
  49.2 1.7 %collective-permute-done.18 = bf16[144,256]{1,0:T(8,128)(2,1)S(1)} collective-permute-done((bf16[144,256]{1,0:T(8,128)(2,1)S(1)}, bf16[144,256]{1,0:T(8,128)(2,1)S(1)}, u32[]{:S(2)}, u32[]{:S(2)}) %collective-permute-start.18) | collective-permute-done | bytes 73760 | tf_op jit(solution)/shard_map/ppermute | solution.py:213
  51.0 1.3 %collective-permute-done.20.other_ref = bf16[144,256]{1,0:T(8,128)(2,1)S(1)} collective-permute-done((bf16[144,256]{1,0:T(8,128)(2,1)S(1)}, bf16[144,256]{1,0:T(8,128)(2,1)S(1)}, u32[]{:S(2)}, u32[]{:S(2)}) %collective-permute-start.20) | collective-permute-done | bytes 73760 | tf_op jit(solution)/shard_map/ppermute | solution.py:299
  52.3 0.8 %finish.1 = (f32[256,256]{1,0:T(8,128)}, f32[1,256]{1,0:T(1,128)}, bf16[256,256]{1,0:T(8,128)(2,1)}) custom-call(bf16[144,256]{1,0:T(8,128)(2,1)S(1)} %add_convert_fusion.mine_ref, bf16[144,256]{1,0:T(8,128)(2,1)S(1)} %collective-permute-done.20.other_ref, bf16[256,256]{1,0:T(8,128)(2,1)S(1)} %get-tuple-element.31.outcome_ref), custom_call_target="tpu_custom_call" | custom-call | tf_op jit(solution)/shard_map/finish/pallas_call | solution.py:37
  (35 shorter events, 0.5 us)
Async XLA Ops:
  0.6 6.9 %copy-start.1 = (bf16[256,256]{1,0:T(8,128)(2,1)S(1)}, bf16[256,256]{1,0:T(8,128)(2,1)}, u32[]{:S(2)}) copy-start(bf16[256,256]{1,0:T(8,128)(2,1)} %refs_0_.3) | copy-start | bytes 393220
  2.3 5.2 %copy-start.7 = (f32[256]{0:T(256)S(1)}, f32[256]{0:T(256)}, u32[]{:S(2)}) copy-start(f32[256]{0:T(256)} %param.15) | copy-start | bytes 3076
  2.3 10.0 %collective-permute-start.1 = (bf16[256,128]{1,0:T(8,128)(2,1)}, bf16[256,128]{1,0:T(8,128)(2,1)S(1)}, u32[]{:S(2)}, u32[]{:S(2)}) collective-permute-start(bf16[256,128]{1,0:T(8,128)(2,1)} %get-tuple-element.20), channel_id=1, source_target_pairs={{0,24},{1,16},{2,8},{3,0},{4,28},{5,20},{6,12},{7,4},{8,1},{9,17},... | collective-permute-start | bytes 196616 | tf_op jit(solution)/shard_map/ppermute | solution.py:248
  6.3 1.3 %copy-start.5 = (s32[1,2,4]{2,1,0:T(2,128)S(1)}, s32[1,2,4]{2,1,0:T(2,128)}, u32[]{:S(2)}) copy-start(s32[1,2,4]{2,1,0:T(2,128)} %refs_1_.1) | copy-start | bytes 100
  6.3 1.3 %copy-start.6 = (s32[1,2,4]{2,1,0:T(2,128)S(1)}, s32[1,2,4]{2,1,0:T(2,128)}, u32[]{:S(2)}) copy-start(s32[1,2,4]{2,1,0:T(2,128)} %refs_2_.1) | copy-start | bytes 100
  6.3 1.3 %copy-start.4 = (s32[256]{0:T(256)S(1)}, s32[256]{0:T(256)}, u32[]{:S(2)}) copy-start(s32[256]{0:T(256)} %param.10) | copy-start | bytes 3076
  6.3 6.7 %collective-permute-start.2 = (bf16[256,128]{1,0:T(8,128)(2,1)}, bf16[256,128]{1,0:T(8,128)(2,1)S(1)}, u32[]{:S(2)}, u32[]{:S(2)}) collective-permute-start(bf16[256,128]{1,0:T(8,128)(2,1)} %get-tuple-element.21), channel_id=1, source_target_pairs={{0,3},{1,11},{2,19},{3,27},{4,7},{5,15},{6,23},{7,31},{8,10},{9,2}... | collective-permute-start | bytes 196616 | tf_op jit(solution)/shard_map/ppermute | solution.py:248
  7.6 1.0 %copy-start = (s32[1,2,4,128,128]{4,3,2,1,0:T(8,128)S(1)}, s32[1,2,4,128,128]{4,3,2,1,0:T(8,128)}, u32[]{:S(2)}) copy-start(s32[1,2,4,128,128]{4,3,2,1,0:T(8,128)} %refs_0_.2) | copy-start | bytes 1572868
  9.4 12.7 %collective-permute-start = (bf16[1040,128]{1,0:T(8,128)(2,1)S(1)}, bf16[1040,128]{1,0:T(8,128)(2,1)S(1)}, u32[]{:S(2)}, u32[]{:S(2)}) collective-permute-start(bf16[1040,128]{1,0:T(8,128)(2,1)S(1)} %get-tuple-element.19.refs_0_), channel_id=1, source_target_pairs={{0,3},{1,2},{2,1},{3,0},{4,7},{5,6},{6,5},{7,4},{8,11},{9,10},{10,... | collective-permute-start | bytes 798728 | tf_op jit(solution)/shard_map/ppermute | solution.py:261
  13.0 19.8 %copy-start.2 = (bf16[256,256]{1,0:T(8,128)(2,1)S(1)}, bf16[256,256]{1,0:T(8,128)(2,1)}, u32[]{:S(2)}) copy-start(bf16[256,256]{1,0:T(8,128)(2,1)} %refs_6_.1) | copy-start | bytes 393220
  13.0 19.8 %copy-start.3 = (bf16[256,256]{1,0:T(8,128)(2,1)S(1)}, bf16[256,256]{1,0:T(8,128)(2,1)}, u32[]{:S(2)}) copy-start(bf16[256,256]{1,0:T(8,128)(2,1)} %refs_8_.1) | copy-start | bytes 393220
  13.0 7.5 %collective-permute-start.8 = (bf16[512,128]{1,0:T(8,128)(2,1)S(1)}, bf16[512,128]{1,0:T(8,128)(2,1)S(1)}, u32[]{:S(2)}, u32[]{:S(2)}) collective-permute-start(bf16[512,128]{1,0:T(8,128)(2,1)S(1)} %join.1.refs_2_), channel_id=1, source_target_pairs={{0,24},{4,28},{8,16},{12,20},{16,8},{20,12},{24,0},{28,4},{1,25},{... | collective-permute-start | bytes 393224 | tf_op jit(solution)/shard_map/ppermute | solution.py:269
  16.4 5.2 %collective-permute-start.6 = (bf16[512,128]{1,0:T(8,128)(2,1)S(1)}, bf16[512,128]{1,0:T(8,128)(2,1)S(1)}, u32[]{:S(2)}, u32[]{:S(2)}) collective-permute-start(bf16[512,128]{1,0:T(8,128)(2,1)S(1)} %join.1.refs_2_), channel_id=1, source_target_pairs={{0,16},{4,20},{8,24},{12,28},{16,0},{20,4},{24,8},{28,12},{1,17},{... | collective-permute-start | bytes 393224 | tf_op jit(solution)/shard_map/ppermute | solution.py:269
  16.4 5.2 %collective-permute-start.4 = (bf16[512,128]{1,0:T(8,128)(2,1)S(1)}, bf16[512,128]{1,0:T(8,128)(2,1)S(1)}, u32[]{:S(2)}, u32[]{:S(2)}) collective-permute-start(bf16[512,128]{1,0:T(8,128)(2,1)S(1)} %join.1.refs_2_), channel_id=1, source_target_pairs={{0,8},{4,12},{8,0},{12,4},{16,24},{20,28},{24,16},{28,20},{1,9},{5... | collective-permute-start | bytes 393224 | tf_op jit(solution)/shard_map/ppermute | solution.py:269
  17.0 5.1 %collective-permute-start.3 = (bf16[512,128]{1,0:T(8,128)(2,1)S(1)}, bf16[512,128]{1,0:T(8,128)(2,1)S(1)}, u32[]{:S(2)}, u32[]{:S(2)}) collective-permute-start(bf16[512,128]{1,0:T(8,128)(2,1)S(1)} %join.1.refs_2_), channel_id=1, source_target_pairs={{0,4},{4,0},{8,12},{12,8},{16,20},{20,16},{24,28},{28,24},{1,5},{5... | collective-permute-start | bytes 393224 | tf_op jit(solution)/shard_map/ppermute | solution.py:271
  20.5 1.7 %collective-permute-start.9 = (bf16[512,128]{1,0:T(8,128)(2,1)S(1)}, bf16[512,128]{1,0:T(8,128)(2,1)S(1)}, u32[]{:S(2)}, u32[]{:S(2)}) collective-permute-start(bf16[512,128]{1,0:T(8,128)(2,1)S(1)} %collective-permute-done.8.refs_8_), channel_id=1, source_target_pairs={{0,4},{4,0},{8,12},{12,8},{16,20},{20,16},{24,28},{28,24},{1,5},{5... | collective-permute-start | bytes 393224 | tf_op jit(solution)/shard_map/ppermute | solution.py:271
  21.6 1.3 %collective-permute-start.7 = (bf16[512,128]{1,0:T(8,128)(2,1)S(1)}, bf16[512,128]{1,0:T(8,128)(2,1)S(1)}, u32[]{:S(2)}, u32[]{:S(2)}) collective-permute-start(bf16[512,128]{1,0:T(8,128)(2,1)S(1)} %collective-permute-done.6.refs_6_), channel_id=1, source_target_pairs={{0,4},{4,0},{8,12},{12,8},{16,20},{20,16},{24,28},{28,24},{1,5},{5... | collective-permute-start | bytes 393224 | tf_op jit(solution)/shard_map/ppermute | solution.py:271
  21.6 1.5 %collective-permute-start.5 = (bf16[512,128]{1,0:T(8,128)(2,1)S(1)}, bf16[512,128]{1,0:T(8,128)(2,1)S(1)}, u32[]{:S(2)}, u32[]{:S(2)}) collective-permute-start(bf16[512,128]{1,0:T(8,128)(2,1)S(1)} %collective-permute-done.4.refs_4_), channel_id=1, source_target_pairs={{0,4},{4,0},{8,12},{12,8},{16,20},{20,16},{24,28},{28,24},{1,5},{5... | collective-permute-start | bytes 393224 | tf_op jit(solution)/shard_map/ppermute | solution.py:271
  23.7 5.1 %collective-permute-start.10 = (bf16[256,128]{1,0:T(8,128)(2,1)S(1)}, bf16[256,128]{1,0:T(8,128)(2,1)S(1)}, u32[]{:S(2)}, u32[]{:S(2)}) collective-permute-start(bf16[256,128]{1,0:T(8,128)(2,1)S(1)} %get-tuple-element.23), channel_id=1, source_target_pairs={{0,1},{1,0},{2,3},{3,2},{4,5},{5,4},{6,7},{7,6},{8,9},{9,8},{10,11... | collective-permute-start | bytes 196616 | tf_op jit(solution)/shard_map/ppermute | solution.py:285
  25.2 7.6 %collective-permute-start.11 = (bf16[256,128]{1,0:T(8,128)(2,1)S(1)}, bf16[256,128]{1,0:T(8,128)(2,1)S(1)}, u32[]{:S(2)}, u32[]{:S(2)}) collective-permute-start(bf16[256,128]{1,0:T(8,128)(2,1)S(1)} %get-tuple-element.24), channel_id=1, source_target_pairs={{0,2},{1,3},{2,0},{3,1},{4,6},{5,7},{6,4},{7,5},{8,10},{9,11},{10,... | collective-permute-start | bytes 196616 | tf_op jit(solution)/shard_map/ppermute | solution.py:285
  26.3 6.5 %collective-permute-start.12 = (bf16[256,128]{1,0:T(8,128)(2,1)S(1)}, bf16[256,128]{1,0:T(8,128)(2,1)S(1)}, u32[]{:S(2)}, u32[]{:S(2)}) collective-permute-start(bf16[256,128]{1,0:T(8,128)(2,1)S(1)} %get-tuple-element.25), channel_id=1, source_target_pairs={{0,3},{1,2},{2,1},{3,0},{4,7},{5,6},{6,5},{7,4},{8,11},{9,10},{10,... | collective-permute-start | bytes 196616 | tf_op jit(solution)/shard_map/ppermute | solution.py:285
  33.3 1.3 %collective-permute-start.13 = (bf16[144,256]{1,0:T(8,128)(2,1)S(1)}, bf16[144,256]{1,0:T(8,128)(2,1)S(1)}, u32[]{:S(2)}, u32[]{:S(2)}) collective-permute-start(bf16[144,256]{1,0:T(8,128)(2,1)S(1)} %get-tuple-element.30), channel_id=1, source_target_pairs={{0,4},{4,0},{8,12},{12,8},{16,20},{20,16},{24,28},{28,24},{1,5},{5... | collective-permute-start | bytes 221192 | tf_op jit(solution)/shard_map/ppermute | solution.py:296
  34.7 5.6 %collective-permute-start.16 = (bf16[144,256]{1,0:T(8,128)(2,1)S(1)}, bf16[144,256]{1,0:T(8,128)(2,1)S(1)}, u32[]{:S(2)}, u32[]{:S(2)}) collective-permute-start(bf16[144,256]{1,0:T(8,128)(2,1)S(1)} %add_convert_fusion.2), channel_id=1, source_target_pairs={{0,24},{4,28},{8,16},{12,20},{16,8},{20,12},{24,0},{28,4},{1,25},{... | collective-permute-start | bytes 221192 | tf_op jit(solution)/shard_map/ppermute | solution.py:214
  37.7 4.4 %collective-permute-start.15 = (bf16[144,256]{1,0:T(8,128)(2,1)S(1)}, bf16[144,256]{1,0:T(8,128)(2,1)S(1)}, u32[]{:S(2)}, u32[]{:S(2)}) collective-permute-start(bf16[144,256]{1,0:T(8,128)(2,1)S(1)} %add_convert_fusion.2), channel_id=1, source_target_pairs={{0,16},{4,20},{8,24},{12,28},{16,0},{20,4},{24,8},{28,12},{1,17},{... | collective-permute-start | bytes 221192 | tf_op jit(solution)/shard_map/ppermute | solution.py:213
  37.7 4.4 %collective-permute-start.14 = (bf16[144,256]{1,0:T(8,128)(2,1)S(1)}, bf16[144,256]{1,0:T(8,128)(2,1)S(1)}, u32[]{:S(2)}, u32[]{:S(2)}) collective-permute-start(bf16[144,256]{1,0:T(8,128)(2,1)S(1)} %add_convert_fusion.2), channel_id=1, source_target_pairs={{0,8},{4,12},{8,0},{12,4},{16,24},{20,28},{24,16},{28,20},{1,9},{5... | collective-permute-start | bytes 221192 | tf_op jit(solution)/shard_map/ppermute | solution.py:209
  42.1 7.1 %collective-permute-start.19 = (bf16[144,256]{1,0:T(8,128)(2,1)S(1)}, bf16[144,256]{1,0:T(8,128)(2,1)S(1)}, u32[]{:S(2)}, u32[]{:S(2)}) collective-permute-start(bf16[144,256]{1,0:T(8,128)(2,1)S(1)} %add_convert_fusion.1), channel_id=1, source_target_pairs={{0,3},{1,2},{2,1},{3,0},{4,7},{5,6},{6,5},{7,4},{8,11},{9,10},{10,... | collective-permute-start | bytes 221192 | tf_op jit(solution)/shard_map/ppermute | solution.py:214
  43.6 7.3 %collective-permute-start.18 = (bf16[144,256]{1,0:T(8,128)(2,1)S(1)}, bf16[144,256]{1,0:T(8,128)(2,1)S(1)}, u32[]{:S(2)}, u32[]{:S(2)}) collective-permute-start(bf16[144,256]{1,0:T(8,128)(2,1)S(1)} %add_convert_fusion.1), channel_id=1, source_target_pairs={{0,2},{1,3},{2,0},{3,1},{4,6},{5,7},{6,4},{7,5},{8,10},{9,11},{10,... | collective-permute-start | bytes 221192 | tf_op jit(solution)/shard_map/ppermute | solution.py:213
  44.9 6.0 %collective-permute-start.17 = (bf16[144,256]{1,0:T(8,128)(2,1)S(1)}, bf16[144,256]{1,0:T(8,128)(2,1)S(1)}, u32[]{:S(2)}, u32[]{:S(2)}) collective-permute-start(bf16[144,256]{1,0:T(8,128)(2,1)S(1)} %add_convert_fusion.1), channel_id=1, source_target_pairs={{0,1},{1,0},{2,3},{3,2},{4,5},{5,4},{6,7},{7,6},{8,9},{9,8},{10,11... | collective-permute-start | bytes 221192 | tf_op jit(solution)/shard_map/ppermute | solution.py:209
  51.0 1.3 %collective-permute-start.20 = (bf16[144,256]{1,0:T(8,128)(2,1)S(1)}, bf16[144,256]{1,0:T(8,128)(2,1)S(1)}, u32[]{:S(2)}, u32[]{:S(2)}) collective-permute-start(bf16[144,256]{1,0:T(8,128)(2,1)S(1)} %add_convert_fusion.mine_ref), channel_id=1, source_target_pairs={{0,4},{4,0},{8,12},{12,8},{16,20},{20,16},{24,28},{28,24},{1,5},{5... | collective-permute-start | bytes 221192 | tf_op jit(solution)/shard_map/ppermute | solution.py:299

commit v8 on v7

--- a/solution.py
+++ b/solution.py
@@ -40,7 +40,7 @@
         in_specs=in_specs,
         out_specs=jax.tree.map(lambda each: VMEM, out_shape),
         scratch_shapes=[pltpu.VMEM(each.shape, each.dtype) for each in scratch] + list(small),
-        compiler_params=pltpu.CompilerParams(vmem_limit_bytes=size + spare * 1024 * 1024),
+        compiler_params=pltpu.CompilerParams(vmem_limit_bytes=size + int(spare * 1024) * 1024),
         name=name,
     )(*inputs)
 
@@ -235,7 +235,7 @@
     outgoing = local_call(
         lambda *refs: scale_kernel(sections, *refs), "scale",
         (features, degree_row), [HBM] * 2, (half, half), (features, degree_row),
-        [pltpu.SemaphoreType.DMA((2,))], 58,
+        [pltpu.SemaphoreType.DMA((2,))], 53.375,
     )
     arrived = []
     for flip, part in enumerate(outgoing):

time: 53.2 us -> 53 us (level)
  Pallas kernels: 4.34 us -> 3.63 us
  local copies, waits for them, and re-layouts: 1.07 us -> 1.77 us
    pallas_call x6, Pallas kernels: 4.34 us -> 3.63 us  [local_call(): pl.pallas_call(kernel, out_shape=out_shape, in_specs=in_specs, out_specs=...]
    unnamed x16, local copies, waits for them, and re-layouts: 1.07 us -> 1.77 us
where the time goes in v8:
time: 53 us; the launch traced here: 52.8 us
  starting transfers between devices  25.4 us (48%)
  waiting for transfers between devices  21.1 us (40%)
  Pallas kernels  3.63 us (7%)
  local copies, waits for them, and re-layouts  1.77 us (3%)
  between operations  0.76 us (1%)
    ppermute x2, starting transfers between devices, on_device(): arrived.append(lax.ppermute(part, ('dom', 'rep'), moves))  5.2 us
    ppermute x2, starting transfers between devices, exchange_sum(): third = lax.ppermute(value, axis, xor_pairs(size, now[0] ^ now[1]))  4.81 us
    ppermute x3, waiting for transfers between devices, on_device(): parts.append(lax.ppermute(partials[mask], 'rep', xor_pairs(rep_size, mask)))  4.59 us
    ppermute x2, waiting for transfers between devices, exchange_sum(): third = lax.ppermute(value, axis, xor_pairs(size, now[0] ^ now[1]))  4.5 us
    ppermute x3, waiting for transfers between devices, on_device(): pieces[mask] = lax.ppermute(pieces[0], 'dom', xor_pairs(dom_size, mask))  4.48 us
    ppermute x3, starting transfers between devices, on_device(): parts.append(lax.ppermute(partials[mask], 'rep', xor_pairs(rep_size, mask)))  4.45 us
    ppermute x3, starting transfers between devices, on_device(): pieces[mask] = lax.ppermute(pieces[0], 'dom', xor_pairs(dom_size, mask))  4.03 us
    pallas_call x6, Pallas kernels, local_call(): pl.pallas_call(kernel, out_shape=out_shape, in_specs=in_specs, out_specs=...  3.63 us
  transfers between devices with their start and end apart: 21, of which 13 were waited for; matrix products, arithmetic and copies ran while one was open for 0% of the time, Pallas kernels for 2%

profile of v8, /device:TPU:0, one launch (start us, length us, event | category | flops | bytes accessed | tf_op | source)
XLA Modules:
  0.0 52.8 jit_solution(9466909069635691986)
XLA Ops:
  0.6 0.7 %copy-done.4 = s32[256]{0:T(256)S(1)} copy-done((s32[256]{0:T(256)S(1)}, s32[256]{0:T(256)}, u32[]{:S(2)}) %copy-start.4) | copy-done | bytes 1048
  1.4 1.0 %scale.1 = (bf16[256,128]{1,0:T(8,128)(2,1)S(1)}, bf16[256,128]{1,0:T(8,128)(2,1)S(1)}) custom-call(bf16[256,256]{1,0:T(8,128)(2,1)} %refs_0_.3, s32[1,256]{1,0:T(1,128)S(1)} %bitcast.3), custom_call_target="tpu_custom_call" | custom-call | tf_op jit(solution)/shard_map/scale/pallas_call | solution.py:37
  2.3 3.9 %collective-permute-start.1 = (bf16[256,128]{1,0:T(8,128)(2,1)S(1)}, bf16[256,128]{1,0:T(8,128)(2,1)S(1)}, u32[]{:S(2)}, u32[]{:S(2)}) collective-permute-start(bf16[256,128]{1,0:T(8,128)(2,1)S(1)} %get-tuple-element.20), channel_id=1, source_target_pairs={{0,24},{1,16},{2,8},{3,0},{4,28},{5,20},{6,12},{7,4},{8,1},{9,17},... | collective-permute-start | bytes 196616 | tf_op jit(solution)/shard_map/ppermute | solution.py:248
  6.3 1.3 %collective-permute-start.2 = (bf16[256,128]{1,0:T(8,128)(2,1)S(1)}, bf16[256,128]{1,0:T(8,128)(2,1)S(1)}, u32[]{:S(2)}, u32[]{:S(2)}) collective-permute-start(bf16[256,128]{1,0:T(8,128)(2,1)S(1)} %get-tuple-element.21), channel_id=1, source_target_pairs={{0,3},{1,11},{2,19},{3,27},{4,7},{5,15},{6,23},{7,31},{8,10},{9,2}... | collective-permute-start | bytes 196616 | tf_op jit(solution)/shard_map/ppermute | solution.py:248
  7.6 1.0 %copy-done = s32[1,2,4,128,128]{4,3,2,1,0:T(8,128)S(1)} copy-done((s32[1,2,4,128,128]{4,3,2,1,0:T(8,128)S(1)}, s32[1,2,4,128,128]{4,3,2,1,0:T(8,128)}, u32[]{:S(2)}) %copy-start) | copy-done | bytes 524312
  8.6 0.8 %prepare.1 = (bf16[1040,128]{1,0:T(8,128)(2,1)S(1)}, bf16[256,256]{1,0:T(8,128)(2,1)S(1)}, f32[256,128]{1,0:T(8,128)S(1)}, f32[1,256]{1,0:T(1,128)S(1)}) custom-call(s32[1,2,4,128,128]{4,3,2,1,0:T(8,128)S(1)} %copy-done, s32[1,2,4]{2,1,0:T(2,128)S(1)} %copy-done.5, s32[1,2,4]{2,1,0:T(2,128)S(1)} %copy-done.6, bf16[256,256]{1,0:T(8,128)(2,1)S(1)} %copy-done.1, ...), custom_call_target="tpu_custom_call" | custom-call | tf_op jit(solution)/shard_map/prepare/pallas_call | solution.py:37
  9.4 2.9 %collective-permute-start = (bf16[1040,128]{1,0:T(8,128)(2,1)S(1)}, bf16[1040,128]{1,0:T(8,128)(2,1)S(1)}, u32[]{:S(2)}, u32[]{:S(2)}) collective-permute-start(bf16[1040,128]{1,0:T(8,128)(2,1)S(1)} %get-tuple-element.19.refs_0_), channel_id=1, source_target_pairs={{0,3},{1,2},{2,1},{3,0},{4,7},{5,6},{6,5},{7,4},{8,11},{9,10},{10,... | collective-permute-start | bytes 798728 | tf_op jit(solution)/shard_map/ppermute | solution.py:261
  12.8 3.4 %collective-permute-start.8 = (bf16[512,128]{1,0:T(8,128)(2,1)S(1)}, bf16[512,128]{1,0:T(8,128)(2,1)S(1)}, u32[]{:S(2)}, u32[]{:S(2)}) collective-permute-start(bf16[512,128]{1,0:T(8,128)(2,1)S(1)} %join.1.refs_2_), channel_id=1, source_target_pairs={{0,24},{4,28},{8,16},{12,20},{16,8},{20,12},{24,0},{28,4},{1,25},{... | collective-permute-start | bytes 393224 | tf_op jit(solution)/shard_map/ppermute | solution.py:269
  16.2 0.6 %collective-permute-start.4 = (bf16[512,128]{1,0:T(8,128)(2,1)S(1)}, bf16[512,128]{1,0:T(8,128)(2,1)S(1)}, u32[]{:S(2)}, u32[]{:S(2)}) collective-permute-start(bf16[512,128]{1,0:T(8,128)(2,1)S(1)} %join.1.refs_2_), channel_id=1, source_target_pairs={{0,8},{4,12},{8,0},{12,4},{16,24},{20,28},{24,16},{28,20},{1,9},{5... | collective-permute-start | bytes 393224 | tf_op jit(solution)/shard_map/ppermute | solution.py:269
  16.8 3.2 %collective-permute-done.8.refs_8_ = bf16[512,128]{1,0:T(8,128)(2,1)S(1)} collective-permute-done((bf16[512,128]{1,0:T(8,128)(2,1)S(1)}, bf16[512,128]{1,0:T(8,128)(2,1)S(1)}, u32[]{:S(2)}, u32[]{:S(2)}) %collective-permute-start.8) | collective-permute-done | bytes 131104 | tf_op jit(solution)/shard_map/ppermute | solution.py:269
  20.0 1.2 %collective-permute-done.6.refs_6_ = bf16[512,128]{1,0:T(8,128)(2,1)S(1)} collective-permute-done((bf16[512,128]{1,0:T(8,128)(2,1)S(1)}, bf16[512,128]{1,0:T(8,128)(2,1)S(1)}, u32[]{:S(2)}, u32[]{:S(2)}) %collective-permute-start.6) | collective-permute-done | bytes 131104 | tf_op jit(solution)/shard_map/ppermute | solution.py:269
  21.3 0.5 collective-permute-start.5
  21.8 0.8 %collective-permute-done.7.refs_7_ = bf16[512,128]{1,0:T(8,128)(2,1)S(1)} collective-permute-done((bf16[512,128]{1,0:T(8,128)(2,1)S(1)}, bf16[512,128]{1,0:T(8,128)(2,1)S(1)}, u32[]{:S(2)}, u32[]{:S(2)}) %collective-permute-start.7) | collective-permute-done | bytes 131104 | tf_op jit(solution)/shard_map/ppermute | solution.py:271
  22.8 0.6 %aggregate.1 = (bf16[256,128]{1,0:T(8,128)(2,1)S(1)}, bf16[256,128]{1,0:T(8,128)(2,1)S(1)}, bf16[256,128]{1,0:T(8,128)(2,1)S(1)}, bf16[256,128]{1,0:T(8,128)(2,1)S(1)}) custom-call(bf16[1040,128]{1,0:T(8,128)(2,1)S(1)} %get-tuple-element.19.refs_0_, bf16[1040,128]{1,0:T(8,128)(2,1)S(1)} %collective-permute-done.refs_1_, bf16[512,128]{1,0:T(8,128)(2,1)S(1)} %join.1.refs_2_, ...), custom_call_target="tpu_custom_call" | custom-call | tf_op jit(solution)/shard_map/aggregate/pallas_call | solution.py:37
  23.4 1.8 %collective-permute-start.10 = (bf16[256,128]{1,0:T(8,128)(2,1)S(1)}, bf16[256,128]{1,0:T(8,128)(2,1)S(1)}, u32[]{:S(2)}, u32[]{:S(2)}) collective-permute-start(bf16[256,128]{1,0:T(8,128)(2,1)S(1)} %get-tuple-element.23), channel_id=1, source_target_pairs={{0,1},{1,0},{2,3},{3,2},{4,5},{5,4},{6,7},{7,6},{8,9},{9,8},{10,11... | collective-permute-start | bytes 196616 | tf_op jit(solution)/shard_map/ppermute | solution.py:285
  25.2 0.9 %collective-permute-start.11 = (bf16[256,128]{1,0:T(8,128)(2,1)S(1)}, bf16[256,128]{1,0:T(8,128)(2,1)S(1)}, u32[]{:S(2)}, u32[]{:S(2)}) collective-permute-start(bf16[256,128]{1,0:T(8,128)(2,1)S(1)} %get-tuple-element.24), channel_id=1, source_target_pairs={{0,2},{1,3},{2,0},{3,1},{4,6},{5,7},{6,4},{7,5},{8,10},{9,11},{10,... | collective-permute-start | bytes 196616 | tf_op jit(solution)/shard_map/ppermute | solution.py:285
  26.0 1.8 %collective-permute-start.12 = (bf16[256,128]{1,0:T(8,128)(2,1)S(1)}, bf16[256,128]{1,0:T(8,128)(2,1)S(1)}, u32[]{:S(2)}, u32[]{:S(2)}) collective-permute-start(bf16[256,128]{1,0:T(8,128)(2,1)S(1)} %get-tuple-element.25), channel_id=1, source_target_pairs={{0,3},{1,2},{2,1},{3,0},{4,7},{5,6},{6,5},{7,4},{8,11},{9,10},{10,... | collective-permute-start | bytes 196616 | tf_op jit(solution)/shard_map/ppermute | solution.py:285
  27.8 0.6 %collective-permute-done.10.refs_1_ = bf16[256,128]{1,0:T(8,128)(2,1)S(1)} collective-permute-done((bf16[256,128]{1,0:T(8,128)(2,1)S(1)}, bf16[256,128]{1,0:T(8,128)(2,1)S(1)}, u32[]{:S(2)}, u32[]{:S(2)}) %collective-permute-start.10) | collective-permute-done | bytes 65568 | tf_op jit(solution)/shard_map/ppermute | solution.py:285
  28.5 3.9 %collective-permute-done.11.refs_2_ = bf16[256,128]{1,0:T(8,128)(2,1)S(1)} collective-permute-done((bf16[256,128]{1,0:T(8,128)(2,1)S(1)}, bf16[256,128]{1,0:T(8,128)(2,1)S(1)}, u32[]{:S(2)}, u32[]{:S(2)}) %collective-permute-start.11) | collective-permute-done | bytes 65568 | tf_op jit(solution)/shard_map/ppermute | solution.py:285
  32.4 0.5 %dense.1 = (bf16[256,256]{1,0:T(8,128)(2,1)S(1)}, f32[144,256]{1,0:T(8,128)S(1)}, bf16[144,256]{1,0:T(8,128)(2,1)S(1)}) custom-call(bf16[256,128]{1,0:T(8,128)(2,1)S(1)} %get-tuple-element.22.refs_0_, bf16[256,128]{1,0:T(8,128)(2,1)S(1)} %collective-permute-done.10.refs_1_, bf16[256,128]{1,0:T(8,128)(2,1)S(1)} %collective-permute-done.11.refs_2_, ...), custom_call_target="tpu_custom_call" | custom-call | tf_op jit(solution)/shard_map/dense/pallas_call | solution.py:37
  33.1 1.3 %collective-permute-done.13 = bf16[144,256]{1,0:T(8,128)(2,1)S(1)} collective-permute-done((bf16[144,256]{1,0:T(8,128)(2,1)S(1)}, bf16[144,256]{1,0:T(8,128)(2,1)S(1)}, u32[]{:S(2)}, u32[]{:S(2)}) %collective-permute-start.13) | collective-permute-done | bytes 73760 | tf_op jit(solution)/shard_map/ppermute | solution.py:296
  34.3 3.0 %collective-permute-start.16 = (bf16[144,256]{1,0:T(8,128)(2,1)S(1)}, bf16[144,256]{1,0:T(8,128)(2,1)S(1)}, u32[]{:S(2)}, u32[]{:S(2)}) collective-permute-start(bf16[144,256]{1,0:T(8,128)(2,1)S(1)} %add_convert_fusion.2), channel_id=1, source_target_pairs={{0,24},{4,28},{8,16},{12,20},{16,8},{20,12},{24,0},{28,4},{1,25},{... | collective-permute-start | bytes 221192 | tf_op jit(solution)/shard_map/ppermute | solution.py:214
  37.4 0.6 %collective-permute-start.14 = (bf16[144,256]{1,0:T(8,128)(2,1)S(1)}, bf16[144,256]{1,0:T(8,128)(2,1)S(1)}, u32[]{:S(2)}, u32[]{:S(2)}) collective-permute-start(bf16[144,256]{1,0:T(8,128)(2,1)S(1)} %add_convert_fusion.2), channel_id=1, source_target_pairs={{0,8},{4,12},{8,0},{12,4},{16,24},{20,28},{24,16},{28,20},{1,9},{5... | collective-permute-start | bytes 221192 | tf_op jit(solution)/shard_map/ppermute | solution.py:209
  38.0 2.0 %collective-permute-done.16 = bf16[144,256]{1,0:T(8,128)(2,1)S(1)} collective-permute-done((bf16[144,256]{1,0:T(8,128)(2,1)S(1)}, bf16[144,256]{1,0:T(8,128)(2,1)S(1)}, u32[]{:S(2)}, u32[]{:S(2)}) %collective-permute-start.16) | collective-permute-done | bytes 73760 | tf_op jit(solution)/shard_map/ppermute | solution.py:214
  40.0 1.7 %collective-permute-done.15 = bf16[144,256]{1,0:T(8,128)(2,1)S(1)} collective-permute-done((bf16[144,256]{1,0:T(8,128)(2,1)S(1)}, bf16[144,256]{1,0:T(8,128)(2,1)S(1)}, u32[]{:S(2)}, u32[]{:S(2)}) %collective-permute-start.15) | collective-permute-done | bytes 73760 | tf_op jit(solution)/shard_map/ppermute | solution.py:213
  41.8 1.8 %collective-permute-start.19 = (bf16[144,256]{1,0:T(8,128)(2,1)S(1)}, bf16[144,256]{1,0:T(8,128)(2,1)S(1)}, u32[]{:S(2)}, u32[]{:S(2)}) collective-permute-start(bf16[144,256]{1,0:T(8,128)(2,1)S(1)} %add_convert_fusion.1), channel_id=1, source_target_pairs={{0,3},{1,2},{2,1},{3,0},{4,7},{5,6},{6,5},{7,4},{8,11},{9,10},{10,... | collective-permute-start | bytes 221192 | tf_op jit(solution)/shard_map/ppermute | solution.py:214
  43.6 1.0 %collective-permute-start.18 = (bf16[144,256]{1,0:T(8,128)(2,1)S(1)}, bf16[144,256]{1,0:T(8,128)(2,1)S(1)}, u32[]{:S(2)}, u32[]{:S(2)}) collective-permute-start(bf16[144,256]{1,0:T(8,128)(2,1)S(1)} %add_convert_fusion.1), channel_id=1, source_target_pairs={{0,2},{1,3},{2,0},{3,1},{4,6},{5,7},{6,4},{7,5},{8,10},{9,11},{10,... | collective-permute-start | bytes 221192 | tf_op jit(solution)/shard_map/ppermute | solution.py:213
  44.6 1.7 %collective-permute-start.17 = (bf16[144,256]{1,0:T(8,128)(2,1)S(1)}, bf16[144,256]{1,0:T(8,128)(2,1)S(1)}, u32[]{:S(2)}, u32[]{:S(2)}) collective-permute-start(bf16[144,256]{1,0:T(8,128)(2,1)S(1)} %add_convert_fusion.1), channel_id=1, source_target_pairs={{0,1},{1,0},{2,3},{3,2},{4,5},{5,4},{6,7},{7,6},{8,9},{9,8},{10,11... | collective-permute-start | bytes 221192 | tf_op jit(solution)/shard_map/ppermute | solution.py:209
  46.2 2.5 %collective-permute-done.19 = bf16[144,256]{1,0:T(8,128)(2,1)S(1)} collective-permute-done((bf16[144,256]{1,0:T(8,128)(2,1)S(1)}, bf16[144,256]{1,0:T(8,128)(2,1)S(1)}, u32[]{:S(2)}, u32[]{:S(2)}) %collective-permute-start.19) | collective-permute-done | bytes 73760 | tf_op jit(solution)/shard_map/ppermute | solution.py:214
  48.8 1.9 %collective-permute-done.18 = bf16[144,256]{1,0:T(8,128)(2,1)S(1)} collective-permute-done((bf16[144,256]{1,0:T(8,128)(2,1)S(1)}, bf16[144,256]{1,0:T(8,128)(2,1)S(1)}, u32[]{:S(2)}, u32[]{:S(2)}) %collective-permute-start.18) | collective-permute-done | bytes 73760 | tf_op jit(solution)/shard_map/ppermute | solution.py:213
  50.7 1.3 %collective-permute-done.20.other_ref = bf16[144,256]{1,0:T(8,128)(2,1)S(1)} collective-permute-done((bf16[144,256]{1,0:T(8,128)(2,1)S(1)}, bf16[144,256]{1,0:T(8,128)(2,1)S(1)}, u32[]{:S(2)}, u32[]{:S(2)}) %collective-permute-start.20) | collective-permute-done | bytes 73760 | tf_op jit(solution)/shard_map/ppermute | solution.py:299
  52.0 0.8 %finish.1 = (f32[256,256]{1,0:T(8,128)}, f32[1,256]{1,0:T(1,128)}, bf16[256,256]{1,0:T(8,128)(2,1)}) custom-call(bf16[144,256]{1,0:T(8,128)(2,1)S(1)} %add_convert_fusion.mine_ref, bf16[144,256]{1,0:T(8,128)(2,1)S(1)} %collective-permute-done.20.other_ref, bf16[256,256]{1,0:T(8,128)(2,1)S(1)} %get-tuple-element.31.outcome_ref), custom_call_target="tpu_custom_call" | custom-call | tf_op jit(solution)/shard_map/finish/pallas_call | solution.py:37
  (35 shorter events, 0.9 us)
Async XLA Ops:
  0.6 6.9 %copy-start.1 = (bf16[256,256]{1,0:T(8,128)(2,1)S(1)}, bf16[256,256]{1,0:T(8,128)(2,1)}, u32[]{:S(2)}) copy-start(bf16[256,256]{1,0:T(8,128)(2,1)} %refs_0_.3) | copy-start | bytes 393220
  0.6 0.7 %copy-start.4 = (s32[256]{0:T(256)S(1)}, s32[256]{0:T(256)}, u32[]{:S(2)}) copy-start(s32[256]{0:T(256)} %param.10) | copy-start | bytes 3076
  2.3 10.0 %collective-permute-start.1 = (bf16[256,128]{1,0:T(8,128)(2,1)S(1)}, bf16[256,128]{1,0:T(8,128)(2,1)S(1)}, u32[]{:S(2)}, u32[]{:S(2)}) collective-permute-start(bf16[256,128]{1,0:T(8,128)(2,1)S(1)} %get-tuple-element.20), channel_id=1, source_target_pairs={{0,24},{1,16},{2,8},{3,0},{4,28},{5,20},{6,12},{7,4},{8,1},{9,17},... | collective-permute-start | bytes 196616 | tf_op jit(solution)/shard_map/ppermute | solution.py:248
  6.3 1.3 %copy-start.6 = (s32[1,2,4]{2,1,0:T(2,128)S(1)}, s32[1,2,4]{2,1,0:T(2,128)}, u32[]{:S(2)}) copy-start(s32[1,2,4]{2,1,0:T(2,128)} %refs_2_.1) | copy-start | bytes 100
  6.3 1.3 %copy-start.7 = (f32[256]{0:T(256)S(1)}, f32[256]{0:T(256)}, u32[]{:S(2)}) copy-start(f32[256]{0:T(256)} %param.15) | copy-start | bytes 3076
  6.3 1.3 %copy-start.5 = (s32[1,2,4]{2,1,0:T(2,128)S(1)}, s32[1,2,4]{2,1,0:T(2,128)}, u32[]{:S(2)}) copy-start(s32[1,2,4]{2,1,0:T(2,128)} %refs_1_.1) | copy-start | bytes 100
  6.3 6.4 %collective-permute-start.2 = (bf16[256,128]{1,0:T(8,128)(2,1)S(1)}, bf16[256,128]{1,0:T(8,128)(2,1)S(1)}, u32[]{:S(2)}, u32[]{:S(2)}) collective-permute-start(bf16[256,128]{1,0:T(8,128)(2,1)S(1)} %get-tuple-element.21), channel_id=1, source_target_pairs={{0,3},{1,11},{2,19},{3,27},{4,7},{5,15},{6,23},{7,31},{8,10},{9,2}... | collective-permute-start | bytes 196616 | tf_op jit(solution)/shard_map/ppermute | solution.py:248
  7.5 1.0 %copy-start = (s32[1,2,4,128,128]{4,3,2,1,0:T(8,128)S(1)}, s32[1,2,4,128,128]{4,3,2,1,0:T(8,128)}, u32[]{:S(2)}) copy-start(s32[1,2,4,128,128]{4,3,2,1,0:T(8,128)} %refs_0_.2) | copy-start | bytes 1572868
  9.4 12.4 %collective-permute-start = (bf16[1040,128]{1,0:T(8,128)(2,1)S(1)}, bf16[1040,128]{1,0:T(8,128)(2,1)S(1)}, u32[]{:S(2)}, u32[]{:S(2)}) collective-permute-start(bf16[1040,128]{1,0:T(8,128)(2,1)S(1)} %get-tuple-element.19.refs_0_), channel_id=1, source_target_pairs={{0,3},{1,2},{2,1},{3,0},{4,7},{5,6},{6,5},{7,4},{8,11},{9,10},{10,... | collective-permute-start | bytes 798728 | tf_op jit(solution)/shard_map/ppermute | solution.py:261
  12.7 19.7 %copy-start.2 = (bf16[256,256]{1,0:T(8,128)(2,1)S(1)}, bf16[256,256]{1,0:T(8,128)(2,1)}, u32[]{:S(2)}) copy-start(bf16[256,256]{1,0:T(8,128)(2,1)} %refs_6_.1) | copy-start | bytes 393220
  12.8 19.7 %copy-start.3 = (bf16[256,256]{1,0:T(8,128)(2,1)S(1)}, bf16[256,256]{1,0:T(8,128)(2,1)}, u32[]{:S(2)}) copy-start(bf16[256,256]{1,0:T(8,128)(2,1)} %refs_8_.1) | copy-start | bytes 393220
  12.8 7.3 %collective-permute-start.8 = (bf16[512,128]{1,0:T(8,128)(2,1)S(1)}, bf16[512,128]{1,0:T(8,128)(2,1)S(1)}, u32[]{:S(2)}, u32[]{:S(2)}) collective-permute-start(bf16[512,128]{1,0:T(8,128)(2,1)S(1)} %join.1.refs_2_), channel_id=1, source_target_pairs={{0,24},{4,28},{8,16},{12,20},{16,8},{20,12},{24,0},{28,4},{1,25},{... | collective-permute-start | bytes 393224 | tf_op jit(solution)/shard_map/ppermute | solution.py:269
  16.2 5.1 %collective-permute-start.6 = (bf16[512,128]{1,0:T(8,128)(2,1)S(1)}, bf16[512,128]{1,0:T(8,128)(2,1)S(1)}, u32[]{:S(2)}, u32[]{:S(2)}) collective-permute-start(bf16[512,128]{1,0:T(8,128)(2,1)S(1)} %join.1.refs_2_), channel_id=1, source_target_pairs={{0,16},{4,20},{8,24},{12,28},{16,0},{20,4},{24,8},{28,12},{1,17},{... | collective-permute-start | bytes 393224 | tf_op jit(solution)/shard_map/ppermute | solution.py:269
  16.2 5.1 %collective-permute-start.4 = (bf16[512,128]{1,0:T(8,128)(2,1)S(1)}, bf16[512,128]{1,0:T(8,128)(2,1)S(1)}, u32[]{:S(2)}, u32[]{:S(2)}) collective-permute-start(bf16[512,128]{1,0:T(8,128)(2,1)S(1)} %join.1.refs_2_), channel_id=1, source_target_pairs={{0,8},{4,12},{8,0},{12,4},{16,24},{20,28},{24,16},{28,20},{1,9},{5... | collective-permute-start | bytes 393224 | tf_op jit(solution)/shard_map/ppermute | solution.py:269
  16.8 5.0 %collective-permute-start.3 = (bf16[512,128]{1,0:T(8,128)(2,1)S(1)}, bf16[512,128]{1,0:T(8,128)(2,1)S(1)}, u32[]{:S(2)}, u32[]{:S(2)}) collective-permute-start(bf16[512,128]{1,0:T(8,128)(2,1)S(1)} %join.1.refs_2_), channel_id=1, source_target_pairs={{0,4},{4,0},{8,12},{12,8},{16,20},{20,16},{24,28},{28,24},{1,5},{5... | collective-permute-start | bytes 393224 | tf_op jit(solution)/shard_map/ppermute | solution.py:271
  20.0 1.8 %collective-permute-start.9 = (bf16[512,128]{1,0:T(8,128)(2,1)S(1)}, bf16[512,128]{1,0:T(8,128)(2,1)S(1)}, u32[]{:S(2)}, u32[]{:S(2)}) collective-permute-start(bf16[512,128]{1,0:T(8,128)(2,1)S(1)} %collective-permute-done.8.refs_8_), channel_id=1, source_target_pairs={{0,4},{4,0},{8,12},{12,8},{16,20},{20,16},{24,28},{28,24},{1,5},{5... | collective-permute-start | bytes 393224 | tf_op jit(solution)/shard_map/ppermute | solution.py:271
  21.3 1.3 %collective-permute-start.7 = (bf16[512,128]{1,0:T(8,128)(2,1)S(1)}, bf16[512,128]{1,0:T(8,128)(2,1)S(1)}, u32[]{:S(2)}, u32[]{:S(2)}) collective-permute-start(bf16[512,128]{1,0:T(8,128)(2,1)S(1)} %collective-permute-done.6.refs_6_), channel_id=1, source_target_pairs={{0,4},{4,0},{8,12},{12,8},{16,20},{20,16},{24,28},{28,24},{1,5},{5... | collective-permute-start | bytes 393224 | tf_op jit(solution)/shard_map/ppermute | solution.py:271
  21.3 1.5 %collective-permute-start.5 = (bf16[512,128]{1,0:T(8,128)(2,1)S(1)}, bf16[512,128]{1,0:T(8,128)(2,1)S(1)}, u32[]{:S(2)}, u32[]{:S(2)}) collective-permute-start(bf16[512,128]{1,0:T(8,128)(2,1)S(1)} %collective-permute-done.4.refs_4_), channel_id=1, source_target_pairs={{0,4},{4,0},{8,12},{12,8},{16,20},{20,16},{24,28},{28,24},{1,5},{5... | collective-permute-start | bytes 393224 | tf_op jit(solution)/shard_map/ppermute | solution.py:271
  23.4 5.1 %collective-permute-start.10 = (bf16[256,128]{1,0:T(8,128)(2,1)S(1)}, bf16[256,128]{1,0:T(8,128)(2,1)S(1)}, u32[]{:S(2)}, u32[]{:S(2)}) collective-permute-start(bf16[256,128]{1,0:T(8,128)(2,1)S(1)} %get-tuple-element.23), channel_id=1, source_target_pairs={{0,1},{1,0},{2,3},{3,2},{4,5},{5,4},{6,7},{7,6},{8,9},{9,8},{10,11... | collective-permute-start | bytes 196616 | tf_op jit(solution)/shard_map/ppermute | solution.py:285
  25.2 7.3 %collective-permute-start.11 = (bf16[256,128]{1,0:T(8,128)(2,1)S(1)}, bf16[256,128]{1,0:T(8,128)(2,1)S(1)}, u32[]{:S(2)}, u32[]{:S(2)}) collective-permute-start(bf16[256,128]{1,0:T(8,128)(2,1)S(1)} %get-tuple-element.24), channel_id=1, source_target_pairs={{0,2},{1,3},{2,0},{3,1},{4,6},{5,7},{6,4},{7,5},{8,10},{9,11},{10,... | collective-permute-start | bytes 196616 | tf_op jit(solution)/shard_map/ppermute | solution.py:285
  26.0 6.4 %collective-permute-start.12 = (bf16[256,128]{1,0:T(8,128)(2,1)S(1)}, bf16[256,128]{1,0:T(8,128)(2,1)S(1)}, u32[]{:S(2)}, u32[]{:S(2)}) collective-permute-start(bf16[256,128]{1,0:T(8,128)(2,1)S(1)} %get-tuple-element.25), channel_id=1, source_target_pairs={{0,3},{1,2},{2,1},{3,0},{4,7},{5,6},{6,5},{7,4},{8,11},{9,10},{10,... | collective-permute-start | bytes 196616 | tf_op jit(solution)/shard_map/ppermute | solution.py:285
  33.0 1.3 %collective-permute-start.13 = (bf16[144,256]{1,0:T(8,128)(2,1)S(1)}, bf16[144,256]{1,0:T(8,128)(2,1)S(1)}, u32[]{:S(2)}, u32[]{:S(2)}) collective-permute-start(bf16[144,256]{1,0:T(8,128)(2,1)S(1)} %get-tuple-element.30), channel_id=1, source_target_pairs={{0,4},{4,0},{8,12},{12,8},{16,20},{20,16},{24,28},{28,24},{1,5},{5... | collective-permute-start | bytes 221192 | tf_op jit(solution)/shard_map/ppermute | solution.py:296
  34.3 5.7 %collective-permute-start.16 = (bf16[144,256]{1,0:T(8,128)(2,1)S(1)}, bf16[144,256]{1,0:T(8,128)(2,1)S(1)}, u32[]{:S(2)}, u32[]{:S(2)}) collective-permute-start(bf16[144,256]{1,0:T(8,128)(2,1)S(1)} %add_convert_fusion.2), channel_id=1, source_target_pairs={{0,24},{4,28},{8,16},{12,20},{16,8},{20,12},{24,0},{28,4},{1,25},{... | collective-permute-start | bytes 221192 | tf_op jit(solution)/shard_map/ppermute | solution.py:214
  37.4 4.4 %collective-permute-start.15 = (bf16[144,256]{1,0:T(8,128)(2,1)S(1)}, bf16[144,256]{1,0:T(8,128)(2,1)S(1)}, u32[]{:S(2)}, u32[]{:S(2)}) collective-permute-start(bf16[144,256]{1,0:T(8,128)(2,1)S(1)} %add_convert_fusion.2), channel_id=1, source_target_pairs={{0,16},{4,20},{8,24},{12,28},{16,0},{20,4},{24,8},{28,12},{1,17},{... | collective-permute-start | bytes 221192 | tf_op jit(solution)/shard_map/ppermute | solution.py:213
  37.4 4.4 %collective-permute-start.14 = (bf16[144,256]{1,0:T(8,128)(2,1)S(1)}, bf16[144,256]{1,0:T(8,128)(2,1)S(1)}, u32[]{:S(2)}, u32[]{:S(2)}) collective-permute-start(bf16[144,256]{1,0:T(8,128)(2,1)S(1)} %add_convert_fusion.2), channel_id=1, source_target_pairs={{0,8},{4,12},{8,0},{12,4},{16,24},{20,28},{24,16},{28,20},{1,9},{5... | collective-permute-start | bytes 221192 | tf_op jit(solution)/shard_map/ppermute | solution.py:209
  41.8 7.0 %collective-permute-start.19 = (bf16[144,256]{1,0:T(8,128)(2,1)S(1)}, bf16[144,256]{1,0:T(8,128)(2,1)S(1)}, u32[]{:S(2)}, u32[]{:S(2)}) collective-permute-start(bf16[144,256]{1,0:T(8,128)(2,1)S(1)} %add_convert_fusion.1), channel_id=1, source_target_pairs={{0,3},{1,2},{2,1},{3,0},{4,7},{5,6},{6,5},{7,4},{8,11},{9,10},{10,... | collective-permute-start | bytes 221192 | tf_op jit(solution)/shard_map/ppermute | solution.py:214
  43.6 7.1 %collective-permute-start.18 = (bf16[144,256]{1,0:T(8,128)(2,1)S(1)}, bf16[144,256]{1,0:T(8,128)(2,1)S(1)}, u32[]{:S(2)}, u32[]{:S(2)}) collective-permute-start(bf16[144,256]{1,0:T(8,128)(2,1)S(1)} %add_convert_fusion.1), channel_id=1, source_target_pairs={{0,2},{1,3},{2,0},{3,1},{4,6},{5,7},{6,4},{7,5},{8,10},{9,11},{10,... | collective-permute-start | bytes 221192 | tf_op jit(solution)/shard_map/ppermute | solution.py:213
  44.6 6.0 %collective-permute-start.17 = (bf16[144,256]{1,0:T(8,128)(2,1)S(1)}, bf16[144,256]{1,0:T(8,128)(2,1)S(1)}, u32[]{:S(2)}, u32[]{:S(2)}) collective-permute-start(bf16[144,256]{1,0:T(8,128)(2,1)S(1)} %add_convert_fusion.1), channel_id=1, source_target_pairs={{0,1},{1,0},{2,3},{3,2},{4,5},{5,4},{6,7},{7,6},{8,9},{9,8},{10,11... | collective-permute-start | bytes 221192 | tf_op jit(solution)/shard_map/ppermute | solution.py:209
  50.7 1.3 %collective-permute-start.20 = (bf16[144,256]{1,0:T(8,128)(2,1)S(1)}, bf16[144,256]{1,0:T(8,128)(2,1)S(1)}, u32[]{:S(2)}, u32[]{:S(2)}) collective-permute-start(bf16[144,256]{1,0:T(8,128)(2,1)S(1)} %add_convert_fusion.mine_ref), channel_id=1, source_target_pairs={{0,4},{4,0},{8,12},{12,8},{16,20},{20,16},{24,28},{28,24},{1,5},{5... | collective-permute-start | bytes 221192 | tf_op jit(solution)/shard_map/ppermute | solution.py:299

commit v9 on v8

--- a/solution.py
+++ b/solution.py
@@ -14,7 +14,7 @@
 GELU_C = 0.7978845608028654
 
 
-ASIDE = ((3, 2, 1, 0), (1, 3, 2, 0), (0, 1, 3, 2), (0, 1, 2, 3))
+ASIDE = ((3, 2, 1, 0), (1, 2, 3, 0), (0, 3, 1, 2), (0, 1, 2, 3))
 ASIDE_BITS = sum(
     to << (2 * (4 * plane + rep)) for plane, row in enumerate(ASIDE) for rep, to in enumerate(row)
 )

time: 53 us -> 53 us (level)
  transfers between devices with their start and end apart: 21 -> 21, of which waited for: 13 -> 14; matrix products, arithmetic and copies ran while one was open for 0% -> 0% of each run, Pallas kernels for 2% -> 2%
where the time goes in v9:
time: 53 us; the launch traced here: 52.8 us
  starting transfers between devices  25.3 us (48%)
  waiting for transfers between devices  21.2 us (40%)
  Pallas kernels  3.63 us (7%)
  local copies, waits for them, and re-layouts  1.77 us (3%)
  between operations  0.76 us (1%)
    ppermute x2, starting transfers between devices, on_device(): arrived.append(lax.ppermute(part, ('dom', 'rep'), moves))  5.2 us
    ppermute x2, starting transfers between devices, exchange_sum(): third = lax.ppermute(value, axis, xor_pairs(size, now[0] ^ now[1]))  5.16 us
    ppermute x3, waiting for transfers between devices, on_device(): parts.append(lax.ppermute(partials[mask], 'rep', xor_pairs(rep_size, mask)))  4.67 us
    ppermute x2, waiting for transfers between devices, exchange_sum(): third = lax.ppermute(value, axis, xor_pairs(size, now[0] ^ now[1]))  4.56 us
    ppermute x3, waiting for transfers between devices, on_device(): pieces[mask] = lax.ppermute(pieces[0], 'dom', xor_pairs(dom_size, mask))  4.48 us
    ppermute x3, starting transfers between devices, on_device(): parts.append(lax.ppermute(partials[mask], 'rep', xor_pairs(rep_size, mask)))  4.45 us
    ppermute x3, starting transfers between devices, on_device(): pieces[mask] = lax.ppermute(pieces[0], 'dom', xor_pairs(dom_size, mask))  4.03 us
    pallas_call x6, Pallas kernels, local_call(): pl.pallas_call(kernel, out_shape=out_shape, in_specs=in_specs, out_specs=...  3.63 us
  transfers between devices with their start and end apart: 21, of which 14 were waited for; matrix products, arithmetic and copies ran while one was open for 0% of the time, Pallas kernels for 2%

profile of v9, /device:TPU:0, one launch (start us, length us, event | category | flops | bytes accessed | tf_op | source)
XLA Modules:
  0.0 52.8 jit_solution(4101823955853642543)
XLA Ops:
  0.6 0.7 %copy-done.4 = s32[256]{0:T(256)S(1)} copy-done((s32[256]{0:T(256)S(1)}, s32[256]{0:T(256)}, u32[]{:S(2)}) %copy-start.4) | copy-done | bytes 1048
  1.4 1.0 %scale.1 = (bf16[256,128]{1,0:T(8,128)(2,1)S(1)}, bf16[256,128]{1,0:T(8,128)(2,1)S(1)}) custom-call(bf16[256,256]{1,0:T(8,128)(2,1)} %refs_0_.3, s32[1,256]{1,0:T(1,128)S(1)} %bitcast.3), custom_call_target="tpu_custom_call" | custom-call | tf_op jit(solution)/shard_map/scale/pallas_call | solution.py:37
  2.3 3.9 %collective-permute-start.1 = (bf16[256,128]{1,0:T(8,128)(2,1)S(1)}, bf16[256,128]{1,0:T(8,128)(2,1)S(1)}, u32[]{:S(2)}, u32[]{:S(2)}) collective-permute-start(bf16[256,128]{1,0:T(8,128)(2,1)S(1)} %get-tuple-element.20), channel_id=1, source_target_pairs={{0,24},{1,16},{2,8},{3,0},{4,28},{5,20},{6,12},{7,4},{8,1},{9,25},... | collective-permute-start | bytes 196616 | tf_op jit(solution)/shard_map/ppermute | solution.py:248
  6.3 1.2 %collective-permute-start.2 = (bf16[256,128]{1,0:T(8,128)(2,1)S(1)}, bf16[256,128]{1,0:T(8,128)(2,1)S(1)}, u32[]{:S(2)}, u32[]{:S(2)}) collective-permute-start(bf16[256,128]{1,0:T(8,128)(2,1)S(1)} %get-tuple-element.21), channel_id=1, source_target_pairs={{0,3},{1,11},{2,19},{3,27},{4,7},{5,15},{6,23},{7,31},{8,10},{9,18... | collective-permute-start | bytes 196616 | tf_op jit(solution)/shard_map/ppermute | solution.py:248
  7.6 1.0 %copy-done = s32[1,2,4,128,128]{4,3,2,1,0:T(8,128)S(1)} copy-done((s32[1,2,4,128,128]{4,3,2,1,0:T(8,128)S(1)}, s32[1,2,4,128,128]{4,3,2,1,0:T(8,128)}, u32[]{:S(2)}) %copy-start) | copy-done | bytes 524312
  8.6 0.8 %prepare.1 = (bf16[1040,128]{1,0:T(8,128)(2,1)S(1)}, bf16[256,256]{1,0:T(8,128)(2,1)S(1)}, f32[256,128]{1,0:T(8,128)S(1)}, f32[1,256]{1,0:T(1,128)S(1)}) custom-call(s32[1,2,4,128,128]{4,3,2,1,0:T(8,128)S(1)} %copy-done, s32[1,2,4]{2,1,0:T(2,128)S(1)} %copy-done.5, s32[1,2,4]{2,1,0:T(2,128)S(1)} %copy-done.6, bf16[256,256]{1,0:T(8,128)(2,1)S(1)} %copy-done.1, ...), custom_call_target="tpu_custom_call" | custom-call | tf_op jit(solution)/shard_map/prepare/pallas_call | solution.py:37
  9.4 2.9 %collective-permute-start = (bf16[1040,128]{1,0:T(8,128)(2,1)S(1)}, bf16[1040,128]{1,0:T(8,128)(2,1)S(1)}, u32[]{:S(2)}, u32[]{:S(2)}) collective-permute-start(bf16[1040,128]{1,0:T(8,128)(2,1)S(1)} %get-tuple-element.19.refs_0_), channel_id=1, source_target_pairs={{0,3},{1,2},{2,1},{3,0},{4,7},{5,6},{6,5},{7,4},{8,11},{9,10},{10,... | collective-permute-start | bytes 798728 | tf_op jit(solution)/shard_map/ppermute | solution.py:261
  12.8 3.4 %collective-permute-start.8 = (bf16[512,128]{1,0:T(8,128)(2,1)S(1)}, bf16[512,128]{1,0:T(8,128)(2,1)S(1)}, u32[]{:S(2)}, u32[]{:S(2)}) collective-permute-start(bf16[512,128]{1,0:T(8,128)(2,1)S(1)} %join.1.refs_2_), channel_id=1, source_target_pairs={{0,24},{4,28},{8,16},{12,20},{16,8},{20,12},{24,0},{28,4},{1,25},{... | collective-permute-start | bytes 393224 | tf_op jit(solution)/shard_map/ppermute | solution.py:269
  16.2 0.6 %collective-permute-start.4 = (bf16[512,128]{1,0:T(8,128)(2,1)S(1)}, bf16[512,128]{1,0:T(8,128)(2,1)S(1)}, u32[]{:S(2)}, u32[]{:S(2)}) collective-permute-start(bf16[512,128]{1,0:T(8,128)(2,1)S(1)} %join.1.refs_2_), channel_id=1, source_target_pairs={{0,8},{4,12},{8,0},{12,4},{16,24},{20,28},{24,16},{28,20},{1,9},{5... | collective-permute-start | bytes 393224 | tf_op jit(solution)/shard_map/ppermute | solution.py:269
  16.8 3.2 %collective-permute-done.8.refs_8_ = bf16[512,128]{1,0:T(8,128)(2,1)S(1)} collective-permute-done((bf16[512,128]{1,0:T(8,128)(2,1)S(1)}, bf16[512,128]{1,0:T(8,128)(2,1)S(1)}, u32[]{:S(2)}, u32[]{:S(2)}) %collective-permute-start.8) | collective-permute-done | bytes 131104 | tf_op jit(solution)/shard_map/ppermute | solution.py:269
  20.0 1.2 %collective-permute-done.6.refs_6_ = bf16[512,128]{1,0:T(8,128)(2,1)S(1)} collective-permute-done((bf16[512,128]{1,0:T(8,128)(2,1)S(1)}, bf16[512,128]{1,0:T(8,128)(2,1)S(1)}, u32[]{:S(2)}, u32[]{:S(2)}) %collective-permute-start.6) | collective-permute-done | bytes 131104 | tf_op jit(solution)/shard_map/ppermute | solution.py:269
  21.3 0.5 collective-permute-start.5
  21.8 0.8 %collective-permute-done.7.refs_7_ = bf16[512,128]{1,0:T(8,128)(2,1)S(1)} collective-permute-done((bf16[512,128]{1,0:T(8,128)(2,1)S(1)}, bf16[512,128]{1,0:T(8,128)(2,1)S(1)}, u32[]{:S(2)}, u32[]{:S(2)}) %collective-permute-start.7) | collective-permute-done | bytes 131104 | tf_op jit(solution)/shard_map/ppermute | solution.py:271
  22.8 0.6 %aggregate.1 = (bf16[256,128]{1,0:T(8,128)(2,1)S(1)}, bf16[256,128]{1,0:T(8,128)(2,1)S(1)}, bf16[256,128]{1,0:T(8,128)(2,1)S(1)}, bf16[256,128]{1,0:T(8,128)(2,1)S(1)}) custom-call(bf16[1040,128]{1,0:T(8,128)(2,1)S(1)} %get-tuple-element.19.refs_0_, bf16[1040,128]{1,0:T(8,128)(2,1)S(1)} %collective-permute-done.refs_1_, bf16[512,128]{1,0:T(8,128)(2,1)S(1)} %join.1.refs_2_, ...), custom_call_target="tpu_custom_call" | custom-call | tf_op jit(solution)/shard_map/aggregate/pallas_call | solution.py:37
  23.4 1.8 %collective-permute-start.10 = (bf16[256,128]{1,0:T(8,128)(2,1)S(1)}, bf16[256,128]{1,0:T(8,128)(2,1)S(1)}, u32[]{:S(2)}, u32[]{:S(2)}) collective-permute-start(bf16[256,128]{1,0:T(8,128)(2,1)S(1)} %get-tuple-element.23), channel_id=1, source_target_pairs={{0,1},{1,0},{2,3},{3,2},{4,5},{5,4},{6,7},{7,6},{8,9},{9,8},{10,11... | collective-permute-start | bytes 196616 | tf_op jit(solution)/shard_map/ppermute | solution.py:285
  25.2 0.9 %collective-permute-start.11 = (bf16[256,128]{1,0:T(8,128)(2,1)S(1)}, bf16[256,128]{1,0:T(8,128)(2,1)S(1)}, u32[]{:S(2)}, u32[]{:S(2)}) collective-permute-start(bf16[256,128]{1,0:T(8,128)(2,1)S(1)} %get-tuple-element.24), channel_id=1, source_target_pairs={{0,2},{1,3},{2,0},{3,1},{4,6},{5,7},{6,4},{7,5},{8,10},{9,11},{10,... | collective-permute-start | bytes 196616 | tf_op jit(solution)/shard_map/ppermute | solution.py:285
  26.0 1.8 %collective-permute-start.12 = (bf16[256,128]{1,0:T(8,128)(2,1)S(1)}, bf16[256,128]{1,0:T(8,128)(2,1)S(1)}, u32[]{:S(2)}, u32[]{:S(2)}) collective-permute-start(bf16[256,128]{1,0:T(8,128)(2,1)S(1)} %get-tuple-element.25), channel_id=1, source_target_pairs={{0,3},{1,2},{2,1},{3,0},{4,7},{5,6},{6,5},{7,4},{8,11},{9,10},{10,... | collective-permute-start | bytes 196616 | tf_op jit(solution)/shard_map/ppermute | solution.py:285
  27.8 0.6 %collective-permute-done.10.refs_1_ = bf16[256,128]{1,0:T(8,128)(2,1)S(1)} collective-permute-done((bf16[256,128]{1,0:T(8,128)(2,1)S(1)}, bf16[256,128]{1,0:T(8,128)(2,1)S(1)}, u32[]{:S(2)}, u32[]{:S(2)}) %collective-permute-start.10) | collective-permute-done | bytes 65568 | tf_op jit(solution)/shard_map/ppermute | solution.py:285
  28.5 4.0 %collective-permute-done.11.refs_2_ = bf16[256,128]{1,0:T(8,128)(2,1)S(1)} collective-permute-done((bf16[256,128]{1,0:T(8,128)(2,1)S(1)}, bf16[256,128]{1,0:T(8,128)(2,1)S(1)}, u32[]{:S(2)}, u32[]{:S(2)}) %collective-permute-start.11) | collective-permute-done | bytes 65568 | tf_op jit(solution)/shard_map/ppermute | solution.py:285
  32.5 0.5 %dense.1 = (bf16[256,256]{1,0:T(8,128)(2,1)S(1)}, f32[144,256]{1,0:T(8,128)S(1)}, bf16[144,256]{1,0:T(8,128)(2,1)S(1)}) custom-call(bf16[256,128]{1,0:T(8,128)(2,1)S(1)} %get-tuple-element.22.refs_0_, bf16[256,128]{1,0:T(8,128)(2,1)S(1)} %collective-permute-done.10.refs_1_, bf16[256,128]{1,0:T(8,128)(2,1)S(1)} %collective-permute-done.11.refs_2_, ...), custom_call_target="tpu_custom_call" | custom-call | tf_op jit(solution)/shard_map/dense/pallas_call | solution.py:37
  33.1 1.3 %collective-permute-done.13 = bf16[144,256]{1,0:T(8,128)(2,1)S(1)} collective-permute-done((bf16[144,256]{1,0:T(8,128)(2,1)S(1)}, bf16[144,256]{1,0:T(8,128)(2,1)S(1)}, u32[]{:S(2)}, u32[]{:S(2)}) %collective-permute-start.13) | collective-permute-done | bytes 73760 | tf_op jit(solution)/shard_map/ppermute | solution.py:296
  34.4 3.0 %collective-permute-start.16 = (bf16[144,256]{1,0:T(8,128)(2,1)S(1)}, bf16[144,256]{1,0:T(8,128)(2,1)S(1)}, u32[]{:S(2)}, u32[]{:S(2)}) collective-permute-start(bf16[144,256]{1,0:T(8,128)(2,1)S(1)} %add_convert_fusion.2), channel_id=1, source_target_pairs={{0,24},{4,28},{8,16},{12,20},{16,8},{20,12},{24,0},{28,4},{1,25},{... | collective-permute-start | bytes 221192 | tf_op jit(solution)/shard_map/ppermute | solution.py:214
  37.5 0.5 collective-permute-start.14
  38.0 2.0 %collective-permute-done.16 = bf16[144,256]{1,0:T(8,128)(2,1)S(1)} collective-permute-done((bf16[144,256]{1,0:T(8,128)(2,1)S(1)}, bf16[144,256]{1,0:T(8,128)(2,1)S(1)}, u32[]{:S(2)}, u32[]{:S(2)}) %collective-permute-start.16) | collective-permute-done | bytes 73760 | tf_op jit(solution)/shard_map/ppermute | solution.py:214
  40.0 1.7 %collective-permute-done.15 = bf16[144,256]{1,0:T(8,128)(2,1)S(1)} collective-permute-done((bf16[144,256]{1,0:T(8,128)(2,1)S(1)}, bf16[144,256]{1,0:T(8,128)(2,1)S(1)}, u32[]{:S(2)}, u32[]{:S(2)}) %collective-permute-start.15) | collective-permute-done | bytes 73760 | tf_op jit(solution)/shard_map/ppermute | solution.py:213
  41.9 2.2 %collective-permute-start.19 = (bf16[144,256]{1,0:T(8,128)(2,1)S(1)}, bf16[144,256]{1,0:T(8,128)(2,1)S(1)}, u32[]{:S(2)}, u32[]{:S(2)}) collective-permute-start(bf16[144,256]{1,0:T(8,128)(2,1)S(1)} %add_convert_fusion.1), channel_id=1, source_target_pairs={{0,3},{1,2},{2,1},{3,0},{4,7},{5,6},{6,5},{7,4},{8,11},{9,10},{10,... | collective-permute-start | bytes 221192 | tf_op jit(solution)/shard_map/ppermute | solution.py:214
  44.1 0.6 %collective-permute-start.18 = (bf16[144,256]{1,0:T(8,128)(2,1)S(1)}, bf16[144,256]{1,0:T(8,128)(2,1)S(1)}, u32[]{:S(2)}, u32[]{:S(2)}) collective-permute-start(bf16[144,256]{1,0:T(8,128)(2,1)S(1)} %add_convert_fusion.1), channel_id=1, source_target_pairs={{0,2},{1,3},{2,0},{3,1},{4,6},{5,7},{6,4},{7,5},{8,10},{9,11},{10,... | collective-permute-start | bytes 221192 | tf_op jit(solution)/shard_map/ppermute | solution.py:213
  44.7 1.7 %collective-permute-start.17 = (bf16[144,256]{1,0:T(8,128)(2,1)S(1)}, bf16[144,256]{1,0:T(8,128)(2,1)S(1)}, u32[]{:S(2)}, u32[]{:S(2)}) collective-permute-start(bf16[144,256]{1,0:T(8,128)(2,1)S(1)} %add_convert_fusion.1), channel_id=1, source_target_pairs={{0,1},{1,0},{2,3},{3,2},{4,5},{5,4},{6,7},{7,6},{8,9},{9,8},{10,11... | collective-permute-start | bytes 221192 | tf_op jit(solution)/shard_map/ppermute | solution.py:209
  46.4 2.6 %collective-permute-done.19 = bf16[144,256]{1,0:T(8,128)(2,1)S(1)} collective-permute-done((bf16[144,256]{1,0:T(8,128)(2,1)S(1)}, bf16[144,256]{1,0:T(8,128)(2,1)S(1)}, u32[]{:S(2)}, u32[]{:S(2)}) %collective-permute-start.19) | collective-permute-done | bytes 73760 | tf_op jit(solution)/shard_map/ppermute | solution.py:214
  48.9 1.7 %collective-permute-done.18 = bf16[144,256]{1,0:T(8,128)(2,1)S(1)} collective-permute-done((bf16[144,256]{1,0:T(8,128)(2,1)S(1)}, bf16[144,256]{1,0:T(8,128)(2,1)S(1)}, u32[]{:S(2)}, u32[]{:S(2)}) %collective-permute-start.18) | collective-permute-done | bytes 73760 | tf_op jit(solution)/shard_map/ppermute | solution.py:213
  50.7 1.3 %collective-permute-done.20.other_ref = bf16[144,256]{1,0:T(8,128)(2,1)S(1)} collective-permute-done((bf16[144,256]{1,0:T(8,128)(2,1)S(1)}, bf16[144,256]{1,0:T(8,128)(2,1)S(1)}, u32[]{:S(2)}, u32[]{:S(2)}) %collective-permute-start.20) | collective-permute-done | bytes 73760 | tf_op jit(solution)/shard_map/ppermute | solution.py:299
  52.0 0.8 %finish.1 = (f32[256,256]{1,0:T(8,128)}, f32[1,256]{1,0:T(1,128)}, bf16[256,256]{1,0:T(8,128)(2,1)}) custom-call(bf16[144,256]{1,0:T(8,128)(2,1)S(1)} %add_convert_fusion.mine_ref, bf16[144,256]{1,0:T(8,128)(2,1)S(1)} %collective-permute-done.20.other_ref, bf16[256,256]{1,0:T(8,128)(2,1)S(1)} %get-tuple-element.31.outcome_ref), custom_call_target="tpu_custom_call" | custom-call | tf_op jit(solution)/shard_map/finish/pallas_call | solution.py:37
  (35 shorter events, 1.2 us)
Async XLA Ops:
  0.6 6.9 %copy-start.1 = (bf16[256,256]{1,0:T(8,128)(2,1)S(1)}, bf16[256,256]{1,0:T(8,128)(2,1)}, u32[]{:S(2)}) copy-start(bf16[256,256]{1,0:T(8,128)(2,1)} %refs_0_.3) | copy-start | bytes 393220
  0.6 0.7 %copy-start.4 = (s32[256]{0:T(256)S(1)}, s32[256]{0:T(256)}, u32[]{:S(2)}) copy-start(s32[256]{0:T(256)} %param.10) | copy-start | bytes 3076
  2.3 10.0 %collective-permute-start.1 = (bf16[256,128]{1,0:T(8,128)(2,1)S(1)}, bf16[256,128]{1,0:T(8,128)(2,1)S(1)}, u32[]{:S(2)}, u32[]{:S(2)}) collective-permute-start(bf16[256,128]{1,0:T(8,128)(2,1)S(1)} %get-tuple-element.20), channel_id=1, source_target_pairs={{0,24},{1,16},{2,8},{3,0},{4,28},{5,20},{6,12},{7,4},{8,1},{9,25},... | collective-permute-start | bytes 196616 | tf_op jit(solution)/shard_map/ppermute | solution.py:248
  6.3 1.3 %copy-start.6 = (s32[1,2,4]{2,1,0:T(2,128)S(1)}, s32[1,2,4]{2,1,0:T(2,128)}, u32[]{:S(2)}) copy-start(s32[1,2,4]{2,1,0:T(2,128)} %refs_2_.1) | copy-start | bytes 100
  6.3 1.3 %copy-start.7 = (f32[256]{0:T(256)S(1)}, f32[256]{0:T(256)}, u32[]{:S(2)}) copy-start(f32[256]{0:T(256)} %param.15) | copy-start | bytes 3076
  6.3 1.3 %copy-start.5 = (s32[1,2,4]{2,1,0:T(2,128)S(1)}, s32[1,2,4]{2,1,0:T(2,128)}, u32[]{:S(2)}) copy-start(s32[1,2,4]{2,1,0:T(2,128)} %refs_1_.1) | copy-start | bytes 100
  6.3 6.4 %collective-permute-start.2 = (bf16[256,128]{1,0:T(8,128)(2,1)S(1)}, bf16[256,128]{1,0:T(8,128)(2,1)S(1)}, u32[]{:S(2)}, u32[]{:S(2)}) collective-permute-start(bf16[256,128]{1,0:T(8,128)(2,1)S(1)} %get-tuple-element.21), channel_id=1, source_target_pairs={{0,3},{1,11},{2,19},{3,27},{4,7},{5,15},{6,23},{7,31},{8,10},{9,18... | collective-permute-start | bytes 196616 | tf_op jit(solution)/shard_map/ppermute | solution.py:248
  7.5 1.0 %copy-start = (s32[1,2,4,128,128]{4,3,2,1,0:T(8,128)S(1)}, s32[1,2,4,128,128]{4,3,2,1,0:T(8,128)}, u32[]{:S(2)}) copy-start(s32[1,2,4,128,128]{4,3,2,1,0:T(8,128)} %refs_0_.2) | copy-start | bytes 1572868
  9.4 12.4 %collective-permute-start = (bf16[1040,128]{1,0:T(8,128)(2,1)S(1)}, bf16[1040,128]{1,0:T(8,128)(2,1)S(1)}, u32[]{:S(2)}, u32[]{:S(2)}) collective-permute-start(bf16[1040,128]{1,0:T(8,128)(2,1)S(1)} %get-tuple-element.19.refs_0_), channel_id=1, source_target_pairs={{0,3},{1,2},{2,1},{3,0},{4,7},{5,6},{6,5},{7,4},{8,11},{9,10},{10,... | collective-permute-start | bytes 798728 | tf_op jit(solution)/shard_map/ppermute | solution.py:261
  12.7 19.8 %copy-start.2 = (bf16[256,256]{1,0:T(8,128)(2,1)S(1)}, bf16[256,256]{1,0:T(8,128)(2,1)}, u32[]{:S(2)}) copy-start(bf16[256,256]{1,0:T(8,128)(2,1)} %refs_6_.1) | copy-start | bytes 393220
  12.8 19.8 %copy-start.3 = (bf16[256,256]{1,0:T(8,128)(2,1)S(1)}, bf16[256,256]{1,0:T(8,128)(2,1)}, u32[]{:S(2)}) copy-start(bf16[256,256]{1,0:T(8,128)(2,1)} %refs_8_.1) | copy-start | bytes 393220
  12.8 7.3 %collective-permute-start.8 = (bf16[512,128]{1,0:T(8,128)(2,1)S(1)}, bf16[512,128]{1,0:T(8,128)(2,1)S(1)}, u32[]{:S(2)}, u32[]{:S(2)}) collective-permute-start(bf16[512,128]{1,0:T(8,128)(2,1)S(1)} %join.1.refs_2_), channel_id=1, source_target_pairs={{0,24},{4,28},{8,16},{12,20},{16,8},{20,12},{24,0},{28,4},{1,25},{... | collective-permute-start | bytes 393224 | tf_op jit(solution)/shard_map/ppermute | solution.py:269
  16.2 5.1 %collective-permute-start.6 = (bf16[512,128]{1,0:T(8,128)(2,1)S(1)}, bf16[512,128]{1,0:T(8,128)(2,1)S(1)}, u32[]{:S(2)}, u32[]{:S(2)}) collective-permute-start(bf16[512,128]{1,0:T(8,128)(2,1)S(1)} %join.1.refs_2_), channel_id=1, source_target_pairs={{0,16},{4,20},{8,24},{12,28},{16,0},{20,4},{24,8},{28,12},{1,17},{... | collective-permute-start | bytes 393224 | tf_op jit(solution)/shard_map/ppermute | solution.py:269
  16.2 5.1 %collective-permute-start.4 = (bf16[512,128]{1,0:T(8,128)(2,1)S(1)}, bf16[512,128]{1,0:T(8,128)(2,1)S(1)}, u32[]{:S(2)}, u32[]{:S(2)}) collective-permute-start(bf16[512,128]{1,0:T(8,128)(2,1)S(1)} %join.1.refs_2_), channel_id=1, source_target_pairs={{0,8},{4,12},{8,0},{12,4},{16,24},{20,28},{24,16},{28,20},{1,9},{5... | collective-permute-start | bytes 393224 | tf_op jit(solution)/shard_map/ppermute | solution.py:269
  16.8 5.0 %collective-permute-start.3 = (bf16[512,128]{1,0:T(8,128)(2,1)S(1)}, bf16[512,128]{1,0:T(8,128)(2,1)S(1)}, u32[]{:S(2)}, u32[]{:S(2)}) collective-permute-start(bf16[512,128]{1,0:T(8,128)(2,1)S(1)} %join.1.refs_2_), channel_id=1, source_target_pairs={{0,4},{4,0},{8,12},{12,8},{16,20},{20,16},{24,28},{28,24},{1,5},{5... | collective-permute-start | bytes 393224 | tf_op jit(solution)/shard_map/ppermute | solution.py:271
  20.0 1.8 %collective-permute-start.9 = (bf16[512,128]{1,0:T(8,128)(2,1)S(1)}, bf16[512,128]{1,0:T(8,128)(2,1)S(1)}, u32[]{:S(2)}, u32[]{:S(2)}) collective-permute-start(bf16[512,128]{1,0:T(8,128)(2,1)S(1)} %collective-permute-done.8.refs_8_), channel_id=1, source_target_pairs={{0,4},{4,0},{8,12},{12,8},{16,20},{20,16},{24,28},{28,24},{1,5},{5... | collective-permute-start | bytes 393224 | tf_op jit(solution)/shard_map/ppermute | solution.py:271
  21.3 1.3 %collective-permute-start.7 = (bf16[512,128]{1,0:T(8,128)(2,1)S(1)}, bf16[512,128]{1,0:T(8,128)(2,1)S(1)}, u32[]{:S(2)}, u32[]{:S(2)}) collective-permute-start(bf16[512,128]{1,0:T(8,128)(2,1)S(1)} %collective-permute-done.6.refs_6_), channel_id=1, source_target_pairs={{0,4},{4,0},{8,12},{12,8},{16,20},{20,16},{24,28},{28,24},{1,5},{5... | collective-permute-start | bytes 393224 | tf_op jit(solution)/shard_map/ppermute | solution.py:271
  21.3 1.5 %collective-permute-start.5 = (bf16[512,128]{1,0:T(8,128)(2,1)S(1)}, bf16[512,128]{1,0:T(8,128)(2,1)S(1)}, u32[]{:S(2)}, u32[]{:S(2)}) collective-permute-start(bf16[512,128]{1,0:T(8,128)(2,1)S(1)} %collective-permute-done.4.refs_4_), channel_id=1, source_target_pairs={{0,4},{4,0},{8,12},{12,8},{16,20},{20,16},{24,28},{28,24},{1,5},{5... | collective-permute-start | bytes 393224 | tf_op jit(solution)/shard_map/ppermute | solution.py:271
  23.4 5.1 %collective-permute-start.10 = (bf16[256,128]{1,0:T(8,128)(2,1)S(1)}, bf16[256,128]{1,0:T(8,128)(2,1)S(1)}, u32[]{:S(2)}, u32[]{:S(2)}) collective-permute-start(bf16[256,128]{1,0:T(8,128)(2,1)S(1)} %get-tuple-element.23), channel_id=1, source_target_pairs={{0,1},{1,0},{2,3},{3,2},{4,5},{5,4},{6,7},{7,6},{8,9},{9,8},{10,11... | collective-permute-start | bytes 196616 | tf_op jit(solution)/shard_map/ppermute | solution.py:285
  25.2 7.3 %collective-permute-start.11 = (bf16[256,128]{1,0:T(8,128)(2,1)S(1)}, bf16[256,128]{1,0:T(8,128)(2,1)S(1)}, u32[]{:S(2)}, u32[]{:S(2)}) collective-permute-start(bf16[256,128]{1,0:T(8,128)(2,1)S(1)} %get-tuple-element.24), channel_id=1, source_target_pairs={{0,2},{1,3},{2,0},{3,1},{4,6},{5,7},{6,4},{7,5},{8,10},{9,11},{10,... | collective-permute-start | bytes 196616 | tf_op jit(solution)/shard_map/ppermute | solution.py:285
  26.0 6.5 %collective-permute-start.12 = (bf16[256,128]{1,0:T(8,128)(2,1)S(1)}, bf16[256,128]{1,0:T(8,128)(2,1)S(1)}, u32[]{:S(2)}, u32[]{:S(2)}) collective-permute-start(bf16[256,128]{1,0:T(8,128)(2,1)S(1)} %get-tuple-element.25), channel_id=1, source_target_pairs={{0,3},{1,2},{2,1},{3,0},{4,7},{5,6},{6,5},{7,4},{8,11},{9,10},{10,... | collective-permute-start | bytes 196616 | tf_op jit(solution)/shard_map/ppermute | solution.py:285
  33.1 1.3 %collective-permute-start.13 = (bf16[144,256]{1,0:T(8,128)(2,1)S(1)}, bf16[144,256]{1,0:T(8,128)(2,1)S(1)}, u32[]{:S(2)}, u32[]{:S(2)}) collective-permute-start(bf16[144,256]{1,0:T(8,128)(2,1)S(1)} %get-tuple-element.30), channel_id=1, source_target_pairs={{0,4},{4,0},{8,12},{12,8},{16,20},{20,16},{24,28},{28,24},{1,5},{5... | collective-permute-start | bytes 221192 | tf_op jit(solution)/shard_map/ppermute | solution.py:296
  34.4 5.6 %collective-permute-start.16 = (bf16[144,256]{1,0:T(8,128)(2,1)S(1)}, bf16[144,256]{1,0:T(8,128)(2,1)S(1)}, u32[]{:S(2)}, u32[]{:S(2)}) collective-permute-start(bf16[144,256]{1,0:T(8,128)(2,1)S(1)} %add_convert_fusion.2), channel_id=1, source_target_pairs={{0,24},{4,28},{8,16},{12,20},{16,8},{20,12},{24,0},{28,4},{1,25},{... | collective-permute-start | bytes 221192 | tf_op jit(solution)/shard_map/ppermute | solution.py:214
  37.4 4.4 %collective-permute-start.15 = (bf16[144,256]{1,0:T(8,128)(2,1)S(1)}, bf16[144,256]{1,0:T(8,128)(2,1)S(1)}, u32[]{:S(2)}, u32[]{:S(2)}) collective-permute-start(bf16[144,256]{1,0:T(8,128)(2,1)S(1)} %add_convert_fusion.2), channel_id=1, source_target_pairs={{0,16},{4,20},{8,24},{12,28},{16,0},{20,4},{24,8},{28,12},{1,17},{... | collective-permute-start | bytes 221192 | tf_op jit(solution)/shard_map/ppermute | solution.py:213
  37.5 4.4 %collective-permute-start.14 = (bf16[144,256]{1,0:T(8,128)(2,1)S(1)}, bf16[144,256]{1,0:T(8,128)(2,1)S(1)}, u32[]{:S(2)}, u32[]{:S(2)}) collective-permute-start(bf16[144,256]{1,0:T(8,128)(2,1)S(1)} %add_convert_fusion.2), channel_id=1, source_target_pairs={{0,8},{4,12},{8,0},{12,4},{16,24},{20,28},{24,16},{28,20},{1,9},{5... | collective-permute-start | bytes 221192 | tf_op jit(solution)/shard_map/ppermute | solution.py:209
  41.9 7.0 %collective-permute-start.19 = (bf16[144,256]{1,0:T(8,128)(2,1)S(1)}, bf16[144,256]{1,0:T(8,128)(2,1)S(1)}, u32[]{:S(2)}, u32[]{:S(2)}) collective-permute-start(bf16[144,256]{1,0:T(8,128)(2,1)S(1)} %add_convert_fusion.1), channel_id=1, source_target_pairs={{0,3},{1,2},{2,1},{3,0},{4,7},{5,6},{6,5},{7,4},{8,11},{9,10},{10,... | collective-permute-start | bytes 221192 | tf_op jit(solution)/shard_map/ppermute | solution.py:214
  44.1 6.5 %collective-permute-start.18 = (bf16[144,256]{1,0:T(8,128)(2,1)S(1)}, bf16[144,256]{1,0:T(8,128)(2,1)S(1)}, u32[]{:S(2)}, u32[]{:S(2)}) collective-permute-start(bf16[144,256]{1,0:T(8,128)(2,1)S(1)} %add_convert_fusion.1), channel_id=1, source_target_pairs={{0,2},{1,3},{2,0},{3,1},{4,6},{5,7},{6,4},{7,5},{8,10},{9,11},{10,... | collective-permute-start | bytes 221192 | tf_op jit(solution)/shard_map/ppermute | solution.py:213
  44.7 5.9 %collective-permute-start.17 = (bf16[144,256]{1,0:T(8,128)(2,1)S(1)}, bf16[144,256]{1,0:T(8,128)(2,1)S(1)}, u32[]{:S(2)}, u32[]{:S(2)}) collective-permute-start(bf16[144,256]{1,0:T(8,128)(2,1)S(1)} %add_convert_fusion.1), channel_id=1, source_target_pairs={{0,1},{1,0},{2,3},{3,2},{4,5},{5,4},{6,7},{7,6},{8,9},{9,8},{10,11... | collective-permute-start | bytes 221192 | tf_op jit(solution)/shard_map/ppermute | solution.py:209
  50.7 1.3 %collective-permute-start.20 = (bf16[144,256]{1,0:T(8,128)(2,1)S(1)}, bf16[144,256]{1,0:T(8,128)(2,1)S(1)}, u32[]{:S(2)}, u32[]{:S(2)}) collective-permute-start(bf16[144,256]{1,0:T(8,128)(2,1)S(1)} %add_convert_fusion.mine_ref), channel_id=1, source_target_pairs={{0,4},{4,0},{8,12},{12,8},{16,20},{20,16},{24,28},{28,24},{1,5},{5... | collective-permute-start | bytes 221192 | tf_op jit(solution)/shard_map/ppermute | solution.py:299
